TPU v7x, 256 devices: a whole 4x4x8 slice. The times are simulated.
256 devices in a mesh: member: 8 (over x, y_hi), fsdp: 32 (over z, y_lo, core).
Axes of the slice: x: 4, y: 4 (y_hi: 2, y_lo: 2; y = y_hi * 2 + y_lo), z: 8, core: 2. Of those that a mesh axis runs over, the one named last changes fastest.
Arguments:
- tokens: bfloat16 [8, 4096, 1792], P('member', 'fsdp'), may hold values from -6 to 6
- cotangent: bfloat16 [8, 4096, 7168], P('member', 'fsdp'), may hold values from -8 to 8
- gate_weight: bfloat16 [8, 7168, 1792], P('member', 'fsdp'), may hold values from -5 to 5
- up_weight: bfloat16 [8, 7168, 1792], P('member', 'fsdp'), may hold values from -5 to 5
- gate_first: bfloat16 [8, 7168, 1792], P('member', 'fsdp'), may hold values from -4 to 4
- up_first: bfloat16 [8, 7168, 1792], P('member', 'fsdp'), may hold values from -4 to 4
- gate_second: bfloat16 [8, 7168, 1792], P('member', 'fsdp'), may hold values from 0.19921875 to 4
- up_second: bfloat16 [8, 7168, 1792], P('member', 'fsdp'), may hold values from 0.19921875 to 4
- winner: int32 [8], replicated, may hold values from 0 to 7, as said below
- rate_index: int32 [8], replicated, may hold values from 0 to 4
Outputs:
- new_gate: bfloat16 [8, 7168, 1792], P('member', 'fsdp')
- new_up: bfloat16 [8, 7168, 1792], P('member', 'fsdp')
- new_gate_first: bfloat16 [8, 7168, 1792], P('member', 'fsdp')
- new_up_first: bfloat16 [8, 7168, 1792], P('member', 'fsdp')
- new_gate_second: bfloat16 [8, 7168, 1792], P('member', 'fsdp')
- new_up_second: bfloat16 [8, 7168, 1792], P('member', 'fsdp')
Inputs may be any that keep to these rules, and one draw needn't show every extreme that they name: Exactly 2 members m have winner[m] != m; for those, winner[m] is a member whose own winner is itself. One winner may serve several of them.
All inputs are finite; a program needn't handle non-finite values.
Results may differ from a plain program's by a relative error of at most 0.003.
Values may be sent and summed in bfloat16 or wider, within the bound.
No kernel may reach another device: no remote copies, remote signals or barrier semaphores. Data moves between devices by JAX's collectives and lax.ppermute only.
A program may use at most 128 MiB of HBM per device.

v0:
```python
import jax
import jax.numpy as jnp
from jax import lax
from jax.sharding import PartitionSpec as P

gelu_c = 0.7978845608028654
bias_first = 1.0 - 0.9**10
bias_second = 1.0 - 0.95**10


def gelu_parts(gate_pre):
    tangent = jnp.tanh(gelu_c * (gate_pre + 0.044715 * gate_pre * gate_pre * gate_pre))
    activated = 0.5 * gate_pre * (1.0 + tangent)
    slope = 0.5 * (1.0 + tangent) + 0.5 * gate_pre * (1.0 - tangent * tangent) * gelu_c * (
        1.0 + 3.0 * 0.044715 * gate_pre * gate_pre
    )
    return (activated, slope)


def branch_terms(token_block, cot_block, gate_w, up_w, scale):
    contract = (((1,), (1,)), ((), ()))
    gate_pre = (
        lax.dot_general(token_block, gate_w, contract, preferred_element_type=jnp.float32) * scale
    )
    up_pre = (
        lax.dot_general(token_block, up_w, contract, preferred_element_type=jnp.float32) * scale
    )
    activated, slope = gelu_parts(gate_pre)
    cot_f32 = cot_block.astype(jnp.float32)
    gate_cot = (cot_f32 * up_pre * slope).astype(jnp.bfloat16)
    up_cot = (cot_f32 * activated).astype(jnp.bfloat16)
    return (gate_cot, up_cot)


def weight_grad(cot_block, token_block, scale):
    contract = (((0,), (0,)), ((), ()))
    return (
        lax.dot_general(cot_block, token_block, contract, preferred_element_type=jnp.float32)
        * scale
    )


def adam_update(weight, moment_one, moment_two, grad, learning):
    first_new = 0.9 * moment_one.astype(jnp.float32) + 0.1 * grad
    second_new = 0.95 * moment_two.astype(jnp.float32) + 0.05 * grad * grad
    update = learning * (first_new / bias_first) / (jnp.sqrt(second_new / bias_second) + 1e-08)
    new_weight = weight.astype(jnp.float32) - update
    return (
        new_weight.astype(jnp.bfloat16)[None],
        first_new.astype(jnp.bfloat16)[None],
        second_new.astype(jnp.bfloat16)[None],
    )


def body(
    tokens,
    cotangent,
    gate_weight,
    up_weight,
    gate_first,
    up_first,
    gate_second,
    up_second,
    winner,
    rate_index,
):
    bundle = jnp.concatenate(
        [gate_weight, up_weight, gate_first, up_first, gate_second, up_second], axis=0
    )
    members = lax.axis_size("member")
    member_index = lax.axis_index("member")
    shard_rows = bundle.shape[1]
    width = bundle.shape[2]
    portion = shard_rows // members
    pieces = bundle.reshape(6, members, portion, width)
    held = lax.all_to_all(pieces, "member", split_axis=1, concat_axis=1, tiled=True)
    wanted = jnp.take(held, winner, axis=1)
    returned = lax.all_to_all(wanted, "member", split_axis=1, concat_axis=1, tiled=True)
    moved = returned.reshape(6, shard_rows, width)
    gate_w = moved[0]
    up_w = moved[1]
    own_rows = tokens[0]
    scale = own_rows.shape[1] ** (-0.5)
    cot_cols = lax.all_to_all(cotangent[0], "fsdp", split_axis=1, concat_axis=0, tiled=True)
    all_rows = lax.all_gather(own_rows, "fsdp", axis=0, tiled=True)
    gate_cot, up_cot = branch_terms(all_rows, cot_cols, gate_w, up_w, scale)
    gate_grad = weight_grad(gate_cot, all_rows, scale)
    up_grad = weight_grad(up_cot, all_rows, scale)
    learning = 0.2 * jnp.exp2((rate_index[member_index].astype(jnp.float32) - 2.0) * 0.5)
    new_gate, gate_one, gate_two = adam_update(gate_w, moved[2], moved[4], gate_grad, learning)
    new_up, up_one, up_two = adam_update(up_w, moved[3], moved[5], up_grad, learning)
    return (new_gate, new_up, gate_one, up_one, gate_two, up_two)


def solution(mesh):
    return jax.shard_map(
        body,
        mesh=mesh,
        in_specs=(
            P("member", "fsdp", None),
            P("member", "fsdp", None),
            P("member", "fsdp", None),
            P("member", "fsdp", None),
            P("member", "fsdp", None),
            P("member", "fsdp", None),
            P("member", "fsdp", None),
            P("member", "fsdp", None),
            P(),
            P(),
        ),
        out_specs=(
            P("member", "fsdp", None),
            P("member", "fsdp", None),
            P("member", "fsdp", None),
            P("member", "fsdp", None),
            P("member", "fsdp", None),
            P("member", "fsdp", None),
        ),
        check_vma=False,
    )
```

profile of v0, /device:TPU:1, one launch (start us, length us, event | category | flops | bytes accessed | tf_op | source)
XLA Modules:
  0.0 313.2 jit_solution(9965555519134581405)
XLA Ops:
  7.2 0.0 copy-start.2
  7.2 0.0 copy-start.3
  7.2 0.0 copy-start.4
  7.2 0.0 all-gather.3.cloned.1.call-start
  7.2 0.7 all-gather.3.cloned.1.call-update
  7.9 0.0 copy-start.5
  7.9 2.1 constant_dynamic-update-slice_fusion.5
  10.1 2.1 constant_dynamic-update-slice_fusion.4
  12.2 0.0 copy-done.2
  12.2 1.0 constant_dynamic-update-slice_fusion.3
  13.1 0.0 copy-done.3
  13.1 1.0 constant_dynamic-update-slice_fusion.2
  14.1 0.0 copy-done.4
  14.1 0.9 constant_dynamic-update-slice_fusion.1
  15.0 0.0 copy-done.5
  15.0 1.0 constant_dynamic-update-slice_fusion
  16.0 7.3 %reshape.57 = bf16[6,8,28,1792]{3,2,1,0:T(8,128)(2,1)} reshape(bf16[6,224,1792]{2,1,0:T(8,128)(2,1)} %constant_dynamic-update-slice_fusion) | data formatting | bytes 9633792 | tf_op jit(solution)/shard_map/reshape | solution.py:75
  23.3 5.4 %copy.19 = bf16[6,8,28,1792]{3,2,0,1:T(8,128)(2,1)} copy(bf16[6,8,28,1792]{3,2,1,0:T(8,128)(2,1)} %reshape.57) | data formatting | bytes 9633792 | tf_op jit(solution)/shard_map/reshape | solution.py:75
  28.7 0.0 copy-start.6
  28.7 7.9 %all-to-all-start = ((bf16[6,8,28,1792]{3,2,0,1:T(8,128)(2,1)}), bf16[6,8,28,1792]{3,2,0,1:T(8,128)(2,1)}, u32[]{:S(2)}, u32[]{:S(2)}) async-start(bf16[6,8,28,1792]{3,2,0,1:T(8,128)(2,1)} %copy.19), calls=%async_computation | async-start | bytes 11010048 | tf_op jit(solution)/shard_map/all_to_all | solution.py:76
  36.6 0.0 copy-done.6
  36.7 77.7 %all-to-all-done = bf16[6,8,28,1792]{3,2,0,1:T(8,128)(2,1)} async-done(((bf16[6,8,28,1792]{3,2,0,1:T(8,128)(2,1)}), bf16[6,8,28,1792]{3,2,0,1:T(8,128)(2,1)}, u32[]{:S(2)}, u32[]{:S(2)}) %all-to-all-start) | async-done | bytes 4816928 | tf_op jit(solution)/shard_map/all_to_all | solution.py:76
  114.4 5.5 %copy.20 = bf16[6,8,28,1792]{3,2,1,0:T(8,128)(2,1)} copy(bf16[6,8,28,1792]{3,2,0,1:T(8,128)(2,1)} %all-to-all-done) | data formatting | bytes 9633792 | tf_op jit(solution)/shard_map/all_to_all | solution.py:76
  119.9 6.1 %gather_fusion = bf16[8,6,28,1792]{3,2,1,0:T(8,128)(2,1)} fusion(bf16[6,8,28,1792]{3,2,1,0:T(8,128)(2,1)} %copy.20, s32[1024]{0:T(1024)S(1)} %pad_clamp_fusion), kind=kCustom, calls=%fused_computation | custom fusion | bytes 9633824 | tf_op jit(solution)/shard_map/jit(_take)/gather | solution.py:77
  126.0 5.8 %select_bitcast_fusion = bf16[6,8,28,1792]{3,2,0,1:T(8,128)(2,1)} fusion(bf16[8,6,28,1792]{3,2,1,0:T(8,128)(2,1)} %gather_fusion, pred[8]{0:T(512)(128)(4,1)S(1)} %compare_and_fusion), kind=kLoop, calls=%fused_computation.9 | loop fusion | flops 2408448 | bytes 9633800 | tf_op jit(solution)/shard_map/jit(_take)/select_n | solution.py:77
  131.7 0.0 copy-start
  131.7 4.8 %all-to-all-start.1 = ((bf16[6,8,28,1792]{3,2,0,1:T(8,128)(2,1)}), bf16[6,8,28,1792]{3,2,0,1:T(8,128)(2,1)}, u32[]{:S(2)}, u32[]{:S(2)}) async-start(bf16[6,8,28,1792]{3,2,0,1:T(8,128)(2,1)} %select_bitcast_fusion), calls=%async_computation.1 | async-start | bytes 11010048 | tf_op jit(solution)/shard_map/all_to_all | solution.py:78
  136.6 0.0 copy-done
  136.6 0.0 copy-start.7
  136.6 2.3 copy.21
  138.9 75.0 %all-to-all-done.1 = bf16[6,8,28,1792]{3,2,0,1:T(8,128)(2,1)} async-done(((bf16[6,8,28,1792]{3,2,0,1:T(8,128)(2,1)}), bf16[6,8,28,1792]{3,2,0,1:T(8,128)(2,1)}, u32[]{:S(2)}, u32[]{:S(2)}) %all-to-all-start.1) | async-done | bytes 4816928 | tf_op jit(solution)/shard_map/all_to_all | solution.py:78
  213.9 9.9 %all-to-all-start.2 = ((bf16[128,32,224]{0,2,1:T(8,128)(2,1)}), bf16[128,32,224]{0,2,1:T(8,128)(2,1)}, u32[]{:S(2)}, u32[]{:S(2)}) async-start(bf16[128,32,224]{0,2,1:T(8,128)(2,1)} %bitcast.1), calls=%async_computation.2 | async-start | bytes 3670016 | tf_op jit(solution)/shard_map/all_to_all | solution.py:84
  223.8 0.0 copy-done.7
  223.8 0.6 dynamic_slice.3
  225.1 1.6 fusion.73
  226.7 1.1 squeeze.7
  227.8 1.0 squeeze.6
  228.8 4.7 %convert_multiply_fusion = (f32[1,8,28,1792]{3,2,0,1:T(8,128)}, f32[1,8,28,1792]{3,2,0,1:T(8,128)}, f32[1,8,28,1792]{3,2,0,1:T(8,128)}, f32[1,8,28,1792]{3,2,0,1:T(8,128)S(1)}) fusion(bf16[6,8,28,1792]{3,2,0,1:T(8,128)(2,1)} %all-to-all-done.1), kind=kLoop, calls=%fused_computation.38 | loop fusion | flops 3211264 | bytes 9633792 | tf_op jit(solution)/shard_map/mul | solution.py:45
  233.5 1.5 mul.187
  235.1 2.6 mul.181
  237.7 2.6 mul.175
  240.3 1.4 mul.144
  241.8 0.0 all-gather.3.cloned.1.call-done
  241.8 11.6 %fusion.4 = f32[224,4096]{1,0:T(8,128)} fusion(bf16[224,1792]{1,0:T(8,128)(2,1)} %squeeze.6, bf16[1,4096,1792]{2,1,0:T(8,128)(2,1)} %all-gather.3.cloned.1.call-done), kind=kOutput, calls=%fused_computation.5 | convolution fusion | flops 3288334336 | bytes 19152896 | tf_op jit(solution)/shard_map/dot_general | solution.py:23
  253.4 15.0 %all-to-all-done.2 = bf16[128,32,224]{0,2,1:T(8,128)(2,1)} async-done(((bf16[128,32,224]{0,2,1:T(8,128)(2,1)}), bf16[128,32,224]{0,2,1:T(8,128)(2,1)}, u32[]{:S(2)}, u32[]{:S(2)}) %all-to-all-start.2) | async-done | bytes 1835040 | tf_op jit(solution)/shard_map/all_to_all | solution.py:84
  268.4 12.5 %fusion = f32[224,1792]{1,0:T(8,128)} fusion(bf16[1,4096,1792]{2,1,0:T(8,128)(2,1)} %all-gather.3.cloned.1.call-done, f32[224,4096]{1,0:T(8,128)} %fusion.4, bf16[128,32,224]{0,2,1:T(8,128)(2,1)} %all-to-all-done.2), kind=kOutput, calls=%fused_computation.1 | convolution fusion | flops 3299344384 | bytes 21790720 | tf_op jit(solution)/shard_map/dot_general | solution.py:38
  280.9 0.0 copy-done.1
  280.9 25.5 %convert_bitcast_fusion.1 = (bf16[1,224,1792]{2,1,0:T(8,128)(2,1)}, bf16[1,224,1792]{2,1,0:T(8,128)(2,1)}, bf16[1,224,1792]{2,1,0:T(8,128)(2,1)}, bf16[1,224,179...) fusion(f32[224,1792]{1,0:T(8,128)S(1)} %mul.187, f32[224,1792]{1,0:T(8,128)} %fusion, ...), kind=kOutput, calls=%fused_computation.60 | convolution fusion | flops 6609813504 | bytes 34635780 | tf_op jit(solution)/shard_map/dot_general | solution.py:38
  (4 shorter events, 0.0 us)
Async XLA Ops:
  7.2 5.0 %copy-start.2 = (bf16[1,224,1792]{2,1,0:T(8,128)(2,1)S(1)}, bf16[1,224,1792]{2,1,0:T(8,128)(2,1)}, u32[]{:S(2)}) copy-start(bf16[1,224,1792]{2,1,0:T(8,128)(2,1)} %param.14) | copy-start | bytes 2408452
  7.2 6.0 %copy-start.3 = (bf16[1,224,1792]{2,1,0:T(8,128)(2,1)S(1)}, bf16[1,224,1792]{2,1,0:T(8,128)(2,1)}, u32[]{:S(2)}) copy-start(bf16[1,224,1792]{2,1,0:T(8,128)(2,1)} %param.15) | copy-start | bytes 2408452
  7.2 6.9 %copy-start.4 = (bf16[1,224,1792]{2,1,0:T(8,128)(2,1)S(1)}, bf16[1,224,1792]{2,1,0:T(8,128)(2,1)}, u32[]{:S(2)}) copy-start(bf16[1,224,1792]{2,1,0:T(8,128)(2,1)} %param.16) | copy-start | bytes 2408452
  7.2 234.6 %all-gather.3.cloned.1.call-start = ((), (), s32[]{:S(2)}) async-start(), calls=%async_computation.3 | async-start | bytes 15138816 | tf_op jit(solution)/shard_map/all_gather | solution.py:85
  7.9 7.1 %copy-start.5 = (bf16[1,224,1792]{2,1,0:T(8,128)(2,1)S(1)}, bf16[1,224,1792]{2,1,0:T(8,128)(2,1)}, u32[]{:S(2)}) copy-start(bf16[1,224,1792]{2,1,0:T(8,128)(2,1)} %param.17) | copy-start | bytes 2408452
  28.7 7.9 %copy-start.6 = (s32[8]{0:T(128)S(1)}, s32[8]{0:T(128)}, u32[]{:S(2)}) copy-start(s32[8]{0:T(128)} %param.18) | copy-start | bytes 100
  28.7 85.7 %all-to-all-start = ((bf16[6,8,28,1792]{3,2,0,1:T(8,128)(2,1)}), bf16[6,8,28,1792]{3,2,0,1:T(8,128)(2,1)}, u32[]{:S(2)}, u32[]{:S(2)}) async-start(bf16[6,8,28,1792]{3,2,0,1:T(8,128)(2,1)} %copy.19), calls=%async_computation | async-start | bytes 11010048 | tf_op jit(solution)/shard_map/all_to_all | solution.py:76
  131.7 4.8 %copy-start = (bf16[1,128,7168]{2,1,0:T(8,128)(2,1)S(1)}, bf16[1,128,7168]{2,1,0:T(8,128)(2,1)}, u32[]{:S(2)}) copy-start(bf16[1,128,7168]{2,1,0:T(8,128)(2,1)} %param.11) | copy-start | bytes 5505028
  131.7 82.2 %all-to-all-start.1 = ((bf16[6,8,28,1792]{3,2,0,1:T(8,128)(2,1)}), bf16[6,8,28,1792]{3,2,0,1:T(8,128)(2,1)}, u32[]{:S(2)}, u32[]{:S(2)}) async-start(bf16[6,8,28,1792]{3,2,0,1:T(8,128)(2,1)} %select_bitcast_fusion), calls=%async_computation.1 | async-start | bytes 11010048 | tf_op jit(solution)/shard_map/all_to_all | solution.py:78
  136.6 87.2 %copy-start.7 = (s32[8]{0:T(128)S(1)}, s32[8]{0:T(128)}, u32[]{:S(2)}) copy-start(s32[8]{0:T(128)} %param.19) | copy-start | bytes 100
  213.9 54.5 %all-to-all-start.2 = ((bf16[128,32,224]{0,2,1:T(8,128)(2,1)}), bf16[128,32,224]{0,2,1:T(8,128)(2,1)}, u32[]{:S(2)}, u32[]{:S(2)}) async-start(bf16[128,32,224]{0,2,1:T(8,128)(2,1)} %bitcast.1), calls=%async_computation.2 | async-start | bytes 3670016 | tf_op jit(solution)/shard_map/all_to_all | solution.py:84
  253.4 27.5 %copy-start.1 = (f32[224,1792]{1,0:T(8,128)S(1)}, f32[224,1792]{1,0:T(8,128)}, u32[]{:S(2)}) copy-start(f32[224,1792]{1,0:T(8,128)} %mul.181) | copy-start | bytes 4816900
Sparse Core Ops, SparseCore 0:
  9.9 211.2 all-gather.2
where the time goes:
time: 314 us; the launch traced here: 313 us
  waiting for transfers between devices  168 us (54%)
  matrix products  49.6 us (16%)
  local copies, waits for them, and re-layouts  47.3 us (15%)
  starting transfers between devices  22.6 us (7%)
  between operations  14.9 us (5%)
  other arithmetic  10.5 us (3%)
    all_to_all x1, waiting for transfers between devices, body(): lax.all_to_all(pieces, 'member', split_axis=1, concat_axis=1, tiled=True)  77.7 us
    all_to_all x1, waiting for transfers between devices, body(): lax.all_to_all(wanted, 'member', split_axis=1, concat_axis=1, tiled=True)  75 us
    dot_general x2, matrix products, weight_grad(): lax.dot_general(cot_block, token_block, contract, preferred_element_type=...  38 us
    all_to_all x1, waiting for transfers between devices, body(): lax.all_to_all(cotangent[0], 'fsdp', split_axis=1, concat_axis=0, tiled=T...  15 us
    reshape x2, local copies, waits for them, and re-layouts, body(): pieces = bundle.reshape(6, members, portion, width)  12.7 us
    dot_general x1, matrix products, branch_terms(): lax.dot_general(token_block, gate_w, contract, preferred_element_type=jnp...  11.6 us
    all_to_all x1, starting transfers between devices, body(): lax.all_to_all(cotangent[0], 'fsdp', split_axis=1, concat_axis=0, tiled=T...  9.87 us
    unnamed x22, local copies, waits for them, and re-layouts  9.46 us
  transfers between devices with their start and end apart: 4, of which 3 were waited for; matrix products, arithmetic and copies ran while one was open for 22% of the time, Pallas kernels for 0%

commit v1 on v0

v1 whole, which is shorter than its diff:
```python
import functools

import jax
import jax.numpy as jnp
from jax import lax
from jax.experimental import pallas as pl
from jax.experimental.pallas import tpu as pltpu
from jax.sharding import PartitionSpec as P

gelu_c = 0.7978845608028654
bias_first = 1.0 - 0.9**10
bias_second = 1.0 - 0.95**10
nz = 8
halves = 2


def device(z, low, core):
    return (z * 2 + low) * 2 + core


everyone = [(z, low, core) for z in range(nz) for low in range(2) for core in range(2)]
z_up = [(device(z, a, c), device((z + 1) % nz, a, c)) for z, a, c in everyone]
z_down = [(b, a) for a, b in z_up]
core_swap = [(i, i ^ 1) for i in range(32)]
low_swap = [(i, i ^ 2) for i in range(32)]


def gelu_parts(gate_pre):
    tangent = jnp.tanh(gelu_c * (gate_pre + 0.044715 * gate_pre * gate_pre * gate_pre))
    activated = 0.5 * gate_pre * (1.0 + tangent)
    slope = 0.5 * (1.0 + tangent) + 0.5 * gate_pre * (1.0 - tangent * tangent) * gelu_c * (
        1.0 + 3.0 * 0.044715 * gate_pre * gate_pre
    )
    return (activated, slope)


def block_terms(weights, token_block, cot, scale):
    half = cot.shape[0]
    pre = (
        lax.dot_general(
            weights, token_block, (((1,), (1,)), ((), ())), preferred_element_type=jnp.float32
        )
        * scale
    )
    activated, slope = gelu_parts(pre[:half])
    gate_cot = (cot * pre[half:] * slope).astype(jnp.bfloat16)
    up_cot = (cot * activated).astype(jnp.bfloat16)
    return jnp.dot(
        jnp.concatenate([gate_cot, up_cot], axis=0),
        token_block,
        preferred_element_type=jnp.float32,
    )


def step_kernel(count, first, last, scale, ids, rate, w_ref, *refs):
    tokens = refs[: 2 * count]
    cots = refs[2 * count : 6 * count]
    refs = refs[6 * count :]
    rows, width = w_ref.shape[1], w_ref.shape[2]
    weights = w_ref[...].reshape(2 * rows, width)
    total = None
    if not first:
        total = refs[0][...].reshape(2 * rows, width)
        refs = refs[1:]
    for j in range(2 * count):
        cot = jnp.concatenate([cots[2 * j][0], cots[2 * j + 1][0]], axis=1).astype(jnp.float32)
        part = block_terms(weights, tokens[j][...], cot, scale)
        total = part if total is None else total + part
    if not last:
        refs[0][...] = total.reshape(2, rows, width)
        return
    moments = refs[0]
    outs = refs[1:]
    learning = rate[0]
    for p in range(2):
        grad = total[p * rows : (p + 1) * rows] * scale
        first_new = 0.9 * moments[p].astype(jnp.float32) + 0.1 * grad
        second_new = 0.95 * moments[2 + p].astype(jnp.float32) + 0.05 * grad * grad
        update = learning * (first_new / bias_first) / (jnp.sqrt(second_new / bias_second) + 1e-08)
        outs[p][0] = (w_ref[p].astype(jnp.float32) - update).astype(jnp.bfloat16)
        outs[2 + p][0] = first_new.astype(jnp.bfloat16)
        outs[4 + p][0] = second_new.astype(jnp.bfloat16)


def step(blocks, ids, rate, weights, cot, total, moments, scale):
    count = len(blocks) // 2
    hidden, width = weights.shape[1], weights.shape[2]
    rows = hidden // halves
    first, last = total is None, moments is not None
    tokens = blocks[0].shape[0]

    def cot_map(k, i, ids, rate):
        return (ids[k], i, 0)

    def rows_map(i, ids, rate):
        return (0, i, 0)

    in_specs = [pl.BlockSpec((2, rows, width), rows_map)]
    in_specs += [pl.BlockSpec((tokens, width), lambda i, ids, rate: (0, 0))] * (2 * count)
    in_specs += [
        pl.BlockSpec((1, rows, cot.shape[2]), functools.partial(cot_map, k))
        for k in range(4 * count)
    ]
    args = [weights, *blocks, *([cot] * (4 * count))]
    if not first:
        in_specs.append(pl.BlockSpec((2, rows, width), rows_map))
        args.append(total)
    if last:
        in_specs.append(pl.BlockSpec((4, rows, width), rows_map))
        args.append(moments)
        out_shape = [jax.ShapeDtypeStruct((1, hidden, width), jnp.bfloat16)] * 6
        out_specs = [pl.BlockSpec((1, rows, width), rows_map)] * 6
    else:
        out_shape = jax.ShapeDtypeStruct((2, hidden, width), jnp.float32)
        out_specs = pl.BlockSpec((2, rows, width), rows_map)
    flops = 2 * 2 * (2 * hidden) * width * tokens * 2 * count
    return pl.pallas_call(
        functools.partial(step_kernel, count, first, last, scale),
        grid_spec=pltpu.PrefetchScalarGridSpec(
            num_scalar_prefetch=2, grid=(halves,), in_specs=in_specs, out_specs=out_specs
        ),
        out_shape=out_shape,
        compiler_params=pltpu.CompilerParams(vmem_limit_bytes=48 * 2**20),
        cost_estimate=pl.CostEstimate(
            flops=flops, bytes_accessed=10 * 2**20, transcendentals=hidden * tokens * 2 * count
        ),
    )(ids, rate, *args)


def pick_kernel(winner, held_ref, out_ref):
    out_ref[...] = held_ref[...]


def pick(held, winner):
    shape = held.shape
    return pl.pallas_call(
        pick_kernel,
        grid_spec=pltpu.PrefetchScalarGridSpec(
            num_scalar_prefetch=1,
            grid=(shape[0],),
            in_specs=[pl.BlockSpec((1,) + shape[1:], lambda i, winner: (winner[i], 0, 0))],
            out_specs=pl.BlockSpec((1,) + shape[1:], lambda i, winner: (i, 0, 0)),
        ),
        out_shape=jax.ShapeDtypeStruct(shape, held.dtype),
        cost_estimate=pl.CostEstimate(
            flops=0, bytes_accessed=4 * held.size, transcendentals=0
        ),
    )(winner, held)


def copy_winner(arrays, winner):
    members = lax.axis_size("member")
    whole = jnp.concatenate(arrays, axis=0)
    count, rows, width = whole.shape
    pieces = whole.reshape(members, count * rows // members, width)
    held = lax.all_to_all(pieces, "member", 0, 0, tiled=True)
    returned = lax.all_to_all(pick(held, winner), "member", 0, 0, tiled=True)
    return returned.reshape(count, rows, width)


def body(
    tokens,
    cotangent,
    gate_weight,
    up_weight,
    gate_first,
    up_first,
    gate_second,
    up_second,
    winner,
    rate_index,
):
    own = tokens[0]
    scale = own.shape[1] ** (-0.5)
    me = lax.axis_index("fsdp")
    z, low, core = me // 4, (me // 2) % 2, me % 2
    with jax.named_scope("gather"):
        block = jnp.concatenate([own, lax.ppermute(own, "fsdp", low_swap)], axis=0)
        up, down = block, block
        chunks = [(0, block)]
        for hop in range(1, 5):
            if hop < 4:
                up = lax.ppermute(up, "fsdp", z_up)
                chunks.append((-hop, up))
            down = lax.ppermute(down, "fsdp", z_down)
            chunks.append((hop, down))
        partners = [lax.ppermute(c, "fsdp", core_swap) for _, c in chunks]
    with jax.named_scope("cotangent"):
        turned = cotangent[0].T.reshape(32, cotangent.shape[2] // 32, cotangent.shape[1])
        cot = lax.all_to_all(turned, "fsdp", 0, 0, tiled=True)
    with jax.named_scope("weights"):
        weights = copy_winner([gate_weight, up_weight], winner)
    with jax.named_scope("moments"):
        moments = copy_winner([gate_first, up_first, gate_second, up_second], winner)
    learning = 0.2 * jnp.exp2(
        (rate_index[lax.axis_index("member")].astype(jnp.float32) - 2.0) * 0.5
    )
    rate = jnp.full((1,), learning, jnp.float32)

    def sources(offset):
        at = (z + offset + nz) % nz
        return [
            device(at, low, core),
            device(at, 1 - low, core),
            device(at, low, 1 - core),
            device(at, 1 - low, 1 - core),
        ]

    total = None
    groups = [[0], [1, 2], [3, 4], [5, 6], [7]]
    for number, group in enumerate(groups):
        blocks, ids = [], []
        for g in group:
            blocks += [chunks[g][1], partners[g]]
            ids += sources(chunks[g][0])
        last = number == len(groups) - 1
        with jax.named_scope("terms"):
            total = step(
                blocks,
                jnp.stack(ids).astype(jnp.int32),
                rate,
                weights,
                cot,
                total,
                moments if last else None,
                scale,
            )
    return tuple(total)


def solution(mesh):
    spread = P("member", "fsdp", None)
    return jax.shard_map(
        body,
        mesh=mesh,
        in_specs=(spread,) * 8 + (P(), P()),
        out_specs=(spread,) * 6,
        check_vma=False,
    )
```

time: 314 us -> 297 us (0.946)
  Pallas kernels: 0 us -> 58.6 us
  matrix products: 49.6 us -> 0 us
  local copies, waits for them, and re-layouts: 47.3 us -> 9.69 us
  blocking collectives: 0 us -> 29.7 us
  waiting for transfers between devices: 168 us -> 144 us
  starting transfers between devices: 22.6 us -> 45.4 us
  between operations: 14.9 us -> 1.75 us
  other arithmetic: 10.5 us -> 5.73 us
    all_to_all x3 -> x4, waiting for transfers between devices: 168 us -> 61.2 us  [the longest x1 42.5 us: copy_winner(): held = lax.all_to_all(pieces, 'member', 0, 0, tiled=True)]
    ppermute x0 -> x16, waiting for transfers between devices: none -> 83.1 us  [the longest x4 62 us: body(): down = lax.ppermute(down, 'fsdp', z_down)]
    pallas_call x0 -> x7, Pallas kernels: none -> 58.6 us  [the longest x5 45.3 us: step(): pl.pallas_call(functools.partial(step_kernel, count, first, last, scale),...]
    dot_general x3 -> x0, matrix products: 49.6 us -> none  [the longest x2 38 us: weight_grad(): lax.dot_general(cot_block, token_block, contract, preferred_element_type=...]
    all_to_all x0 -> x1, blocking collectives: none -> 29.7 us  [copy_winner(): held = lax.all_to_all(pieces, 'member', 0, 0, tiled=True)]
    ppermute x0 -> x16, starting transfers between devices: none -> 21.7 us  [the longest x4 10.9 us: body(): down = lax.ppermute(down, 'fsdp', z_down)]
    reshape x2 -> x0, local copies, waits for them, and re-layouts: 12.7 us -> none  [body(): pieces = bundle.reshape(6, members, portion, width)]
    mul x4 -> x0, local copies, waits for them, and re-layouts: 8.23 us -> none  [the longest x2 4.17 us: adam_update(): second_new = 0.95 * moment_two.astype(jnp.float32) + 0.05 * grad * grad]
  transfers between devices with their start and end apart: 4 -> 20, of which waited for: 3 -> 7; matrix products, arithmetic and copies ran while one was open for 22% -> 3% of each run, Pallas kernels for 0% -> 14%
where the time goes in v1:
time: 297 us; the launch traced here: 295 us
  waiting for transfers between devices  144 us (48%)
  Pallas kernels  58.6 us (20%)
  starting transfers between devices  45.4 us (15%)
  blocking collectives  29.7 us (10%)
  local copies, waits for them, and re-layouts  9.69 us (3%)
  other arithmetic  5.73 us (2%)
    ppermute x4, waiting for transfers between devices, body(): down = lax.ppermute(down, 'fsdp', z_down)  62 us
    pallas_call x5, Pallas kernels, step(): pl.pallas_call(functools.partial(step_kernel, count, first, last, scale),...  45.3 us
    all_to_all x1, waiting for transfers between devices, copy_winner(): held = lax.all_to_all(pieces, 'member', 0, 0, tiled=True)  42.5 us
    all_to_all x1, blocking collectives, copy_winner(): held = lax.all_to_all(pieces, 'member', 0, 0, tiled=True)  29.7 us
    ppermute x1, waiting for transfers between devices, body(): block = jnp.concatenate([own, lax.ppermute(own, 'fsdp', low_swap)], axis=0)  21 us
    all_to_all x2, waiting for transfers between devices, copy_winner(): returned = lax.all_to_all(pick(held, winner), 'member', 0, 0, tiled=True)  18.8 us
    pallas_call x2, Pallas kernels, pick(): pl.pallas_call(pick_kernel, grid_spec=pltpu.PrefetchScalarGridSpec(num_sc...  13.3 us
    all_to_all x1, starting transfers between devices, body(): cot = lax.all_to_all(turned, 'fsdp', 0, 0, tiled=True)  11 us
  transfers between devices with their start and end apart: 20, of which 7 were waited for; matrix products, arithmetic and copies ran while one was open for 3% of the time, Pallas kernels for 14%

profile of v1, /device:TPU:1, one launch (start us, length us, event | category | flops | bytes accessed | tf_op | source)
XLA Modules:
  0.0 295.1 jit_solution(14193718903402455106)
XLA Ops:
  0.6 1.5 pad_maximum_fusion.1
  2.2 29.7 %all_to_all.25.held_ref = bf16[8,56,1792]{2,1,0:T(8,128)(2,1)} all-to-all(bf16[8,56,1792]{2,1,0:T(8,128)(2,1)S(1)} %bitcast.48), channel_id=1, replica_groups=mesh['member'=8,'fsdp'=32] {'member'}, dimensions={0} | all-to-all | bytes 3211264 | tf_op jit(solution)/shard_map/weights/all_to_all | solution.py:156
  31.8 6.3 %weights.1 = bf16[8,56,1792]{2,1,0:T(8,128)(2,1)} custom-call(s32[8]{0:T(128)} %winner.3, bf16[8,56,1792]{2,1,0:T(8,128)(2,1)} %all_to_all.25.held_ref), custom_call_target="tpu_custom_call" | custom-call | bytes 3211264 | tf_op jit(solution)/shard_map/weights/pallas_call | solution.py:136
  38.1 3.6 %all-to-all-start.1 = ((bf16[8,56,1792]{2,1,0:T(8,128)(2,1)}), bf16[8,56,1792]{2,1,0:T(8,128)(2,1)S(1)}, u32[]{:S(2)}, u32[]{:S(2)}) async-start(bf16[8,56,1792]{2,1,0:T(8,128)(2,1)} %weights.1), calls=%async_computation.1 | async-start | bytes 3211264 | tf_op jit(solution)/shard_map/weights/all_to_all | solution.py:157
  41.7 3.0 %pad_maximum_fusion = bf16[4,224,1792]{2,1,0:T(8,128)(2,1)} fusion(bf16[1,224,1792]{2,1,0:T(8,128)(2,1)S(1)} %copy-done.11, bf16[1,224,1792]{2,1,0:T(8,128)(2,1)S(1)} %copy-done.12, bf16[1,224,1792]{2,1,0:T(8,128)(2,1)} %param.15, bf16[1,224,1792]{2,1,0:T(8,128)(2,1)} %param.14), kind=kLoop, calls=%fused_computation | loop fusion | flops 4816896 | bytes 6422528 | tf_op jit(solution)/shard_map/moments/concatenate | solution.py:153
  44.7 18.8 %all-to-all-done.1 = bf16[8,56,1792]{2,1,0:T(8,128)(2,1)S(1)} async-done(((bf16[8,56,1792]{2,1,0:T(8,128)(2,1)}), bf16[8,56,1792]{2,1,0:T(8,128)(2,1)S(1)}, u32[]{:S(2)}, u32[]{:S(2)}) %all-to-all-start.1) | async-done | bytes 1605664 | tf_op jit(solution)/shard_map/weights/all_to_all | solution.py:157
  63.5 4.6 %all-to-all-start.3 = ((bf16[8,112,1792]{2,1,0:T(8,128)(2,1)}), bf16[8,112,1792]{2,1,0:T(8,128)(2,1)}, u32[]{:S(2)}, u32[]{:S(2)}) async-start(bf16[8,112,1792]{2,1,0:T(8,128)(2,1)} %bitcast.46), calls=%async_computation.3 | async-start | bytes 6422528 | tf_op jit(solution)/shard_map/moments/all_to_all | solution.py:156
  68.1 2.4 copy.16
  70.5 42.5 %all-to-all-done.3.held_ref = bf16[8,112,1792]{2,1,0:T(8,128)(2,1)} async-done(((bf16[8,112,1792]{2,1,0:T(8,128)(2,1)}), bf16[8,112,1792]{2,1,0:T(8,128)(2,1)}, u32[]{:S(2)}, u32[]{:S(2)}) %all-to-all-start.3) | async-done | bytes 3211296 | tf_op jit(solution)/shard_map/moments/all_to_all | solution.py:156
  112.9 11.0 %all-to-all-start.2 = ((bf16[32,224,128]{2,1,0:T(8,128)(2,1)}), bf16[32,224,128]{2,1,0:T(8,128)(2,1)S(1)}, u32[]{:S(2)}, u32[]{:S(2)}) async-start(bf16[32,224,128]{2,1,0:T(8,128)(2,1)} %bitcast.47), calls=%async_computation.2 | async-start | bytes 3670016 | tf_op jit(solution)/shard_map/cotangent/all_to_all | solution.py:190
  123.9 1.5 collective-permute-start
  125.4 21.0 %collective-permute-done = bf16[128,1792]{1,0:T(8,128)(2,1)S(1)} collective-permute-done((bf16[128,1792]{1,0:T(8,128)(2,1)}, bf16[128,1792]{1,0:T(8,128)(2,1)S(1)}, u32[]{:S(2)}, u32[]{:S(2)}) %collective-permute-start) | collective-permute-done | bytes 458784 | tf_op jit(solution)/shard_map/gather/ppermute | solution.py:178
  146.4 1.1 pad_maximum_fusion.2.refs_0_
  147.5 3.1 %collective-permute-start.1 = (bf16[256,1792]{1,0:T(8,128)(2,1)S(1)}, bf16[256,1792]{1,0:T(8,128)(2,1)}, u32[]{:S(2)}, u32[]{:S(2)}) collective-permute-start(bf16[256,1792]{1,0:T(8,128)(2,1)S(1)} %pad_maximum_fusion.2.refs_0_), channel_id=1, source_target_pairs={{4,0},{5,1},{6,2},{7,3},{8,4},{9,5},{10,6},{11,7},{12,8},{13,9},{1... | collective-permute-start | bytes 2752520 | tf_op jit(solution)/shard_map/gather/ppermute | solution.py:185
  150.6 0.1 collective-permute-start.6
  150.7 34.6 %collective-permute-done.1.refs_2_ = bf16[256,1792]{1,0:T(8,128)(2,1)} collective-permute-done((bf16[256,1792]{1,0:T(8,128)(2,1)S(1)}, bf16[256,1792]{1,0:T(8,128)(2,1)}, u32[]{:S(2)}, u32[]{:S(2)}) %collective-permute-start.1) | collective-permute-done | bytes 917536 | tf_op jit(solution)/shard_map/gather/ppermute | solution.py:185
  185.3 1.5 collective-permute-start.2
  186.7 7.0 %moments.1 = bf16[8,112,1792]{2,1,0:T(8,128)(2,1)} custom-call(s32[8]{0:T(128)} %winner.3, bf16[8,112,1792]{2,1,0:T(8,128)(2,1)} %all-to-all-done.3.held_ref), custom_call_target="tpu_custom_call" | custom-call | bytes 6422528 | tf_op jit(solution)/shard_map/moments/pallas_call | solution.py:136
  193.7 4.5 %all-to-all-start.4 = ((bf16[8,112,1792]{2,1,0:T(8,128)(2,1)}), bf16[8,112,1792]{2,1,0:T(8,128)(2,1)}, u32[]{:S(2)}, u32[]{:S(2)}) async-start(bf16[8,112,1792]{2,1,0:T(8,128)(2,1)} %moments.1), calls=%async_computation.4 | async-start | bytes 6422528 | tf_op jit(solution)/shard_map/moments/all_to_all | solution.py:157
  198.2 8.4 %collective-permute-done.2.refs_2_ = bf16[256,1792]{1,0:T(8,128)(2,1)} collective-permute-done((bf16[256,1792]{1,0:T(8,128)(2,1)}, bf16[256,1792]{1,0:T(8,128)(2,1)}, u32[]{:S(2)}, u32[]{:S(2)}) %collective-permute-start.2) | collective-permute-done | bytes 917536 | tf_op jit(solution)/shard_map/gather/ppermute | solution.py:185
  206.6 2.9 collective-permute-start.3
  209.5 1.8 collective-permute-start.15
  211.3 0.5 collective-permute-start.14
  211.8 16.0 %collective-permute-done.3.refs_2_ = bf16[256,1792]{1,0:T(8,128)(2,1)} collective-permute-done((bf16[256,1792]{1,0:T(8,128)(2,1)}, bf16[256,1792]{1,0:T(8,128)(2,1)}, u32[]{:S(2)}, u32[]{:S(2)}) %collective-permute-start.3) | collective-permute-done | bytes 917536 | tf_op jit(solution)/shard_map/gather/ppermute | solution.py:185
  227.9 3.4 %collective-permute-start.4 = (bf16[256,1792]{1,0:T(8,128)(2,1)}, bf16[256,1792]{1,0:T(8,128)(2,1)}, u32[]{:S(2)}, u32[]{:S(2)}) collective-permute-start(bf16[256,1792]{1,0:T(8,128)(2,1)} %collective-permute-done.3.refs_2_), channel_id=1, source_target_pairs={{4,0},{5,1},{6,2},{7,3},{8,4},{9,5},{10,6},{11,7},{12,8},{13,9},{1... | collective-permute-start | bytes 2752520 | tf_op jit(solution)/shard_map/gather/ppermute | solution.py:185
  231.3 1.0 copy-done.4
  232.3 2.8 collective-permute-start.11
  235.1 0.9 copy-done.6
  236.0 0.0 collective-permute-start.12
  236.0 0.5 collective-permute-start.10
  236.5 0.3 collective-permute-start.9
  236.8 0.1 pad_add_fusion.1.ids
  237.0 0.6 dynamic_slice.3
  238.3 0.1 stack.142.ids
  238.4 0.1 stack.133.ids
  238.4 0.1 stack.124.ids
  238.5 0.1 pad_add_fusion.ids
  238.6 1.2 copy-done.3
  239.8 1.2 copy-done.5
  241.0 4.7 %terms.5.refs_12_ = f32[2,224,1792]{2,1,0:T(8,128)} custom-call(s32[4]{0:T(128)S(1)} %pad_add_fusion.1.ids, f32[1]{0:T(128)S(6)} %mul_shard_map.4.rate, bf16[2,224,1792]{2,1,0:T(8,128)(2,1)S(1)} %bitcast.41, bf16[256,1792]{1,0:T(8,128)(2,1)S(1)} %copy-done.3, bf16[256,1792]{1,0:T(8,128)(2,1)S(1)} %copy-done.5, ...), custom_call_target="tpu_custom_call" | custom-call | flops 1644167168 | bytes 10485760 | tf_op jit(solution)/shard_map/terms/pallas_call | solution.py:117
  245.7 3.1 %collective-permute-done.4.refs_0_ = bf16[256,1792]{1,0:T(8,128)(2,1)} collective-permute-done((bf16[256,1792]{1,0:T(8,128)(2,1)}, bf16[256,1792]{1,0:T(8,128)(2,1)}, u32[]{:S(2)}, u32[]{:S(2)}) %collective-permute-start.4) | collective-permute-done | bytes 917536 | tf_op jit(solution)/shard_map/gather/ppermute | solution.py:185
  248.8 3.4 %collective-permute-start.5 = (bf16[256,1792]{1,0:T(8,128)(2,1)}, bf16[256,1792]{1,0:T(8,128)(2,1)S(1)}, u32[]{:S(2)}, u32[]{:S(2)}) collective-permute-start(bf16[256,1792]{1,0:T(8,128)(2,1)} %collective-permute-done.4.refs_0_), channel_id=1, source_target_pairs={{0,1},{1,0},{2,3},{3,2},{4,5},{5,4},{6,7},{7,6},{8,9},{9,8},{10,11... | collective-permute-start | bytes 2752520 | tf_op jit(solution)/shard_map/gather/ppermute | solution.py:187
  252.2 10.1 %terms.6.refs_12_ = f32[2,224,1792]{2,1,0:T(8,128)} custom-call(s32[8]{0:T(128)S(1)} %stack.142.ids, f32[1]{0:T(128)S(6)} %mul_shard_map.4.rate, bf16[2,224,1792]{2,1,0:T(8,128)(2,1)S(1)} %bitcast.42, bf16[256,1792]{1,0:T(8,128)(2,1)} %collective-permute-done.6.refs_0_, bf16[256,1792]{1,0:T(8,128)(2,1)S(1)} %copy-done.7, ...), custom_call_target="tpu_custom_call" | custom-call | flops 3288334336 | bytes 10485760 | tf_op jit(solution)/shard_map/terms/pallas_call | solution.py:117
  262.2 10.3 %terms.7.refs_12_ = f32[2,224,1792]{2,1,0:T(8,128)} custom-call(s32[8]{0:T(128)S(1)} %stack.133.ids, f32[1]{0:T(128)S(6)} %mul_shard_map.4.rate, bf16[2,224,1792]{2,1,0:T(8,128)(2,1)S(1)} %bitcast.43, bf16[256,1792]{1,0:T(8,128)(2,1)} %collective-permute-done.7.refs_0_, bf16[256,1792]{1,0:T(8,128)(2,1)} %collective-permute-done.11.refs_1_, ...), custom_call_target="tpu_custom_call" | custom-call | flops 3288334336 | bytes 10485760 | tf_op jit(solution)/shard_map/terms/pallas_call | solution.py:117
  272.6 10.3 %terms.8.refs_6_ = f32[2,224,1792]{2,1,0:T(8,128)} custom-call(s32[8]{0:T(128)S(1)} %stack.124.ids, f32[1]{0:T(128)S(6)} %mul_shard_map.4.rate, bf16[2,224,1792]{2,1,0:T(8,128)(2,1)S(1)} %bitcast.44, bf16[256,1792]{1,0:T(8,128)(2,1)} %collective-permute-done.8.refs_0_, bf16[256,1792]{1,0:T(8,128)(2,1)} %collective-permute-done.9.refs_1_, ...), custom_call_target="tpu_custom_call" | custom-call | flops 3288334336 | bytes 10485760 | tf_op jit(solution)/shard_map/terms/pallas_call | solution.py:117
  282.9 0.9 copy-done.8
  283.8 1.2 copy-done.9
  285.0 10.0 %terms.9 = (bf16[1,224,1792]{2,1,0:T(8,128)(2,1)}, bf16[1,224,1792]{2,1,0:T(8,128)(2,1)}, bf16[1,224,1792]{2,1,0:T(8,128)(2,1)}, bf16[1,224,1792]{2,1,0:T(8,128)...) custom-call(s32[4]{0:T(128)S(1)} %pad_add_fusion.ids, f32[1]{0:T(128)S(6)} %mul_shard_map.4.rate, ...), custom_call_target="tpu_custom_call" | custom-call | flops 1644167168 | bytes 10485760 | tf_op jit(solution)/shard_map/terms/pallas_call | solution.py:117
  (38 shorter events, 0.1 us)
Async XLA Ops:
  31.8 9.9 %copy-start.11 = (bf16[1,224,1792]{2,1,0:T(8,128)(2,1)S(1)}, bf16[1,224,1792]{2,1,0:T(8,128)(2,1)}, u32[]{:S(2)}) copy-start(bf16[1,224,1792]{2,1,0:T(8,128)(2,1)} %param.17) | copy-start | bytes 2408452
  31.8 9.9 %copy-start.12 = (bf16[1,224,1792]{2,1,0:T(8,128)(2,1)S(1)}, bf16[1,224,1792]{2,1,0:T(8,128)(2,1)}, u32[]{:S(2)}) copy-start(bf16[1,224,1792]{2,1,0:T(8,128)(2,1)} %param.16) | copy-start | bytes 2408452
  38.1 25.4 %all-to-all-start.1 = ((bf16[8,56,1792]{2,1,0:T(8,128)(2,1)}), bf16[8,56,1792]{2,1,0:T(8,128)(2,1)S(1)}, u32[]{:S(2)}, u32[]{:S(2)}) async-start(bf16[8,56,1792]{2,1,0:T(8,128)(2,1)} %weights.1), calls=%async_computation.1 | async-start | bytes 3211264 | tf_op jit(solution)/shard_map/weights/all_to_all | solution.py:157
  63.5 4.6 %copy-start.10 = (bf16[1,128,7168]{2,1,0:T(8,128)(2,1)S(1)}, bf16[1,128,7168]{2,1,0:T(8,128)(2,1)}, u32[]{:S(2)}) copy-start(bf16[1,128,7168]{2,1,0:T(8,128)(2,1)} %param.11) | copy-start | bytes 5505028
  63.5 49.4 %all-to-all-start.3 = ((bf16[8,112,1792]{2,1,0:T(8,128)(2,1)}), bf16[8,112,1792]{2,1,0:T(8,128)(2,1)}, u32[]{:S(2)}, u32[]{:S(2)}) async-start(bf16[8,112,1792]{2,1,0:T(8,128)(2,1)} %bitcast.46), calls=%async_computation.3 | async-start | bytes 6422528 | tf_op jit(solution)/shard_map/moments/all_to_all | solution.py:156
  112.9 80.8 %all-to-all-start.2 = ((bf16[32,224,128]{2,1,0:T(8,128)(2,1)}), bf16[32,224,128]{2,1,0:T(8,128)(2,1)S(1)}, u32[]{:S(2)}, u32[]{:S(2)}) async-start(bf16[32,224,128]{2,1,0:T(8,128)(2,1)} %bitcast.47), calls=%async_computation.2 | async-start | bytes 3670016 | tf_op jit(solution)/shard_map/cotangent/all_to_all | solution.py:190
  123.9 22.5 %collective-permute-start = (bf16[128,1792]{1,0:T(8,128)(2,1)}, bf16[128,1792]{1,0:T(8,128)(2,1)S(1)}, u32[]{:S(2)}, u32[]{:S(2)}) collective-permute-start(bf16[128,1792]{1,0:T(8,128)(2,1)} %bitcast.50), channel_id=1, source_target_pairs={{0,2},{1,3},{2,0},{3,1},{4,6},{5,7},{6,4},{7,5},{8,10},{9,11},{10,... | collective-permute-start | bytes 1376264 | tf_op jit(solution)/shard_map/gather/ppermute | solution.py:178
  147.5 3.1 %copy-start.2 = (bf16[256,1792]{1,0:T(8,128)(2,1)}, bf16[256,1792]{1,0:T(8,128)(2,1)S(1)}, u32[]{:S(2)}) copy-start(bf16[256,1792]{1,0:T(8,128)(2,1)S(1)} %pad_maximum_fusion.2.refs_0_) | copy-start | bytes 2752516
  147.5 37.7 %collective-permute-start.1 = (bf16[256,1792]{1,0:T(8,128)(2,1)S(1)}, bf16[256,1792]{1,0:T(8,128)(2,1)}, u32[]{:S(2)}, u32[]{:S(2)}) collective-permute-start(bf16[256,1792]{1,0:T(8,128)(2,1)S(1)} %pad_maximum_fusion.2.refs_0_), channel_id=1, source_target_pairs={{4,0},{5,1},{6,2},{7,3},{8,4},{9,5},{10,6},{11,7},{12,8},{13,9},{1... | collective-permute-start | bytes 2752520 | tf_op jit(solution)/shard_map/gather/ppermute | solution.py:185
  150.6 36.1 %collective-permute-start.6 = (bf16[256,1792]{1,0:T(8,128)(2,1)S(1)}, bf16[256,1792]{1,0:T(8,128)(2,1)}, u32[]{:S(2)}, u32[]{:S(2)}) collective-permute-start(bf16[256,1792]{1,0:T(8,128)(2,1)S(1)} %pad_maximum_fusion.2.refs_0_), channel_id=1, source_target_pairs={{0,4},{1,5},{2,6},{3,7},{4,8},{5,9},{6,10},{7,11},{8,12},{9,13},{1... | collective-permute-start | bytes 2752520 | tf_op jit(solution)/shard_map/gather/ppermute | solution.py:183
  185.3 21.3 %collective-permute-start.2 = (bf16[256,1792]{1,0:T(8,128)(2,1)}, bf16[256,1792]{1,0:T(8,128)(2,1)}, u32[]{:S(2)}, u32[]{:S(2)}) collective-permute-start(bf16[256,1792]{1,0:T(8,128)(2,1)} %collective-permute-done.1.refs_2_), channel_id=1, source_target_pairs={{4,0},{5,1},{6,2},{7,3},{8,4},{9,5},{10,6},{11,7},{12,8},{13,9},{1... | collective-permute-start | bytes 2752520 | tf_op jit(solution)/shard_map/gather/ppermute | solution.py:185
  186.7 25.1 %collective-permute-start.7 = (bf16[256,1792]{1,0:T(8,128)(2,1)}, bf16[256,1792]{1,0:T(8,128)(2,1)}, u32[]{:S(2)}, u32[]{:S(2)}) collective-permute-start(bf16[256,1792]{1,0:T(8,128)(2,1)} %collective-permute-done.6.refs_0_), channel_id=1, source_target_pairs={{0,4},{1,5},{2,6},{3,7},{4,8},{5,9},{6,10},{7,11},{8,12},{9,13},{1... | collective-permute-start | bytes 2752520 | tf_op jit(solution)/shard_map/gather/ppermute | solution.py:183
  193.7 43.3 %copy-start.13 = (s32[8]{0:T(128)S(1)}, s32[8]{0:T(128)}, u32[]{:S(2)}) copy-start(s32[8]{0:T(128)} %param.19) | copy-start | bytes 100
  193.7 44.9 %copy-start = (bf16[32,224,128]{2,1,0:T(8,128)(2,1)}, bf16[32,224,128]{2,1,0:T(8,128)(2,1)S(1)}, u32[]{:S(2)}) copy-start(bf16[32,224,128]{2,1,0:T(8,128)(2,1)S(1)} %all-to-all-done.2.refs_2_.refs_3_.refs_4_.refs_5_.refs_6_.refs_7_.refs_8_.refs_9_.refs_10_.refs_11_) | copy-start | bytes 5505028
  193.7 90.1 %all-to-all-start.4 = ((bf16[8,112,1792]{2,1,0:T(8,128)(2,1)}), bf16[8,112,1792]{2,1,0:T(8,128)(2,1)}, u32[]{:S(2)}, u32[]{:S(2)}) async-start(bf16[8,112,1792]{2,1,0:T(8,128)(2,1)} %moments.1), calls=%async_computation.4 | async-start | bytes 6422528 | tf_op jit(solution)/shard_map/moments/all_to_all | solution.py:157
  206.6 21.3 %collective-permute-start.3 = (bf16[256,1792]{1,0:T(8,128)(2,1)}, bf16[256,1792]{1,0:T(8,128)(2,1)}, u32[]{:S(2)}, u32[]{:S(2)}) collective-permute-start(bf16[256,1792]{1,0:T(8,128)(2,1)} %collective-permute-done.2.refs_2_), channel_id=1, source_target_pairs={{4,0},{5,1},{6,2},{7,3},{8,4},{9,5},{10,6},{11,7},{12,8},{13,9},{1... | collective-permute-start | bytes 2752520 | tf_op jit(solution)/shard_map/gather/ppermute | solution.py:185
  209.5 21.8 %collective-permute-start.15 = (bf16[256,1792]{1,0:T(8,128)(2,1)}, bf16[256,1792]{1,0:T(8,128)(2,1)S(1)}, u32[]{:S(2)}, u32[]{:S(2)}) collective-permute-start(bf16[256,1792]{1,0:T(8,128)(2,1)} %copy-done.2), channel_id=1, source_target_pairs={{0,1},{1,0},{2,3},{3,2},{4,5},{5,4},{6,7},{7,6},{8,9},{9,8},{10,11... | collective-permute-start | bytes 2752520 | tf_op jit(solution)/shard_map/gather/ppermute | solution.py:187
  211.3 23.8 %collective-permute-start.13 = (bf16[256,1792]{1,0:T(8,128)(2,1)}, bf16[256,1792]{1,0:T(8,128)(2,1)S(1)}, u32[]{:S(2)}, u32[]{:S(2)}) collective-permute-start(bf16[256,1792]{1,0:T(8,128)(2,1)} %collective-permute-done.6.refs_0_), channel_id=1, source_target_pairs={{0,1},{1,0},{2,3},{3,2},{4,5},{5,4},{6,7},{7,6},{8,9},{9,8},{10,11... | collective-permute-start | bytes 2752520 | tf_op jit(solution)/shard_map/gather/ppermute | solution.py:187
  211.3 24.7 %collective-permute-start.14 = (bf16[256,1792]{1,0:T(8,128)(2,1)}, bf16[256,1792]{1,0:T(8,128)(2,1)}, u32[]{:S(2)}, u32[]{:S(2)}) collective-permute-start(bf16[256,1792]{1,0:T(8,128)(2,1)} %collective-permute-done.1.refs_2_), channel_id=1, source_target_pairs={{0,1},{1,0},{2,3},{3,2},{4,5},{5,4},{6,7},{7,6},{8,9},{9,8},{10,11... | collective-permute-start | bytes 2752520 | tf_op jit(solution)/shard_map/gather/ppermute | solution.py:187
  211.8 24.7 %collective-permute-start.8 = (bf16[256,1792]{1,0:T(8,128)(2,1)}, bf16[256,1792]{1,0:T(8,128)(2,1)}, u32[]{:S(2)}, u32[]{:S(2)}) collective-permute-start(bf16[256,1792]{1,0:T(8,128)(2,1)} %collective-permute-done.7.refs_0_), channel_id=1, source_target_pairs={{0,4},{1,5},{2,6},{3,7},{4,8},{5,9},{6,10},{7,11},{8,12},{9,13},{1... | collective-permute-start | bytes 2752520 | tf_op jit(solution)/shard_map/gather/ppermute | solution.py:183
  227.9 20.9 %collective-permute-start.4 = (bf16[256,1792]{1,0:T(8,128)(2,1)}, bf16[256,1792]{1,0:T(8,128)(2,1)}, u32[]{:S(2)}, u32[]{:S(2)}) collective-permute-start(bf16[256,1792]{1,0:T(8,128)(2,1)} %collective-permute-done.3.refs_2_), channel_id=1, source_target_pairs={{4,0},{5,1},{6,2},{7,3},{8,4},{9,5},{10,6},{11,7},{12,8},{13,9},{1... | collective-permute-start | bytes 2752520 | tf_op jit(solution)/shard_map/gather/ppermute | solution.py:185
  231.3 1.0 copy-start.4
  232.3 29.9 %collective-permute-start.11 = (bf16[256,1792]{1,0:T(8,128)(2,1)}, bf16[256,1792]{1,0:T(8,128)(2,1)}, u32[]{:S(2)}, u32[]{:S(2)}) collective-permute-start(bf16[256,1792]{1,0:T(8,128)(2,1)} %collective-permute-done.7.refs_0_), channel_id=1, source_target_pairs={{0,1},{1,0},{2,3},{3,2},{4,5},{5,4},{6,7},{7,6},{8,9},{9,8},{10,11... | collective-permute-start | bytes 2752520 | tf_op jit(solution)/shard_map/gather/ppermute | solution.py:187
  235.1 0.9 copy-start.6
  236.0 26.2 %collective-permute-start.12 = (bf16[256,1792]{1,0:T(8,128)(2,1)}, bf16[256,1792]{1,0:T(8,128)(2,1)}, u32[]{:S(2)}, u32[]{:S(2)}) collective-permute-start(bf16[256,1792]{1,0:T(8,128)(2,1)} %collective-permute-done.2.refs_2_), channel_id=1, source_target_pairs={{0,1},{1,0},{2,3},{3,2},{4,5},{5,4},{6,7},{7,6},{8,9},{9,8},{10,11... | collective-permute-start | bytes 2752520 | tf_op jit(solution)/shard_map/gather/ppermute | solution.py:187
  236.0 36.6 %collective-permute-start.10 = (bf16[256,1792]{1,0:T(8,128)(2,1)}, bf16[256,1792]{1,0:T(8,128)(2,1)}, u32[]{:S(2)}, u32[]{:S(2)}) collective-permute-start(bf16[256,1792]{1,0:T(8,128)(2,1)} %collective-permute-done.3.refs_2_), channel_id=1, source_target_pairs={{0,1},{1,0},{2,3},{3,2},{4,5},{5,4},{6,7},{7,6},{8,9},{9,8},{10,11... | collective-permute-start | bytes 2752520 | tf_op jit(solution)/shard_map/gather/ppermute | solution.py:187
  236.5 36.1 %collective-permute-start.9 = (bf16[256,1792]{1,0:T(8,128)(2,1)}, bf16[256,1792]{1,0:T(8,128)(2,1)}, u32[]{:S(2)}, u32[]{:S(2)}) collective-permute-start(bf16[256,1792]{1,0:T(8,128)(2,1)} %collective-permute-done.8.refs_0_), channel_id=1, source_target_pairs={{0,1},{1,0},{2,3},{3,2},{4,5},{5,4},{6,7},{7,6},{8,9},{9,8},{10,11... | collective-permute-start | bytes 2752520 | tf_op jit(solution)/shard_map/gather/ppermute | solution.py:187
  238.6 1.2 copy-start.3
  239.8 1.2 copy-start.5
  241.0 11.2 %copy-start.7 = (bf16[256,1792]{1,0:T(8,128)(2,1)S(1)}, bf16[256,1792]{1,0:T(8,128)(2,1)}, u32[]{:S(2)}) copy-start(bf16[256,1792]{1,0:T(8,128)(2,1)} %copy-done.6) | copy-start | bytes 2752516
  248.8 34.1 %collective-permute-start.5 = (bf16[256,1792]{1,0:T(8,128)(2,1)}, bf16[256,1792]{1,0:T(8,128)(2,1)S(1)}, u32[]{:S(2)}, u32[]{:S(2)}) collective-permute-start(bf16[256,1792]{1,0:T(8,128)(2,1)} %collective-permute-done.4.refs_0_), channel_id=1, source_target_pairs={{0,1},{1,0},{2,3},{3,2},{4,5},{5,4},{6,7},{7,6},{8,9},{9,8},{10,11... | collective-permute-start | bytes 2752520 | tf_op jit(solution)/shard_map/gather/ppermute | solution.py:187
  272.6 11.3 %copy-start.1 = (bf16[32,224,128]{2,1,0:T(8,128)(2,1)S(1)}, bf16[32,224,128]{2,1,0:T(8,128)(2,1)}, u32[]{:S(2)}) copy-start(bf16[32,224,128]{2,1,0:T(8,128)(2,1)} %copy-done) | copy-start | bytes 5505028
  282.9 0.9 copy-start.8
  283.8 1.2 copy-start.9

commit v2 on v0

v2 whole, which is shorter than its diff:
```python
import functools

import jax
import jax.numpy as jnp
from jax import lax
from jax.experimental import pallas as pl
from jax.experimental.pallas import tpu as pltpu
from jax.sharding import PartitionSpec as P

gelu_c = 0.7978845608028654
bias_first = 1.0 - 0.9**10
bias_second = 1.0 - 0.95**10
nz = 8
tile = 256


def device(z, low, core):
    return (z * 2 + low) * 2 + core


everyone = [(z, low, core) for z in range(nz) for low in range(2) for core in range(2)]
z_up = [(device(z, a, c), device((z + 1) % nz, a, c)) for z, a, c in everyone]
z_down = [(b, a) for a, b in z_up]
core_swap = [(i, i ^ 1) for i in range(32)]
same_core = [[i for i in range(32) if i % 2 == core] for core in range(2)]
low_swap = [(i, i ^ 2) for i in range(32)]
row_swap = [(m, m ^ 1) for m in range(8)]


rows_of_members = [[m for m in range(8) if m % 2 == row] for row in range(2)]


def along_row(hops):
    return [(m, (m + 2 * hops) % 8) for m in range(8)]


def gelu_parts(gate_pre):
    tangent = jnp.tanh(gelu_c * (gate_pre + 0.044715 * gate_pre * gate_pre * gate_pre))
    activated = 0.5 * gate_pre * (1.0 + tangent)
    slope = 0.5 * (1.0 + tangent) + 0.5 * gate_pre * (1.0 - tangent * tangent) * gelu_c * (
        1.0 + 3.0 * 0.044715 * gate_pre * gate_pre
    )
    return (activated, slope)


def launch(copies):
    for copy in copies:
        copy.start()
    for copy in copies:
        copy.wait()


def terms_kernel(lengths, sources, first, scale, here, mine, theirs, cots, *refs):
    count = len(lengths)
    tokens, refs = refs[:count], refs[count:]
    if not first:
        kept, sent, refs = refs[:2], refs[2:4], refs[4:]
    keep, send = refs[:2], refs[2:4]
    x, c, w, grad, cot, sems = refs[4:]
    rows, hidden = mine.shape[1], 2 * mine.shape[1]
    me = here[1]
    z, low, core = me // 4, (me // 2) % 2, me % 2
    mine_at = pl.multiple_of(core * rows, 32)
    theirs_at = pl.multiple_of((1 - core) * rows, 32)
    pairs = []
    for p in range(2):
        pairs.append((mine.at[p], w.at[pl.ds(p * hidden + mine_at, rows)]))
        pairs.append((theirs.at[p], w.at[pl.ds(p * hidden + theirs_at, rows)]))
    at = 0
    for ref, length in zip(tokens, lengths):
        pairs.append((ref, x.at[pl.ds(at, length)]))
        at += length
    for k, (hops, other) in enumerate(sources):
        source = ((z + hops + nz) % nz) * 2 + (low + other) % 2
        pairs.append((cots.at[source], c.at[k]))
    ready = len(pairs)
    if not first:
        for p in range(2):
            pairs.append((kept[p], grad.at[pl.ds(p * hidden + mine_at, rows)]))
            pairs.append((sent[p], grad.at[pl.ds(p * hidden + theirs_at, rows)]))
    copies = [pltpu.make_async_copy(a, b, sems.at[k]) for k, (a, b) in enumerate(pairs)]
    for copy in copies:
        copy.start()
    for copy in copies[:ready]:
        copy.wait()

    @pl.loop(0, x.shape[0] // tile)
    def _(t):
        block = x[pl.ds(pl.multiple_of(t * tile, tile), tile), :]
        pre = (
            lax.dot_general(
                w[...], block, (((1,), (1,)), ((), ())), preferred_element_type=jnp.float32
            )
            * scale
        )
        value = jnp.concatenate([c[2 * t], c[2 * t + 1]], axis=1).astype(jnp.float32)
        activated, slope = gelu_parts(pre[:hidden])
        columns = pl.ds(pl.multiple_of(t * tile, tile), tile)
        cot[pl.ds(0, hidden), columns] = (value * pre[hidden:] * slope).astype(jnp.bfloat16)
        cot[pl.ds(hidden, hidden), columns] = (value * activated).astype(jnp.bfloat16)

    for copy in copies[ready:]:
        copy.wait()

    @pl.loop(0, x.shape[1] // tile)
    def _(n):
        columns = pl.ds(pl.multiple_of(n * tile, tile), tile)
        part = jnp.dot(cot[...], x[:, columns], preferred_element_type=jnp.float32)
        if first:
            grad[:, columns] = part
        else:
            grad[:, columns] += part

    outs = []
    for p in range(2):
        outs.append((grad.at[pl.ds(p * hidden + theirs_at, rows)], send[p]))
        outs.append((grad.at[pl.ds(p * hidden + mine_at, rows)], keep[p]))
    launch([pltpu.make_async_copy(a, b, sems.at[k]) for k, (a, b) in enumerate(outs)])


def terms(here, mine, theirs, cots, blocks, sources, totals, scale):
    rows, width = mine.shape[1], mine.shape[2]
    total = sum(b.shape[0] for b in blocks)
    first = totals is None
    anywhere = pl.BlockSpec(memory_space=pl.ANY)
    args = [mine, theirs, cots, *blocks, *([] if first else totals)]
    sums = jax.ShapeDtypeStruct((rows, width), jnp.float32)
    kernel = functools.partial(
        terms_kernel, tuple(b.shape[0] for b in blocks), tuple(sources), first, scale
    )
    return pl.pallas_call(
        kernel,
        in_specs=[pl.BlockSpec(memory_space=pltpu.SMEM)] + [anywhere] * len(args),
        out_specs=[anywhere] * 4,
        out_shape=[sums] * 4,
        scratch_shapes=[
            pltpu.VMEM((total, width), jnp.bfloat16),
            pltpu.VMEM((len(sources), 2 * rows, cots.shape[2]), jnp.bfloat16),
            pltpu.VMEM((4 * rows, width), jnp.bfloat16),
            pltpu.VMEM((4 * rows, width), jnp.float32),
            pltpu.VMEM((4 * rows, total), jnp.bfloat16),
            pltpu.SemaphoreType.DMA((8 + len(blocks) + len(sources),)),
        ],
        compiler_params=pltpu.CompilerParams(vmem_limit_bytes=48 * 2**20),
        cost_estimate=pl.CostEstimate(
            flops=16 * rows * width * total,
            bytes_accessed=20 * 2**20,
            transcendentals=2 * rows * total,
        ),
    )(here, *args)


def moved(here, winner, part):
    source = winner[here[0]]
    return (here[0] // 2 - source // 2 - part + 8) % 4


def adam_kernel(scale, here, winner, rate, w_ref, *refs):
    got, kept, came, outs = refs[0], refs[1:3], refs[3:5], refs[5:]
    learning = rate[0]
    column = winner[here[0]] // 2

    def moment(part):
        return got[(column + part) % 4].astype(jnp.float32)

    for p in range(2):
        grad = (kept[p][...] + came[p][...]) * scale
        first_new = 0.9 * moment(p) + 0.1 * grad
        second_new = 0.95 * moment(2 + p) + 0.05 * grad * grad
        update = learning * (first_new / bias_first) / (jnp.sqrt(second_new / bias_second) + 1e-08)
        outs[p][0] = (w_ref[p].astype(jnp.float32) - update).astype(jnp.bfloat16)
        outs[2 + p][0] = first_new.astype(jnp.bfloat16)
        outs[4 + p][0] = second_new.astype(jnp.bfloat16)


def adam(here, winner, rate, weights, got, mine, other, scale):
    hidden, width = weights.shape[1], weights.shape[2]
    rows = 32
    pair = pl.BlockSpec((2, rows, width), lambda i, *_: (0, i, 0))
    four = pl.BlockSpec((4, rows, width), lambda i, *_: (0, i, 0))
    flat = pl.BlockSpec((rows, width), lambda i, *_: (i, 0))
    one = pl.BlockSpec((1, rows, width), lambda i, *_: (0, i, 0))
    return pl.pallas_call(
        functools.partial(adam_kernel, scale),
        grid_spec=pltpu.PrefetchScalarGridSpec(
            num_scalar_prefetch=3,
            grid=(hidden // rows,),
            in_specs=[pair, four] + [flat] * 4,
            out_specs=[one] * 6,
        ),
        out_shape=[jax.ShapeDtypeStruct((1, hidden, width), jnp.bfloat16)] * 6,
        compiler_params=pltpu.CompilerParams(vmem_limit_bytes=48 * 2**20),
    )(here, winner, rate, weights, got, *mine, *other)


def losers(winner):
    low, high = 0, 0
    for m in range(7, -1, -1):
        low = jnp.where(winner[m] != m, m, low)
    for m in range(8):
        high = jnp.where(winner[m] != m, m, high)
    return low, high


def route(mode, here, winner):
    member = here[0]
    column, row = member // 2, member % 2
    low, high = losers(winner)
    if mode == "cross":
        return [(column - winner[m] // 2 + 4) % 4 for m in (low, high)]
    if mode == "place":
        return [moved(here, winner, part) for part in range(4)]
    wanted = []
    for j in range(4):
        target = j * 2 + row if mode == "columns" else ((column + j) % 4) * 2 + row
        source = winner[target]
        inside = (column - source // 2 + 4) % 4
        outside = jnp.where(target == low, 4, 5)
        wanted.append(jnp.where(source % 2 == row, inside, outside))
    return wanted


def pick_kernel(mode, here, winner, *refs):
    count = 2 if mode == "cross" else 4
    sems = refs[-1]
    if mode == "gather":
        outs, refs = list(refs[-5:-1]), list(refs[:-5])
    else:
        outs, refs = [refs[-2].at[k] for k in range(count)], list(refs[:-2])
    if mode in ("gather", "columns"):
        came = refs.pop()
        refs += [came.at[0], came.at[1]]
    index = route(mode, here, winner)
    for k in range(count):
        for i, ref in enumerate(refs):

            @pl.when(index[k] == i)
            def _():
                pltpu.make_async_copy(ref, outs[k], sems.at[k]).start()

    for k in range(count):
        pltpu.make_async_copy(refs[0], outs[k], sems.at[k]).wait()


def pick(mode, here, winner, arrays):
    shape, kind = arrays[0].shape, arrays[0].dtype
    smem = pl.BlockSpec(memory_space=pltpu.SMEM)
    anywhere = pl.BlockSpec(memory_space=pl.ANY)
    if mode == "gather":
        out_shape, out_specs = [jax.ShapeDtypeStruct(shape, kind)] * 4, [anywhere] * 4
    else:
        count = 2 if mode == "cross" else 4
        out_shape, out_specs = jax.ShapeDtypeStruct((count,) + shape, kind), anywhere
    return pl.pallas_call(
        functools.partial(pick_kernel, mode),
        in_specs=[smem, smem] + [anywhere] * len(arrays),
        out_specs=out_specs,
        out_shape=out_shape,
        scratch_shapes=[pltpu.SemaphoreType.DMA((4,))],
    )(here, winner, *arrays)


def spread(pieces):
    return [lax.ppermute(pieces[j], "member", along_row(j)) for j in (1, 2, 3)]


def body(
    tokens,
    cotangent,
    gate_weight,
    up_weight,
    gate_first,
    up_first,
    gate_second,
    up_second,
    winner,
    rate_index,
):
    sync = lax.optimization_barrier
    own = tokens[0]
    count, width = own.shape
    hidden = gate_weight.shape[1]
    scale = width ** (-0.5)
    here = jnp.stack([lax.axis_index("member"), lax.axis_index("fsdp")]).astype(jnp.int32)
    learning = 0.2 * jnp.exp2(
        (rate_index[lax.axis_index("member")].astype(jnp.float32) - 2.0) * 0.5
    )
    rate = jnp.full((1,), learning, jnp.float32)

    def fsdp(value, pairs):
        return lax.ppermute(value, "fsdp", pairs)

    def exchange(held):
        return lax.ppermute(pick("cross", here, winner, held), "member", row_swap)

    def gathered(held, came):
        sent = pick("gather", here, winner, [*held, came])
        return [sent[0], *spread(sent)]

    half = hidden // 2
    weights = [w[0, k * half : (k + 1) * half] for w in (gate_weight, up_weight) for k in range(2)]
    moments = [m[0] for m in (gate_first, up_first, gate_second, up_second)]
    turned = cotangent[0].T.reshape(16, 2 * hidden, count)
    with jax.named_scope("tick_a"):
        cots = lax.all_to_all(turned, "fsdp", 0, 0, axis_index_groups=same_core, tiled=True)
        start = jnp.concatenate([own, fsdp(own, low_swap)])
        held0 = [weights[0], *spread(weights)]
    start, held0, moments = sync((start, held0, moments))
    with jax.named_scope("tick_b"):
        up1, down1 = fsdp(start, z_up), fsdp(start, z_down)
        came0 = exchange(held0)
        held1 = [moments[0], *spread(moments)]
    up1, down1, came0, held0, cots = sync((up1, down1, came0, held0, cots))
    with jax.named_scope("tick_c"):
        up2, down2 = fsdp(up1, z_up), fsdp(down1, z_down)
        got0 = gathered(held0, came0)
    up2, down2, got0, held1 = sync((up2, down2, got0, held1))
    with jax.named_scope("tick_d"):
        up3, down3 = fsdp(up2, z_up), fsdp(down2, z_down)
        came1 = exchange(held1)
        mine = pick("place", here, winner, got0).reshape(2, hidden, width)
        theirs = fsdp(mine, core_swap)
        blocks = [start, up1, down1, up2, down2]
        sources = [(d, b) for d in (0, -1, 1, -2, 2) for b in range(2)]
        totals = terms(here, mine, theirs, cots, blocks, sources, None, scale)
    up3, down3, came1, totals, held1 = sync((up3, down3, came1, totals, held1))
    with jax.named_scope("tick_e"):
        sides = [fsdp(up3[:count], z_up), fsdp(down3[count:], z_down)]
        got1 = lax.all_to_all(
            pick("columns", here, winner, [*held1, came1]),
            "member",
            0,
            0,
            axis_index_groups=rows_of_members,
            tiled=True,
        )
        sources = [(d, b) for d in (-3, 3, 4) for b in range(2)]
        sums = terms(here, mine, theirs, cots, [up3, down3, *sides], sources, totals, scale)
        other = [fsdp(part, core_swap) for part in sums[2:]]
    with jax.named_scope("adam"):
        return tuple(adam(here, winner, rate, mine, got1, sums[:2], other, scale))


def solution(mesh):
    split = P("member", "fsdp", None)
    return jax.shard_map(
        body,
        mesh=mesh,
        in_specs=(split,) * 8 + (P(), P()),
        out_specs=(split,) * 6,
        check_vma=False,
    )
```

time: 314 us -> 460 us (1.46)
  Pallas kernels: 0 us -> 316 us
  waiting for transfers between devices: 168 us -> 75.3 us
  matrix products: 49.6 us -> 0 us
  local copies, waits for them, and re-layouts: 47.3 us -> 19 us
  starting transfers between devices: 22.6 us -> 47.1 us
  between operations: 14.9 us -> 1.78 us
  other arithmetic: 10.5 us -> 0.68 us
    pallas_call x0 -> x8, Pallas kernels: none -> 316 us  [the longest x5 277 us: pick(): pl.pallas_call(functools.partial(pick_kernel, mode), in_specs=[smem, smem...]
    all_to_all x3 -> x2, waiting for transfers between devices: 168 us -> 10.3 us  [the longest x1 10.3 us: body(): lax.all_to_all(pick('columns', here, winner, [*held1, came1]), 'member',...]
    ppermute x0 -> x23, waiting for transfers between devices: none -> 65 us  [the longest x2 25.3 us: exchange(): return lax.ppermute(pick('cross', here, winner, held), 'member', row_swap)]
    dot_general x3 -> x0, matrix products: 49.6 us -> none  [the longest x2 38 us: weight_grad(): lax.dot_general(cot_block, token_block, contract, preferred_element_type=...]
    ppermute x0 -> x23, starting transfers between devices: none -> 32.1 us  [the longest x12 15 us: fsdp(): return lax.ppermute(value, 'fsdp', pairs)]
    reshape x2 -> x0, local copies, waits for them, and re-layouts: 12.7 us -> none  [body(): pieces = bundle.reshape(6, members, portion, width)]
    mul x4 -> x0, local copies, waits for them, and re-layouts: 8.23 us -> none  [the longest x2 4.17 us: adam_update(): second_new = 0.95 * moment_two.astype(jnp.float32) + 0.05 * grad * grad]
    all_to_all x3 -> x2, starting transfers between devices: 22.6 us -> 15 us  [the longest x1 10.3 us: body(): lax.all_to_all(turned, 'fsdp', 0, 0, axis_index_groups=same_core, tiled=T...]
  transfers between devices with their start and end apart: 4 -> 25, of which waited for: 3 -> 13; matrix products, arithmetic and copies ran while one was open for 22% -> 1% of each run, Pallas kernels for 0% -> 56%
where the time goes in v2:
time: 460 us
  Pallas kernels  316 us (69%)
  waiting for transfers between devices  75.3 us (16%)
  starting transfers between devices  47.1 us (10%)
  local copies, waits for them, and re-layouts  19 us (4%)
    pallas_call x5, Pallas kernels, pick(): pl.pallas_call(functools.partial(pick_kernel, mode), in_specs=[smem, smem...  277 us
    pallas_call x2, Pallas kernels, terms(): pl.pallas_call(kernel, in_specs=[pl.BlockSpec(memory_space=pltpu.SMEM)] +...  30.3 us
    ppermute x2, waiting for transfers between devices, exchange(): return lax.ppermute(pick('cross', here, winner, held), 'member', row_swap)  25.3 us
    ppermute x9, waiting for transfers between devices, spread(): return [lax.ppermute(pieces[j], 'member', along_row(j)) for j in (1, 2, 3)]  23.7 us
    ppermute x12, waiting for transfers between devices, fsdp(): return lax.ppermute(value, 'fsdp', pairs)  15.9 us
    ppermute x12, starting transfers between devices, fsdp(): return lax.ppermute(value, 'fsdp', pairs)  15 us
    ppermute x9, starting transfers between devices, spread(): return [lax.ppermute(pieces[j], 'member', along_row(j)) for j in (1, 2, 3)]  13.7 us
    unnamed x56, local copies, waits for them, and re-layouts  12.7 us
  transfers between devices with their start and end apart: 25, of which 13 were waited for; matrix products, arithmetic and copies ran while one was open for 1% of the time, Pallas kernels for 56%

profile of v2, /device:TPU:1, one launch (start us, length us, event | category | flops | bytes accessed | tf_op | source)
XLA Modules:
  0.0 459.6 jit_solution(3940292031022901860)
XLA Ops:
  0.6 3.9 copy.16
  4.5 10.3 %all-to-all-start = ((bf16[16,448,128]{2,1,0:T(8,128)(2,1)}), bf16[16,448,128]{2,1,0:T(8,128)(2,1)}, u32[]{:S(2)}, u32[]{:S(2)}) async-start(bf16[16,448,128]{2,1,0:T(8,128)(2,1)} %bitcast.13), calls=%async_computation | async-start | bytes 3670016 | tf_op jit(solution)/shard_map/tick_a/all_to_all | solution.py:305
  14.9 1.4 collective-permute-start
  17.1 1.2 collective-permute-start.1
  19.2 1.5 collective-permute-start.3
  20.7 1.5 collective-permute-start.2
  22.8 5.7 %collective-permute-done = bf16[128,1792]{1,0:T(8,128)(2,1)S(1)} collective-permute-done((bf16[128,1792]{1,0:T(8,128)(2,1)S(1)}, bf16[128,1792]{1,0:T(8,128)(2,1)S(1)}, u32[]{:S(2)}, u32[]{:S(2)}) %collective-permute-start) | collective-permute-done | bytes 458784 | tf_op jit(solution)/shard_map/tick_a/ppermute | solution.py:291
  28.6 8.6 %collective-permute-done.2.refs_2_ = bf16[112,1792]{1,0:T(8,128)(2,1)S(1)} collective-permute-done((bf16[112,1792]{1,0:T(8,128)(2,1)}, bf16[112,1792]{1,0:T(8,128)(2,1)S(1)}, u32[]{:S(2)}, u32[]{:S(2)}) %collective-permute-start.2) | collective-permute-done | bytes 401440 | tf_op jit(solution)/shard_map/tick_a/ppermute | solution.py:264
  38.0 26.2 %tick_b.1 = bf16[2,112,1792]{2,1,0:T(8,128)(2,1)} custom-call(s32[2]{0:T(128)} %pad_add_fusion.here, s32[8]{0:T(128)} %winner.11, bf16[112,1792]{1,0:T(8,128)(2,1)} %get-tuple-element.63.refs_0_, bf16[112,1792]{1,0:T(8,128)(2,1)} %copy-done.17, bf16[112,1792]{1,0:T(8,128)(2,1)} %copy-done.19, bf16[112,1792]{1,0:T(8,128)(2,1)} %copy-done.18), custom_call_target="tpu_custom_call" | custom-call | tf_op jit(solution)/shard_map/tick_b/pallas_call | solution.py:254
  64.1 2.7 collective-permute-start.6
  66.9 2.3 collective-permute-start.5
  69.1 1.8 collective-permute-start.12
  71.0 1.7 collective-permute-start.13
  72.7 10.3 %collective-permute-done.6.refs_4_ = bf16[2,112,1792]{2,1,0:T(8,128)(2,1)S(1)} collective-permute-done((bf16[2,112,1792]{2,1,0:T(8,128)(2,1)}, bf16[2,112,1792]{2,1,0:T(8,128)(2,1)S(1)}, u32[]{:S(2)}, u32[]{:S(2)}) %collective-permute-start.6) | collective-permute-done | bytes 802848 | tf_op jit(solution)/shard_map/tick_b/ppermute | solution.py:294
  83.0 1.8 collective-permute-start.14
  84.8 1.3 collective-permute-done.5.refs_2_
  86.1 3.1 collective-permute-done.4.refs_1_
  89.2 2.7 collective-permute-start.8
  91.9 50.5 %tick_c.1 = (bf16[112,1792]{1,0:T(8,128)(2,1)}, bf16[112,1792]{1,0:T(8,128)(2,1)}, bf16[112,1792]{1,0:T(8,128)(2,1)}, bf16[112,1792]{1,0:T(8,128)(2,1)}) custom-call(s32[2]{0:T(128)} %pad_add_fusion.here, s32[8]{0:T(128)} %winner.11, bf16[112,1792]{1,0:T(8,128)(2,1)} %get-tuple-element.63.refs_0_, bf16[112,1792]{1,0:T(8,128)(2,1)} %copy-done.17, ...), custom_call_target="tpu_custom_call" | custom-call | tf_op jit(solution)/shard_map/tick_c/pallas_call | solution.py:254
  142.4 1.7 collective-permute-start.9
  144.1 1.3 collective-permute-start.10
  145.4 1.2 collective-permute-start.11
  146.6 4.0 collective-permute-done.9.refs_1_
  150.6 7.6 %collective-permute-done.10.refs_2_ = bf16[112,1792]{1,0:T(8,128)(2,1)S(1)} collective-permute-done((bf16[112,1792]{1,0:T(8,128)(2,1)}, bf16[112,1792]{1,0:T(8,128)(2,1)S(1)}, u32[]{:S(2)}, u32[]{:S(2)}) %collective-permute-start.10) | collective-permute-done | bytes 401440 | tf_op jit(solution)/shard_map/tick_c/ppermute | solution.py:264
  158.2 3.6 collective-permute-done.11.refs_3_
  162.5 50.5 %tick_d.3 = bf16[4,112,1792]{2,1,0:T(8,128)(2,1)} custom-call(s32[2]{0:T(128)} %pad_add_fusion.here, s32[8]{0:T(128)} %winner.11, bf16[112,1792]{1,0:T(8,128)(2,1)} %get-tuple-element.76.refs_0_, bf16[112,1792]{1,0:T(8,128)(2,1)} %copy-done.24, bf16[112,1792]{1,0:T(8,128)(2,1)} %copy-done.25, bf16[112,1792]{1,0:T(8,128)(2,1)} %copy-done.26), custom_call_target="tpu_custom_call" | custom-call | tf_op jit(solution)/shard_map/tick_d/pallas_call | solution.py:254
  213.0 3.1 collective-permute-start.18
  216.2 50.5 %tick_d.4 = bf16[2,224,1792]{2,1,0:T(8,128)(2,1)} custom-call(s32[2]{0:T(128)} %pad_add_fusion.here, s32[8]{0:T(128)} %winner.11, bf16[224,1792]{1,0:T(8,128)(2,1)} %bitcast.24, bf16[224,1792]{1,0:T(8,128)(2,1)} %copy-done.15, bf16[224,1792]{1,0:T(8,128)(2,1)} %collective-permute-done.13.refs_2_, bf16[224,1792]{1,0:T(8,128)(2,1)} %collective-permute-done.14.refs_3_), custom_call_target="tpu_custom_call" | custom-call | tf_op jit(solution)/shard_map/tick_d/pallas_call | solution.py:254
  267.3 2.7 collective-permute-start.16
  269.9 17.9 %tick_d.5 = (f32[224,1792]{1,0:T(8,128)S(1)}, f32[224,1792]{1,0:T(8,128)}, f32[224,1792]{1,0:T(8,128)}, f32[224,1792]{1,0:T(8,128)}) custom-call(s32[2]{0:T(128)S(1)} %copy-done.8, bf16[2,224,1792]{2,1,0:T(8,128)(2,1)} %bitcast.21, bf16[2,224,1792]{2,1,0:T(8,128)(2,1)} %collective-permute-done.18.theirs, bf16[16,448,128]{2,1,0:T(8,128)(2,1)} %all-to-all-done.cots, ...), custom_call_target="tpu_custom_call" | custom-call | flops 8220835840 | bytes 20971520 | tf_op jit(solution)/shard_map/tick_d/pallas_call | solution.py:131
  287.8 1.2 copy-done.14
  289.0 1.3 collective-permute-done.15.refs_0_
  290.3 15.0 %collective-permute-done.17.refs_4_ = bf16[2,224,1792]{2,1,0:T(8,128)(2,1)S(1)} collective-permute-done((bf16[2,224,1792]{2,1,0:T(8,128)(2,1)}, bf16[2,224,1792]{2,1,0:T(8,128)(2,1)S(1)}, u32[]{:S(2)}, u32[]{:S(2)}) %collective-permute-start.17) | collective-permute-done | bytes 1605664 | tf_op jit(solution)/shard_map/tick_d/ppermute | solution.py:294
  306.8 1.5 collective-permute-start.19
  308.3 99.1 %tick_e.2 = bf16[4,224,1792]{2,1,0:T(8,128)(2,1)} custom-call(s32[2]{0:T(128)} %pad_add_fusion.here, s32[8]{0:T(128)} %winner.11, bf16[224,1792]{1,0:T(8,128)(2,1)} %bitcast.25, bf16[224,1792]{1,0:T(8,128)(2,1)} %copy-done.15, bf16[224,1792]{1,0:T(8,128)(2,1)} %collective-permute-done.13.refs_2_, bf16[224,1792]{1,0:T(8,128)(2,1)} %collective-permute-done.14.refs_3_, ...), custom_call_target="tpu_custom_call" | custom-call | tf_op jit(solution)/shard_map/tick_e/pallas_call | solution.py:254
  407.4 4.7 %all-to-all-start.1 = ((bf16[4,224,1792]{2,1,0:T(8,128)(2,1)}), bf16[4,224,1792]{2,1,0:T(8,128)(2,1)}, u32[]{:S(2)}, u32[]{:S(2)}) async-start(bf16[4,224,1792]{2,1,0:T(8,128)(2,1)} %tick_e.2), calls=%async_computation.1 | async-start | bytes 6422528 | tf_op jit(solution)/shard_map/tick_e/all_to_all | solution.py:329
  413.7 1.2 copy-done.4
  414.8 1.2 copy-done.6
  416.0 1.0 copy-done.11
  417.0 1.0 copy-done.13
  418.1 12.4 %tick_e.3 = (f32[224,1792]{1,0:T(8,128)S(1)}, f32[224,1792]{1,0:T(8,128)S(1)}, f32[224,1792]{1,0:T(8,128)}, f32[224,1792]{1,0:T(8,128)}) custom-call(s32[2]{0:T(128)S(1)} %copy-done.9, bf16[2,224,1792]{2,1,0:T(8,128)(2,1)} %bitcast.22, bf16[2,224,1792]{2,1,0:T(8,128)(2,1)} %collective-permute-done.18.theirs, bf16[16,448,128]{2,1,0:T(8,128)(2,1)} %all-to-all-done.cots, ...), custom_call_target="tpu_custom_call" | custom-call | flops 4932501504 | bytes 20971520 | tf_op jit(solution)/shard_map/tick_e/pallas_call | solution.py:131
  430.5 1.2 copy-done.1
  431.7 1.4 collective-permute-start.21
  434.4 2.1 collective-permute-done.21.refs_3_
  436.5 2.3 collective-permute-done.22.refs_4_
  438.8 10.3 %all-to-all-done.1.refs_0_ = bf16[4,224,1792]{2,1,0:T(8,128)(2,1)} async-done(((bf16[4,224,1792]{2,1,0:T(8,128)(2,1)}), bf16[4,224,1792]{2,1,0:T(8,128)(2,1)}, u32[]{:S(2)}, u32[]{:S(2)}) %all-to-all-start.1) | async-done | bytes 3211296 | tf_op jit(solution)/shard_map/tick_e/all_to_all | solution.py:329
  449.1 1.4 copy-done.2
  450.5 8.9 %adam.1 = (bf16[1,224,1792]{2,1,0:T(8,128)(2,1)}, bf16[1,224,1792]{2,1,0:T(8,128)(2,1)}, bf16[1,224,1792]{2,1,0:T(8,128)(2,1)}, bf16[1,224,1792]{2,1,0:T(8,128)(...) custom-call(s32[2]{0:T(128)S(1)} %copy-done.9, s32[8]{0:T(128)S(1)} %copy-done.7, ...), custom_call_target="tpu_custom_call" | custom-call | tf_op jit(solution)/shard_map/adam/pallas_call | solution.py:183
  (74 shorter events, 8.2 us)
Async XLA Ops:
  4.5 10.3 %copy-start.23 = (bf16[1,128,1792]{2,1,0:T(8,128)(2,1)S(1)}, bf16[1,128,1792]{2,1,0:T(8,128)(2,1)}, u32[]{:S(2)}) copy-start(bf16[1,128,1792]{2,1,0:T(8,128)(2,1)} %param.10) | copy-start | bytes 1376260
  4.5 11.7 %copy-start.20 = (bf16[1,224,1792]{2,1,0:T(8,128)(2,1)S(1)}, bf16[1,224,1792]{2,1,0:T(8,128)(2,1)}, u32[]{:S(2)}) copy-start(bf16[1,224,1792]{2,1,0:T(8,128)(2,1)} %param.12) | copy-start | bytes 2408452
  4.5 84.7 %all-to-all-start = ((bf16[16,448,128]{2,1,0:T(8,128)(2,1)}), bf16[16,448,128]{2,1,0:T(8,128)(2,1)}, u32[]{:S(2)}, u32[]{:S(2)}) async-start(bf16[16,448,128]{2,1,0:T(8,128)(2,1)} %bitcast.13), calls=%async_computation | async-start | bytes 3670016 | tf_op jit(solution)/shard_map/tick_a/all_to_all | solution.py:305
  14.8 3.4 copy-start.21
  14.9 13.7 %collective-permute-start = (bf16[128,1792]{1,0:T(8,128)(2,1)S(1)}, bf16[128,1792]{1,0:T(8,128)(2,1)S(1)}, u32[]{:S(2)}, u32[]{:S(2)}) collective-permute-start(bf16[128,1792]{1,0:T(8,128)(2,1)S(1)} %bitcast.27), channel_id=1, source_target_pairs={{0,2},{1,3},{2,0},{3,1},{4,6},{5,7},{6,4},{7,5},{8,10},{9,11},{10,... | collective-permute-start | bytes 1376264 | tf_op jit(solution)/shard_map/tick_a/ppermute | solution.py:291
  17.1 11.5 %collective-permute-start.1 = (bf16[112,1792]{1,0:T(8,128)(2,1)S(1)}, bf16[112,1792]{1,0:T(8,128)(2,1)S(1)}, u32[]{:S(2)}, u32[]{:S(2)}) collective-permute-start(bf16[112,1792]{1,0:T(8,128)(2,1)S(1)} %get-tuple-element.108), channel_id=1, source_target_pairs={{0,64},{32,96},{64,128},{96,160},{128,192},{160,224},{192,0},{224,... | collective-permute-start | bytes 1204232 | tf_op jit(solution)/shard_map/tick_a/ppermute | solution.py:264
  19.2 9.4 %collective-permute-start.3 = (bf16[112,1792]{1,0:T(8,128)(2,1)}, bf16[112,1792]{1,0:T(8,128)(2,1)S(1)}, u32[]{:S(2)}, u32[]{:S(2)}) collective-permute-start(bf16[112,1792]{1,0:T(8,128)(2,1)} %get-tuple-element.106), channel_id=1, source_target_pairs={{0,192},{32,224},{64,0},{96,32},{128,64},{160,96},{192,128},{224,1... | collective-permute-start | bytes 1204232 | tf_op jit(solution)/shard_map/tick_a/ppermute | solution.py:264
  20.7 16.6 %collective-permute-start.2 = (bf16[112,1792]{1,0:T(8,128)(2,1)}, bf16[112,1792]{1,0:T(8,128)(2,1)S(1)}, u32[]{:S(2)}, u32[]{:S(2)}) collective-permute-start(bf16[112,1792]{1,0:T(8,128)(2,1)} %get-tuple-element.107), channel_id=1, source_target_pairs={{0,128},{32,160},{64,192},{96,224},{128,0},{160,32},{192,64},{224,... | collective-permute-start | bytes 1204232 | tf_op jit(solution)/shard_map/tick_a/ppermute | solution.py:264
  28.6 8.6 %copy-start.17 = (bf16[112,1792]{1,0:T(8,128)(2,1)}, bf16[112,1792]{1,0:T(8,128)(2,1)S(1)}, u32[]{:S(2)}) copy-start(bf16[112,1792]{1,0:T(8,128)(2,1)S(1)} %collective-permute-done.1.refs_1_) | copy-start | bytes 1204228
  28.6 8.6 %copy-start.18 = (bf16[112,1792]{1,0:T(8,128)(2,1)}, bf16[112,1792]{1,0:T(8,128)(2,1)S(1)}, u32[]{:S(2)}) copy-start(bf16[112,1792]{1,0:T(8,128)(2,1)S(1)} %collective-permute-done.3.refs_3_) | copy-start | bytes 1204228
  64.1 18.9 %collective-permute-start.6 = (bf16[2,112,1792]{2,1,0:T(8,128)(2,1)}, bf16[2,112,1792]{2,1,0:T(8,128)(2,1)S(1)}, u32[]{:S(2)}, u32[]{:S(2)}) collective-permute-start(bf16[2,112,1792]{2,1,0:T(8,128)(2,1)} %tick_b.1), channel_id=1, source_target_pairs={{0,32},{32,0},{64,96},{96,64},{128,160},{160,128},{192,224},{224,1... | collective-permute-start | bytes 2408456 | tf_op jit(solution)/shard_map/tick_b/ppermute | solution.py:294
  66.9 19.2 %collective-permute-start.5 = (bf16[256,1792]{1,0:T(8,128)(2,1)S(1)}, bf16[256,1792]{1,0:T(8,128)(2,1)S(1)}, u32[]{:S(2)}, u32[]{:S(2)}) collective-permute-start(bf16[256,1792]{1,0:T(8,128)(2,1)S(1)} %pad_maximum_fusion.refs_0_), channel_id=1, source_target_pairs={{4,0},{5,1},{6,2},{7,3},{8,4},{9,5},{10,6},{11,7},{12,8},{13,9},{1... | collective-permute-start | bytes 2752520 | tf_op jit(solution)/shard_map/tick_b/ppermute | solution.py:291
  69.1 20.1 %collective-permute-start.4 = (bf16[256,1792]{1,0:T(8,128)(2,1)S(1)}, bf16[256,1792]{1,0:T(8,128)(2,1)S(1)}, u32[]{:S(2)}, u32[]{:S(2)}) collective-permute-start(bf16[256,1792]{1,0:T(8,128)(2,1)S(1)} %pad_maximum_fusion.refs_0_), channel_id=1, source_target_pairs={{0,4},{1,5},{2,6},{3,7},{4,8},{5,9},{6,10},{7,11},{8,12},{9,13},{1... | collective-permute-start | bytes 2752520 | tf_op jit(solution)/shard_map/tick_b/ppermute | solution.py:291
  69.1 73.2 %collective-permute-start.12 = (bf16[224,1792]{1,0:T(8,128)(2,1)}, bf16[224,1792]{1,0:T(8,128)(2,1)S(1)}, u32[]{:S(2)}, u32[]{:S(2)}) collective-permute-start(bf16[224,1792]{1,0:T(8,128)(2,1)} %bitcast.29), channel_id=1, source_target_pairs={{0,64},{32,96},{64,128},{96,160},{128,192},{160,224},{192,0},{224,... | collective-permute-start | bytes 2408456 | tf_op jit(solution)/shard_map/tick_b/ppermute | solution.py:264
  71.0 73.2 %collective-permute-start.13 = (bf16[224,1792]{1,0:T(8,128)(2,1)}, bf16[224,1792]{1,0:T(8,128)(2,1)}, u32[]{:S(2)}, u32[]{:S(2)}) collective-permute-start(bf16[224,1792]{1,0:T(8,128)(2,1)} %bitcast.30), channel_id=1, source_target_pairs={{0,128},{32,160},{64,192},{96,224},{128,0},{160,32},{192,64},{224,... | collective-permute-start | bytes 2408456 | tf_op jit(solution)/shard_map/tick_b/ppermute | solution.py:264
  83.0 3.1 copy-start.22
  83.0 62.5 %collective-permute-start.14 = (bf16[224,1792]{1,0:T(8,128)(2,1)}, bf16[224,1792]{1,0:T(8,128)(2,1)}, u32[]{:S(2)}, u32[]{:S(2)}) collective-permute-start(bf16[224,1792]{1,0:T(8,128)(2,1)} %bitcast.31), channel_id=1, source_target_pairs={{0,192},{32,224},{64,0},{96,32},{128,64},{160,96},{192,128},{224,1... | collective-permute-start | bytes 2408456 | tf_op jit(solution)/shard_map/tick_b/ppermute | solution.py:264
  89.2 72.6 %collective-permute-start.7 = (bf16[256,1792]{1,0:T(8,128)(2,1)S(1)}, bf16[256,1792]{1,0:T(8,128)(2,1)}, u32[]{:S(2)}, u32[]{:S(2)}) collective-permute-start(bf16[256,1792]{1,0:T(8,128)(2,1)S(1)} %collective-permute-done.4.refs_1_), channel_id=1, source_target_pairs={{0,4},{1,5},{2,6},{3,7},{4,8},{5,9},{6,10},{7,11},{8,12},{9,13},{1... | collective-permute-start | bytes 2752520 | tf_op jit(solution)/shard_map/tick_c/ppermute | solution.py:291
  89.2 72.6 %collective-permute-start.8 = (bf16[256,1792]{1,0:T(8,128)(2,1)S(1)}, bf16[256,1792]{1,0:T(8,128)(2,1)}, u32[]{:S(2)}, u32[]{:S(2)}) collective-permute-start(bf16[256,1792]{1,0:T(8,128)(2,1)S(1)} %collective-permute-done.5.refs_2_), channel_id=1, source_target_pairs={{4,0},{5,1},{6,2},{7,3},{8,4},{9,5},{10,6},{11,7},{12,8},{13,9},{1... | collective-permute-start | bytes 2752520 | tf_op jit(solution)/shard_map/tick_c/ppermute | solution.py:291
  142.4 70.6 %copy-start.15 = (bf16[224,1792]{1,0:T(8,128)(2,1)}, bf16[224,1792]{1,0:T(8,128)(2,1)S(1)}, u32[]{:S(2)}) copy-start(bf16[224,1792]{1,0:T(8,128)(2,1)S(1)} %collective-permute-done.12.refs_1_) | copy-start | bytes 2408452
  142.4 8.2 %collective-permute-start.9 = (bf16[112,1792]{1,0:T(8,128)(2,1)}, bf16[112,1792]{1,0:T(8,128)(2,1)S(1)}, u32[]{:S(2)}, u32[]{:S(2)}) collective-permute-start(bf16[112,1792]{1,0:T(8,128)(2,1)} %get-tuple-element.69), channel_id=1, source_target_pairs={{0,64},{32,96},{64,128},{96,160},{128,192},{160,224},{192,0},{224,... | collective-permute-start | bytes 1204232 | tf_op jit(solution)/shard_map/tick_c/ppermute | solution.py:264
  144.1 14.0 %collective-permute-start.10 = (bf16[112,1792]{1,0:T(8,128)(2,1)}, bf16[112,1792]{1,0:T(8,128)(2,1)S(1)}, u32[]{:S(2)}, u32[]{:S(2)}) collective-permute-start(bf16[112,1792]{1,0:T(8,128)(2,1)} %get-tuple-element.70), channel_id=1, source_target_pairs={{0,128},{32,160},{64,192},{96,224},{128,0},{160,32},{192,64},{224,... | collective-permute-start | bytes 1204232 | tf_op jit(solution)/shard_map/tick_c/ppermute | solution.py:264
  145.4 16.3 %collective-permute-start.11 = (bf16[112,1792]{1,0:T(8,128)(2,1)}, bf16[112,1792]{1,0:T(8,128)(2,1)S(1)}, u32[]{:S(2)}, u32[]{:S(2)}) collective-permute-start(bf16[112,1792]{1,0:T(8,128)(2,1)} %get-tuple-element.71), channel_id=1, source_target_pairs={{0,192},{32,224},{64,0},{96,32},{128,64},{160,96},{192,128},{224,1... | collective-permute-start | bytes 1204232 | tf_op jit(solution)/shard_map/tick_c/ppermute | solution.py:264
  150.6 11.2 %copy-start.24 = (bf16[112,1792]{1,0:T(8,128)(2,1)}, bf16[112,1792]{1,0:T(8,128)(2,1)S(1)}, u32[]{:S(2)}) copy-start(bf16[112,1792]{1,0:T(8,128)(2,1)S(1)} %collective-permute-done.9.refs_1_) | copy-start | bytes 1204228
  158.2 3.6 copy-start.25
  213.0 56.9 %copy-start.8 = (s32[2]{0:T(128)S(1)}, s32[2]{0:T(128)}, u32[]{:S(2)}) copy-start(s32[2]{0:T(128)} %pad_add_fusion.here) | copy-start | bytes 28
  213.0 56.9 %collective-permute-start.18 = (bf16[2,224,1792]{2,1,0:T(8,128)(2,1)}, bf16[2,224,1792]{2,1,0:T(8,128)(2,1)}, u32[]{:S(2)}, u32[]{:S(2)}) collective-permute-start(bf16[2,224,1792]{2,1,0:T(8,128)(2,1)} %bitcast.20), channel_id=1, source_target_pairs={{0,1},{1,0},{2,3},{3,2},{4,5},{5,4},{6,7},{7,6},{8,9},{9,8},{10,11... | collective-permute-start | bytes 4816904 | tf_op jit(solution)/shard_map/tick_d/ppermute | solution.py:291
  266.6 38.7 %collective-permute-start.17 = (bf16[2,224,1792]{2,1,0:T(8,128)(2,1)}, bf16[2,224,1792]{2,1,0:T(8,128)(2,1)S(1)}, u32[]{:S(2)}, u32[]{:S(2)}) collective-permute-start(bf16[2,224,1792]{2,1,0:T(8,128)(2,1)} %tick_d.4), channel_id=1, source_target_pairs={{0,32},{32,0},{64,96},{96,64},{128,160},{160,128},{192,224},{224,1... | collective-permute-start | bytes 4816904 | tf_op jit(solution)/shard_map/tick_d/ppermute | solution.py:294
  267.3 23.1 %collective-permute-start.15 = (bf16[256,1792]{1,0:T(8,128)(2,1)}, bf16[256,1792]{1,0:T(8,128)(2,1)S(1)}, u32[]{:S(2)}, u32[]{:S(2)}) collective-permute-start(bf16[256,1792]{1,0:T(8,128)(2,1)} %collective-permute-done.7.refs_3_), channel_id=1, source_target_pairs={{0,4},{1,5},{2,6},{3,7},{4,8},{5,9},{6,10},{7,11},{8,12},{9,13},{1... | collective-permute-start | bytes 2752520 | tf_op jit(solution)/shard_map/tick_d/ppermute | solution.py:291
  267.3 23.1 %collective-permute-start.16 = (bf16[256,1792]{1,0:T(8,128)(2,1)}, bf16[256,1792]{1,0:T(8,128)(2,1)S(1)}, u32[]{:S(2)}, u32[]{:S(2)}) collective-permute-start(bf16[256,1792]{1,0:T(8,128)(2,1)} %collective-permute-done.8.refs_4_), channel_id=1, source_target_pairs={{4,0},{5,1},{6,2},{7,3},{8,4},{9,5},{10,6},{11,7},{12,8},{13,9},{1... | collective-permute-start | bytes 2752520 | tf_op jit(solution)/shard_map/tick_d/ppermute | solution.py:291
  287.8 1.2 copy-start.14
  290.3 15.0 %copy-start.5 = (bf16[256,1792]{1,0:T(8,128)(2,1)}, bf16[256,1792]{1,0:T(8,128)(2,1)S(1)}, u32[]{:S(2)}) copy-start(bf16[256,1792]{1,0:T(8,128)(2,1)S(1)} %collective-permute-done.16.refs_1_) | copy-start | bytes 2752516
  305.3 1.5 copy-start.16
  306.8 105.3 %collective-permute-start.20 = (bf16[128,1792]{1,0:T(8,128)(2,1)S(1)}, bf16[128,1792]{1,0:T(8,128)(2,1)S(1)}, u32[]{:S(2)}, u32[]{:S(2)}) collective-permute-start(bf16[128,1792]{1,0:T(8,128)(2,1)S(1)} %slice.23), channel_id=1, source_target_pairs={{4,0},{5,1},{6,2},{7,3},{8,4},{9,5},{10,6},{11,7},{12,8},{13,9},{1... | collective-permute-start | bytes 1376264 | tf_op jit(solution)/shard_map/tick_e/ppermute | solution.py:291
  306.8 106.1 %collective-permute-start.19 = (bf16[128,1792]{1,0:T(8,128)(2,1)S(1)}, bf16[128,1792]{1,0:T(8,128)(2,1)S(1)}, u32[]{:S(2)}, u32[]{:S(2)}) collective-permute-start(bf16[128,1792]{1,0:T(8,128)(2,1)S(1)} %slice.22), channel_id=1, source_target_pairs={{0,4},{1,5},{2,6},{3,7},{4,8},{5,9},{6,10},{7,11},{8,12},{9,13},{1... | collective-permute-start | bytes 1376264 | tf_op jit(solution)/shard_map/tick_e/ppermute | solution.py:291
  407.4 6.3 %copy-start.9 = (s32[2]{0:T(128)S(1)}, s32[2]{0:T(128)}, u32[]{:S(2)}) copy-start(s32[2]{0:T(128)} %pad_add_fusion.here) | copy-start | bytes 28
  407.4 25.7 %copy-start.27 = (s32[8]{0:T(128)S(1)}, s32[8]{0:T(128)}, u32[]{:S(2)}) copy-start(s32[8]{0:T(128)} %param.19) | copy-start | bytes 100
  407.4 41.7 %copy-start.7 = (s32[8]{0:T(128)S(1)}, s32[8]{0:T(128)}, u32[]{:S(2)}) copy-start(s32[8]{0:T(128)} %winner.11) | copy-start | bytes 100
  407.4 41.7 %all-to-all-start.1 = ((bf16[4,224,1792]{2,1,0:T(8,128)(2,1)}), bf16[4,224,1792]{2,1,0:T(8,128)(2,1)}, u32[]{:S(2)}, u32[]{:S(2)}) async-start(bf16[4,224,1792]{2,1,0:T(8,128)(2,1)} %tick_e.2), calls=%async_computation.1 | async-start | bytes 6422528 | tf_op jit(solution)/shard_map/tick_e/all_to_all | solution.py:329
  412.1 37.0 %copy-start = (bf16[4,112,1792]{2,1,0:T(8,128)(2,1)S(1)}, bf16[4,112,1792]{2,1,0:T(8,128)(2,1)}, u32[]{:S(2)}) copy-start(bf16[4,112,1792]{2,1,0:T(8,128)(2,1)} %tick_d.3) | copy-start | bytes 4816900
  413.7 1.2 copy-start.4
  414.8 1.2 copy-start.6
  416.0 1.0 copy-start.11
  417.0 1.0 copy-start.13
  430.5 1.2 copy-start.1
  431.7 4.8 %collective-permute-start.21 = (f32[224,1792]{1,0:T(8,128)}, f32[224,1792]{1,0:T(8,128)}, u32[]{:S(2)}, u32[]{:S(2)}) collective-permute-start(f32[224,1792]{1,0:T(8,128)} %get-tuple-element.104), channel_id=1, source_target_pairs={{0,1},{1,0},{2,3},{3,2},{4,5},{5,4},{6,7},{7,6},{8,9},{9,8},{10,11... | collective-permute-start | bytes 4816904 | tf_op jit(solution)/shard_map/tick_e/ppermute | solution.py:291
  433.1 5.7 %collective-permute-start.22 = (f32[224,1792]{1,0:T(8,128)}, f32[224,1792]{1,0:T(8,128)}, u32[]{:S(2)}, u32[]{:S(2)}) collective-permute-start(f32[224,1792]{1,0:T(8,128)} %get-tuple-element.105), channel_id=1, source_target_pairs={{0,1},{1,0},{2,3},{3,2},{4,5},{5,4},{6,7},{7,6},{8,9},{9,8},{10,11... | collective-permute-start | bytes 4816904 | tf_op jit(solution)/shard_map/tick_e/ppermute | solution.py:291
  449.1 1.4 copy-start.2
  (5 other events, 4.0 us)

commit v3 on v2

--- a/solution.py
+++ b/solution.py
@@ -54,10 +54,11 @@
     count = len(lengths)
     tokens, refs = refs[:count], refs[count:]
     if not first:
-        kept, sent, refs = refs[:2], refs[2:4], refs[4:]
-    keep, send = refs[:2], refs[2:4]
-    x, c, w, grad, cot, sems = refs[4:]
+        kept, sent, refs = refs[:2], refs[2:6], refs[6:]
+    keep, send = refs[:2], refs[2:6]
+    x, c, w, grad, cot, sems = refs[6:]
     rows, hidden = mine.shape[1], 2 * mine.shape[1]
+    half = rows // 2
     me = here[1]
     z, low, core = me // 4, (me // 2) % 2, me % 2
     mine_at = pl.multiple_of(core * rows, 32)
@@ -77,7 +78,9 @@
     if not first:
         for p in range(2):
             pairs.append((kept[p], grad.at[pl.ds(p * hidden + mine_at, rows)]))
-            pairs.append((sent[p], grad.at[pl.ds(p * hidden + theirs_at, rows)]))
+            for h in range(2):
+                to = p * hidden + theirs_at + h * half
+                pairs.append((sent[2 * p + h], grad.at[pl.ds(to, half)]))
     copies = [pltpu.make_async_copy(a, b, sems.at[k]) for k, (a, b) in enumerate(pairs)]
     for copy in copies:
         copy.start()
@@ -113,7 +116,9 @@
 
     outs = []
     for p in range(2):
-        outs.append((grad.at[pl.ds(p * hidden + theirs_at, rows)], send[p]))
+        for h in range(2):
+            to = p * hidden + theirs_at + h * half
+            outs.append((grad.at[pl.ds(to, half)], send[2 * p + h]))
         outs.append((grad.at[pl.ds(p * hidden + mine_at, rows)], keep[p]))
     launch([pltpu.make_async_copy(a, b, sems.at[k]) for k, (a, b) in enumerate(outs)])
 
@@ -125,21 +130,22 @@
     anywhere = pl.BlockSpec(memory_space=pl.ANY)
     args = [mine, theirs, cots, *blocks, *([] if first else totals)]
     sums = jax.ShapeDtypeStruct((rows, width), jnp.float32)
+    parts = jax.ShapeDtypeStruct((rows // 2, width), jnp.float32)
     kernel = functools.partial(
         terms_kernel, tuple(b.shape[0] for b in blocks), tuple(sources), first, scale
     )
     return pl.pallas_call(
         kernel,
         in_specs=[pl.BlockSpec(memory_space=pltpu.SMEM)] + [anywhere] * len(args),
-        out_specs=[anywhere] * 4,
-        out_shape=[sums] * 4,
+        out_specs=[anywhere] * 6,
+        out_shape=[sums] * 2 + [parts] * 4,
         scratch_shapes=[
             pltpu.VMEM((total, width), jnp.bfloat16),
             pltpu.VMEM((len(sources), 2 * rows, cots.shape[2]), jnp.bfloat16),
             pltpu.VMEM((4 * rows, width), jnp.bfloat16),
             pltpu.VMEM((4 * rows, width), jnp.float32),
             pltpu.VMEM((4 * rows, total), jnp.bfloat16),
-            pltpu.SemaphoreType.DMA((8 + len(blocks) + len(sources),)),
+            pltpu.SemaphoreType.DMA((10 + len(blocks) + len(sources),)),
         ],
         compiler_params=pltpu.CompilerParams(vmem_limit_bytes=48 * 2**20),
         cost_estimate=pl.CostEstimate(
@@ -156,7 +162,7 @@
 
 
 def adam_kernel(scale, here, winner, rate, w_ref, *refs):
-    got, kept, came, outs = refs[0], refs[1:3], refs[3:5], refs[5:]
+    got, kept, came, outs = refs[0], refs[1:3], refs[3:5], refs[-6:]
     learning = rate[0]
     column = winner[here[0]] // 2
 
@@ -173,24 +179,32 @@
         outs[4 + p][0] = second_new.astype(jnp.bfloat16)
 
 
-def adam(here, winner, rate, weights, got, mine, other, scale):
+def adam(here, winner, rate, weights, got, mine, other, scale, part, earlier):
     hidden, width = weights.shape[1], weights.shape[2]
-    rows = 32
-    pair = pl.BlockSpec((2, rows, width), lambda i, *_: (0, i, 0))
+    rows = 16
+    steps = got.shape[1] // rows
+    off = part * steps
+    pair = pl.BlockSpec((2, rows, width), lambda i, *_: (0, i + off, 0))
     four = pl.BlockSpec((4, rows, width), lambda i, *_: (0, i, 0))
-    flat = pl.BlockSpec((rows, width), lambda i, *_: (i, 0))
-    one = pl.BlockSpec((1, rows, width), lambda i, *_: (0, i, 0))
+    flat = pl.BlockSpec((rows, width), lambda i, *_: (i + off, 0))
+    piece = pl.BlockSpec((rows, width), lambda i, *_: (i, 0))
+    one = pl.BlockSpec((1, rows, width), lambda i, *_: (0, i + off, 0))
+    whole = pl.BlockSpec(memory_space=pl.ANY)
     return pl.pallas_call(
         functools.partial(adam_kernel, scale),
         grid_spec=pltpu.PrefetchScalarGridSpec(
             num_scalar_prefetch=3,
-            grid=(hidden // rows,),
-            in_specs=[pair, four] + [flat] * 4,
+            grid=(steps,),
+            in_specs=[pair, four] + [flat] * 2 + [piece] * 2 + [whole] * len(earlier),
             out_specs=[one] * 6,
         ),
         out_shape=[jax.ShapeDtypeStruct((1, hidden, width), jnp.bfloat16)] * 6,
-        compiler_params=pltpu.CompilerParams(vmem_limit_bytes=48 * 2**20),
-    )(here, winner, rate, weights, got, *mine, *other)
+        input_output_aliases={9 + k: k for k in range(len(earlier))},
+        compiler_params=pltpu.CompilerParams(vmem_limit_bytes=32 * 2**20),
+        cost_estimate=pl.CostEstimate(
+            flops=40 * hidden * width, bytes_accessed=8 * 2**20, transcendentals=hidden * width
+        ),
+    )(here, winner, rate, weights, got, *mine, *other, *earlier)
 
 
 def losers(winner):
@@ -220,43 +234,58 @@
     return wanted
 
 
-def pick_kernel(mode, here, winner, *refs):
+def pick_kernel(mode, span, here, winner, *refs):
     count = 2 if mode == "cross" else 4
-    sems = refs[-1]
+    stage, sems = refs[-2:]
     if mode == "gather":
-        outs, refs = list(refs[-5:-1]), list(refs[:-5])
+        outs, refs = list(refs[-6:-2]), list(refs[:-6])
     else:
-        outs, refs = [refs[-2].at[k] for k in range(count)], list(refs[:-2])
+        outs, refs = [refs[-3].at[k] for k in range(count)], list(refs[:-3])
+    came = []
     if mode in ("gather", "columns"):
-        came = refs.pop()
-        refs += [came.at[0], came.at[1]]
+        last = refs.pop()
+        came = [last.at[0], last.at[1]]
+    choices = [ref.at[pl.ds(span[0], span[1])] for ref in refs] + came
     index = route(mode, here, winner)
     for k in range(count):
-        for i, ref in enumerate(refs):
+        for i, ref in enumerate(choices):
 
             @pl.when(index[k] == i)
             def _():
-                pltpu.make_async_copy(ref, outs[k], sems.at[k]).start()
+                pltpu.make_async_copy(ref, stage.at[k], sems.at[k]).start()
 
     for k in range(count):
-        pltpu.make_async_copy(refs[0], outs[k], sems.at[k]).wait()
-
-
-def pick(mode, here, winner, arrays):
-    shape, kind = arrays[0].shape, arrays[0].dtype
+        pltpu.make_async_copy(choices[0], stage.at[k], sems.at[k]).wait()
+        pltpu.make_async_copy(stage.at[k], outs[k], sems.at[4 + k]).start()
+    for k in range(count):
+        pltpu.make_async_copy(stage.at[k], outs[k], sems.at[4 + k]).wait()
+
+
+def pick(mode, here, winner, arrays, span=None):
+    rows, width = arrays[0].shape
+    span = span or (0, rows)
+    kind = arrays[0].dtype
+    count = 2 if mode == "cross" else 4
+    shape = (span[1], width)
     smem = pl.BlockSpec(memory_space=pltpu.SMEM)
     anywhere = pl.BlockSpec(memory_space=pl.ANY)
     if mode == "gather":
         out_shape, out_specs = [jax.ShapeDtypeStruct(shape, kind)] * 4, [anywhere] * 4
     else:
-        count = 2 if mode == "cross" else 4
         out_shape, out_specs = jax.ShapeDtypeStruct((count,) + shape, kind), anywhere
     return pl.pallas_call(
-        functools.partial(pick_kernel, mode),
+        functools.partial(pick_kernel, mode, span),
         in_specs=[smem, smem] + [anywhere] * len(arrays),
         out_specs=out_specs,
         out_shape=out_shape,
-        scratch_shapes=[pltpu.SemaphoreType.DMA((4,))],
+        scratch_shapes=[
+            pltpu.VMEM((count,) + shape, kind),
+            pltpu.SemaphoreType.DMA((8,)),
+        ],
+        compiler_params=pltpu.CompilerParams(vmem_limit_bytes=16 * 2**20),
+        cost_estimate=pl.CostEstimate(
+            flops=0, bytes_accessed=4 * count * span[1] * width, transcendentals=0
+        ),
     )(here, winner, *arrays)
 
 
@@ -290,55 +319,67 @@
     def fsdp(value, pairs):
         return lax.ppermute(value, "fsdp", pairs)
 
-    def exchange(held):
-        return lax.ppermute(pick("cross", here, winner, held), "member", row_swap)
+    def exchange(held, span=None):
+        return lax.ppermute(pick("cross", here, winner, held, span), "member", row_swap)
 
     def gathered(held, came):
         sent = pick("gather", here, winner, [*held, came])
         return [sent[0], *spread(sent)]
 
-    half = hidden // 2
-    weights = [w[0, k * half : (k + 1) * half] for w in (gate_weight, up_weight) for k in range(2)]
-    moments = [m[0] for m in (gate_first, up_first, gate_second, up_second)]
-    turned = cotangent[0].T.reshape(16, 2 * hidden, count)
-    with jax.named_scope("tick_a"):
-        cots = lax.all_to_all(turned, "fsdp", 0, 0, axis_index_groups=same_core, tiled=True)
-        start = jnp.concatenate([own, fsdp(own, low_swap)])
-        held0 = [weights[0], *spread(weights)]
-    start, held0, moments = sync((start, held0, moments))
-    with jax.named_scope("tick_b"):
-        up1, down1 = fsdp(start, z_up), fsdp(start, z_down)
-        came0 = exchange(held0)
-        held1 = [moments[0], *spread(moments)]
-    up1, down1, came0, held0, cots = sync((up1, down1, came0, held0, cots))
-    with jax.named_scope("tick_c"):
-        up2, down2 = fsdp(up1, z_up), fsdp(down1, z_down)
-        got0 = gathered(held0, came0)
-    up2, down2, got0, held1 = sync((up2, down2, got0, held1))
-    with jax.named_scope("tick_d"):
-        up3, down3 = fsdp(up2, z_up), fsdp(down2, z_down)
-        came1 = exchange(held1)
-        mine = pick("place", here, winner, got0).reshape(2, hidden, width)
-        theirs = fsdp(mine, core_swap)
-        blocks = [start, up1, down1, up2, down2]
-        sources = [(d, b) for d in (0, -1, 1, -2, 2) for b in range(2)]
-        totals = terms(here, mine, theirs, cots, blocks, sources, None, scale)
-    up3, down3, came1, totals, held1 = sync((up3, down3, came1, totals, held1))
-    with jax.named_scope("tick_e"):
-        sides = [fsdp(up3[:count], z_up), fsdp(down3[count:], z_down)]
-        got1 = lax.all_to_all(
-            pick("columns", here, winner, [*held1, came1]),
+    def columns(held, came, span):
+        return lax.all_to_all(
+            pick("columns", here, winner, [*held, came], span),
             "member",
             0,
             0,
             axis_index_groups=rows_of_members,
             tiled=True,
         )
+
+    half = hidden // 2
+    spans = [(0, half), (half, half)]
+    weights = [w[0, k * half : (k + 1) * half] for w in (gate_weight, up_weight) for k in range(2)]
+    moments = [m[0] for m in (gate_first, up_first, gate_second, up_second)]
+    with jax.named_scope("tick_a"):
+        held0 = [weights[0], *spread(weights)]
+        partner = fsdp(own, low_swap)
+    partner, held0, own, turned, moments = sync((partner, held0, own, cotangent[0], moments))
+    with jax.named_scope("tick_b"):
+        came0 = exchange(held0)
+        near = [lax.ppermute(moments[j], "member", along_row(j)) for j in (1, 3)]
+        start = jnp.concatenate([own, partner])
+        up1, down1 = fsdp(start, z_up), fsdp(start, z_down)
+        turned = turned.T.reshape(16, 2 * hidden, count)
+        cots = lax.all_to_all(turned, "fsdp", 0, 0, axis_index_groups=same_core, tiled=True)
+    up1, down1, came0, held0, near, moments = sync((up1, down1, came0, held0, near, moments))
+    with jax.named_scope("tick_b"):
+        up2, down2 = fsdp(up1, z_up), fsdp(down1, z_down)
+        far = lax.ppermute(moments[2], "member", along_row(2))
+        held1 = [moments[0], near[0], far, near[1]]
+    up2, down2, came0, held0, held1 = sync((up2, down2, came0, held0, held1))
+    with jax.named_scope("tick_c"):
+        up3, down3 = fsdp(up2, z_up), fsdp(down2, z_down)
+        got0 = gathered(held0, came0)
+        came1 = exchange(held1, spans[0])
+    up3, down3, got0, came1, held1, cots = sync((up3, down3, got0, came1, held1, cots))
+    with jax.named_scope("tick_d"):
+        mine = pick("place", here, winner, got0).reshape(2, hidden, width)
+        theirs = fsdp(mine, core_swap)
+        got1 = columns(held1, came1, spans[0])
+        came2 = exchange(held1, spans[1])
+        sides = [fsdp(up3[:count], z_up), fsdp(down3[count:], z_down)]
+        blocks = [start, up1, down1, up2, down2]
+        sources = [(d, b) for d in (0, -1, 1, -2, 2) for b in range(2)]
+        totals = terms(here, mine, theirs, cots, blocks, sources, None, scale)
+    sides, came2, totals, got1, held1 = sync((sides, came2, totals, got1, held1))
+    with jax.named_scope("tick_e"):
+        got2 = columns(held1, came2, spans[1])
         sources = [(d, b) for d in (-3, 3, 4) for b in range(2)]
         sums = terms(here, mine, theirs, cots, [up3, down3, *sides], sources, totals, scale)
         other = [fsdp(part, core_swap) for part in sums[2:]]
     with jax.named_scope("adam"):
-        return tuple(adam(here, winner, rate, mine, got1, sums[:2], other, scale))
+        new = adam(here, winner, rate, mine, got1, sums[:2], other[0::2], scale, 0, [])
+        return tuple(adam(here, winner, rate, mine, got2, sums[:2], other[1::2], scale, 1, new))
 
 
 def solution(mesh):

time: 460 us -> 262 us (0.57)
  Pallas kernels: 316 us -> 59.5 us
  waiting for transfers between devices: 75.3 us -> 99 us
  local copies, waits for them, and re-layouts: 19 us -> 40.1 us
  starting transfers between devices: 47.1 us -> 59.7 us
    pallas_call x5 -> x7, Pallas kernels: 277 us -> 14.2 us  [pick(): pl.pallas_call(functools.partial(pick_kernel, mode, span), in_specs=[smem...]
    unnamed x56 -> x89, local copies, waits for them, and re-layouts: 12.7 us -> 31.6 us
    ppermute x12 -> x14, waiting for transfers between devices: 15.9 us -> 32.6 us  [fsdp(): return lax.ppermute(value, 'fsdp', pairs)]
    ppermute x2 -> x6, waiting for transfers between devices: 25.3 us -> 37 us  [the longest x3 19.1 us: exchange(): lax.ppermute(pick('cross', here, winner, held, span), 'member', row_swap)]
    all_to_all x1 -> x2, waiting for transfers between devices: 10.3 us -> 0.01 us  [columns(): lax.all_to_all(pick('columns', here, winner, [*held, came], span), 'membe...]
    ppermute x12 -> x14, starting transfers between devices: 15 us -> 23.6 us  [fsdp(): return lax.ppermute(value, 'fsdp', pairs)]
    ppermute x2 -> x6, starting transfers between devices: 3.32 us -> 11.8 us  [the longest x3 8.66 us: exchange(): lax.ppermute(pick('cross', here, winner, held, span), 'member', row_swap)]
    ppermute x9 -> x6, starting transfers between devices: 13.7 us -> 7.22 us  [spread(): return [lax.ppermute(pieces[j], 'member', along_row(j)) for j in (1, 2, 3)]]
  transfers between devices with their start and end apart: 25 -> 29, of which waited for: 13 -> 12; matrix products, arithmetic and copies ran while one was open for 1% -> 2% of each run, Pallas kernels for 56% -> 18%
where the time goes in v3:
time: 262 us; the launch traced here: 260 us
  waiting for transfers between devices  99 us (38%)
  starting transfers between devices  59.7 us (23%)
  Pallas kernels  59.5 us (23%)
  local copies, waits for them, and re-layouts  40.1 us (15%)
    ppermute x14, waiting for transfers between devices, fsdp(): return lax.ppermute(value, 'fsdp', pairs)  32.6 us
    pallas_call x2, Pallas kernels, terms(): pl.pallas_call(kernel, in_specs=[pl.BlockSpec(memory_space=pltpu.SMEM)] +...  32.1 us
    unnamed x89, local copies, waits for them, and re-layouts  31.6 us
    ppermute x6, waiting for transfers between devices, spread(): return [lax.ppermute(pieces[j], 'member', along_row(j)) for j in (1, 2, 3)]  29.3 us
    ppermute x14, starting transfers between devices, fsdp(): return lax.ppermute(value, 'fsdp', pairs)  23.6 us
    ppermute x3, waiting for transfers between devices, exchange(): lax.ppermute(pick('cross', here, winner, held, span), 'member', row_swap)  19.1 us
    ppermute x1, waiting for transfers between devices, body(): far = lax.ppermute(moments[2], 'member', along_row(2))  18 us
    pallas_call x7, Pallas kernels, pick(): pl.pallas_call(functools.partial(pick_kernel, mode, span), in_specs=[smem...  14.2 us
  transfers between devices with their start and end apart: 29, of which 12 were waited for; matrix products, arithmetic and copies ran while one was open for 2% of the time, Pallas kernels for 18%

profile of v3, /device:TPU:1, one launch (start us, length us, event | category | flops | bytes accessed | tf_op | source)
XLA Modules:
  0.0 260.2 jit_solution(18075744346031692453)
XLA Ops:
  0.6 2.2 collective-permute-start
  2.9 1.2 slice_bitcast_fusion.2
  4.0 1.3 collective-permute-start.1
  5.4 1.5 collective-permute-start.3
  6.9 1.5 collective-permute-start.2
  8.5 6.5 %collective-permute-done.1.refs_1_ = bf16[112,1792]{1,0:T(8,128)(2,1)S(1)} collective-permute-done((bf16[112,1792]{1,0:T(8,128)(2,1)S(1)}, bf16[112,1792]{1,0:T(8,128)(2,1)S(1)}, u32[]{:S(2)}, u32[]{:S(2)}) %collective-permute-start.1) | collective-permute-done | bytes 401440 | tf_op jit(solution)/shard_map/tick_a/ppermute | solution.py:293
  15.0 9.7 %collective-permute-done.2.refs_2_ = bf16[112,1792]{1,0:T(8,128)(2,1)S(1)} collective-permute-done((bf16[112,1792]{1,0:T(8,128)(2,1)S(1)}, bf16[112,1792]{1,0:T(8,128)(2,1)S(1)}, u32[]{:S(2)}, u32[]{:S(2)}) %collective-permute-start.2) | collective-permute-done | bytes 401440 | tf_op jit(solution)/shard_map/tick_a/ppermute | solution.py:293
  24.7 3.9 %copy.22 = bf16[7168,128]{1,0:T(8,128)(2,1)} copy(bf16[7168,128]{0,1:T(8,128)(2,1)} %bitcast.29) | data formatting | bytes 3670016 | tf_op jit(solution)/shard_map/tick_b/transpose | solution.py:352
  28.6 8.5 %all-to-all-start = ((bf16[16,448,128]{2,1,0:T(8,128)(2,1)}), bf16[16,448,128]{2,1,0:T(8,128)(2,1)}, u32[]{:S(2)}, u32[]{:S(2)}) async-start(bf16[16,448,128]{2,1,0:T(8,128)(2,1)} %bitcast.28), calls=%async_computation | async-start | bytes 3670016 | tf_op jit(solution)/shard_map/tick_b/all_to_all | solution.py:353
  38.8 2.5 collective-permute-start.5
  41.4 1.5 tick_b.1
  42.9 2.9 %collective-permute-start.6 = (bf16[2,112,1792]{2,1,0:T(8,128)(2,1)S(1)}, bf16[2,112,1792]{2,1,0:T(8,128)(2,1)S(1)}, u32[]{:S(2)}, u32[]{:S(2)}) collective-permute-start(bf16[2,112,1792]{2,1,0:T(8,128)(2,1)S(1)} %tick_b.1), channel_id=1, source_target_pairs={{0,32},{32,0},{64,96},{96,64},{128,160},{160,128},{192,224},{224,1... | collective-permute-start | bytes 2408456 | tf_op jit(solution)/shard_map/tick_b/ppermute | solution.py:323
  46.5 2.0 collective-permute-start.8
  48.4 19.1 %collective-permute-done.6.refs_4_ = bf16[2,112,1792]{2,1,0:T(8,128)(2,1)S(1)} collective-permute-done((bf16[2,112,1792]{2,1,0:T(8,128)(2,1)S(1)}, bf16[2,112,1792]{2,1,0:T(8,128)(2,1)S(1)}, u32[]{:S(2)}, u32[]{:S(2)}) %collective-permute-start.6) | collective-permute-done | bytes 802848 | tf_op jit(solution)/shard_map/tick_b/ppermute | solution.py:323
  67.5 30.6 %collective-permute-done.5.refs_2_ = bf16[256,1792]{1,0:T(8,128)(2,1)} collective-permute-done((bf16[256,1792]{1,0:T(8,128)(2,1)}, bf16[256,1792]{1,0:T(8,128)(2,1)}, u32[]{:S(2)}, u32[]{:S(2)}) %collective-permute-start.5) | collective-permute-done | bytes 917536 | tf_op jit(solution)/shard_map/tick_b/ppermute | solution.py:320
  99.2 2.0 collective-permute-start.10
  101.7 18.0 %collective-permute-done.11.refs_2_ = bf16[224,1792]{1,0:T(8,128)(2,1)S(1)} collective-permute-done((bf16[224,1792]{1,0:T(8,128)(2,1)}, bf16[224,1792]{1,0:T(8,128)(2,1)S(1)}, u32[]{:S(2)}, u32[]{:S(2)}) %collective-permute-start.11) | collective-permute-done | bytes 802848 | tf_op jit(solution)/shard_map/tick_b/ppermute | solution.py:357
  119.7 4.1 %collective-permute-start.12 = (bf16[256,1792]{1,0:T(8,128)(2,1)S(1)}, bf16[256,1792]{1,0:T(8,128)(2,1)}, u32[]{:S(2)}, u32[]{:S(2)}) collective-permute-start(bf16[256,1792]{1,0:T(8,128)(2,1)S(1)} %collective-permute-done.9.refs_3_), channel_id=1, source_target_pairs={{0,4},{1,5},{2,6},{3,7},{4,8},{5,9},{6,10},{7,11},{8,12},{9,13},{1... | collective-permute-start | bytes 2752520 | tf_op jit(solution)/shard_map/tick_c/ppermute | solution.py:320
  123.8 2.4 tick_c.2
  127.6 1.5 tick_c.3
  129.1 2.9 %collective-permute-start.17 = (bf16[2,112,1792]{2,1,0:T(8,128)(2,1)S(1)}, bf16[2,112,1792]{2,1,0:T(8,128)(2,1)S(1)}, u32[]{:S(2)}, u32[]{:S(2)}) collective-permute-start(bf16[2,112,1792]{2,1,0:T(8,128)(2,1)S(1)} %tick_c.3), channel_id=1, source_target_pairs={{0,32},{32,0},{64,96},{96,64},{128,160},{160,128},{192,224},{224,1... | collective-permute-start | bytes 2408456 | tf_op jit(solution)/shard_map/tick_c/ppermute | solution.py:323
  132.0 1.8 collective-permute-start.15
  133.8 2.5 collective-permute-done.14.refs_1_
  137.4 7.5 %collective-permute-done.15.refs_2_ = bf16[112,1792]{1,0:T(8,128)(2,1)S(1)} collective-permute-done((bf16[112,1792]{1,0:T(8,128)(2,1)S(1)}, bf16[112,1792]{1,0:T(8,128)(2,1)S(1)}, u32[]{:S(2)}, u32[]{:S(2)}) %collective-permute-start.15) | collective-permute-done | bytes 401440 | tf_op jit(solution)/shard_map/tick_c/ppermute | solution.py:293
  145.7 3.1 %collective-permute-done.16.refs_3_ = bf16[112,1792]{1,0:T(8,128)(2,1)S(1)} collective-permute-done((bf16[112,1792]{1,0:T(8,128)(2,1)S(1)}, bf16[112,1792]{1,0:T(8,128)(2,1)S(1)}, u32[]{:S(2)}, u32[]{:S(2)}) %collective-permute-start.16) | collective-permute-done | bytes 401440 | tf_op jit(solution)/shard_map/tick_c/ppermute | solution.py:293
  154.4 2.3 tick_d.4
  156.7 8.4 %collective-permute-start.21 = (bf16[2,224,1792]{2,1,0:T(8,128)(2,1)S(1)}, bf16[2,224,1792]{2,1,0:T(8,128)(2,1)}, u32[]{:S(2)}, u32[]{:S(2)}) collective-permute-start(bf16[2,224,1792]{2,1,0:T(8,128)(2,1)S(1)} %bitcast.19), channel_id=1, source_target_pairs={{0,1},{1,0},{2,3},{3,2},{4,5},{5,4},{6,7},{7,6},{8,9},{9,8},{10,11... | collective-permute-start | bytes 4816904 | tf_op jit(solution)/shard_map/tick_d/ppermute | solution.py:320
  165.2 2.4 tick_d.7
  167.6 1.1 copy-done.11
  168.7 4.4 %all-to-all-start.1 = ((bf16[4,112,1792]{2,1,0:T(8,128)(2,1)}), bf16[4,112,1792]{2,1,0:T(8,128)(2,1)}, u32[]{:S(2)}, u32[]{:S(2)}) async-start(bf16[4,112,1792]{2,1,0:T(8,128)(2,1)} %copy-done.11), calls=%async_computation.1 | async-start | bytes 3211264 | tf_op jit(solution)/shard_map/tick_d/all_to_all | solution.py:330
  174.2 1.1 copy-done.9
  175.4 1.5 tick_d.5
  176.8 2.9 %collective-permute-start.20 = (bf16[2,112,1792]{2,1,0:T(8,128)(2,1)S(1)}, bf16[2,112,1792]{2,1,0:T(8,128)(2,1)S(1)}, u32[]{:S(2)}, u32[]{:S(2)}) collective-permute-start(bf16[2,112,1792]{2,1,0:T(8,128)(2,1)S(1)} %tick_d.5), channel_id=1, source_target_pairs={{0,32},{32,0},{64,96},{96,64},{128,160},{160,128},{192,224},{224,1... | collective-permute-start | bytes 2408456 | tf_op jit(solution)/shard_map/tick_d/ppermute | solution.py:323
  181.9 1.5 collective-permute-start.18
  183.5 18.1 %tick_d.6 = (f32[224,1792]{1,0:T(8,128)}, f32[224,1792]{1,0:T(8,128)}, f32[112,1792]{1,0:T(8,128)S(1)}, f32[112,1792]{1,0:T(8,128)S(1)}, f32[112,1792]{1,0:T(8,128)S(1)}, /*index=5*/f32[112,1792]{1,0:T(8,128)S(1)}) custom-call(s32[2]{0:T(128)S(1)} %pad_add_fusion.here, bf16[2,224,1792]{2,1,0:T(8,128)(2,1)} %bitcast.20, ...), custom_call_target="tpu_custom_call" | custom-call | flops 8220835840 | bytes 20971520 | tf_op jit(solution)/shard_map/tick_d/pallas_call | solution.py:137
  207.6 1.1 copy-done.6
  208.7 1.1 copy-done.10
  211.0 2.7 %tick_e.2 = bf16[4,112,1792]{2,1,0:T(8,128)(2,1)} custom-call(s32[2]{0:T(128)S(1)} %pad_add_fusion.here, s32[8]{0:T(128)S(1)} %copy-done.28, bf16[224,1792]{1,0:T(8,128)(2,1)S(1)} %bitcast.27, bf16[224,1792]{1,0:T(8,128)(2,1)S(1)} %collective-permute-done.7.refs_1_, bf16[224,1792]{1,0:T(8,128)(2,1)S(1)} %copy-done.10, bf16[224,1792]{1,0:T(8,128)(2,1)S(1)} %copy-done.6, ...), custom_call_target="tpu_custom_call" | custom-call | bytes 3211264 | tf_op jit(solution)/shard_map/tick_e/pallas_call | solution.py:276
  213.7 4.2 %all-to-all-start.2 = ((bf16[4,112,1792]{2,1,0:T(8,128)(2,1)}), bf16[4,112,1792]{2,1,0:T(8,128)(2,1)S(1)}, u32[]{:S(2)}, u32[]{:S(2)}) async-start(bf16[4,112,1792]{2,1,0:T(8,128)(2,1)} %tick_e.2), calls=%async_computation.2 | async-start | bytes 3211264 | tf_op jit(solution)/shard_map/tick_e/all_to_all | solution.py:330
  222.3 14.0 %tick_e.3 = (f32[224,1792]{1,0:T(8,128)}, f32[224,1792]{1,0:T(8,128)}, f32[112,1792]{1,0:T(8,128)}, f32[112,1792]{1,0:T(8,128)}, f32[112,1792]{1,0:T(8,128)}, /*index=5*/f32[112,1792]{1,0:T(8,128)}) custom-call(s32[2]{0:T(128)S(1)} %pad_add_fusion.here, bf16[2,224,1792]{2,1,0:T(8,128)(2,1)} %bitcast.21, ...), custom_call_target="tpu_custom_call" | custom-call | flops 4932501504 | bytes 20971520 | tf_op jit(solution)/shard_map/tick_e/pallas_call | solution.py:137
  236.3 1.4 collective-permute-start.24
  240.0 1.1 collective-permute-done.25.refs_4_
  241.1 1.4 copy-done.12
  242.5 1.4 copy-done.14
  244.0 6.9 %adam.2 = (bf16[1,224,1792]{2,1,0:T(8,128)(2,1)}, bf16[1,224,1792]{2,1,0:T(8,128)(2,1)}, bf16[1,224,1792]{2,1,0:T(8,128)(2,1)}, bf16[1,224,1792]{2,1,0:T(8,128)(...) custom-call(s32[2]{0:T(128)S(1)} %pad_add_fusion.here, s32[8]{0:T(128)S(1)} %copy-done.28, ...), custom_call_target="tpu_custom_call" | custom-call | flops 16056320 | bytes 8388608 | tf_op jit(solution)/shard_map/adam/pallas_call | solution.py:193
  250.9 1.4 copy-done.13
  252.3 1.4 copy-done.15
  253.7 6.3 %adam.3 = (bf16[1,224,1792]{2,1,0:T(8,128)(2,1)}, bf16[1,224,1792]{2,1,0:T(8,128)(2,1)}, bf16[1,224,1792]{2,1,0:T(8,128)(2,1)}, bf16[1,224,1792]{2,1,0:T(8,128)(...) custom-call(s32[2]{0:T(128)S(1)} %pad_add_fusion.here, ...), custom_call_target="tpu_custom_call", output_to_operand_aliasing={{0}: (9, {}), {1}: (10, {}), {2}: (11, {}), {3}: (12, {}), ... | custom-call | flops 16056320 | bytes 8388608 | tf_op jit(solution)/shard_map/adam/pallas_call | solution.py:193
  (118 shorter events, 29.6 us)
Async XLA Ops:
  0.6 4.7 %copy-start.39 = (bf16[1,224,1792]{2,1,0:T(8,128)(2,1)S(1)}, bf16[1,224,1792]{2,1,0:T(8,128)(2,1)}, u32[]{:S(2)}) copy-start(bf16[1,224,1792]{2,1,0:T(8,128)(2,1)} %param.13) | copy-start | bytes 2408452
  0.6 24.1 %collective-permute-start = (bf16[128,1792]{1,0:T(8,128)(2,1)}, bf16[128,1792]{1,0:T(8,128)(2,1)S(1)}, u32[]{:S(2)}, u32[]{:S(2)}) collective-permute-start(bf16[128,1792]{1,0:T(8,128)(2,1)} %bitcast.30), channel_id=1, source_target_pairs={{0,2},{1,3},{2,0},{3,1},{4,6},{5,7},{6,4},{7,5},{8,10},{9,11},{10,... | collective-permute-start | bytes 1376264 | tf_op jit(solution)/shard_map/tick_a/ppermute | solution.py:320
  4.0 10.9 %collective-permute-start.1 = (bf16[112,1792]{1,0:T(8,128)(2,1)S(1)}, bf16[112,1792]{1,0:T(8,128)(2,1)S(1)}, u32[]{:S(2)}, u32[]{:S(2)}) collective-permute-start(bf16[112,1792]{1,0:T(8,128)(2,1)S(1)} %get-tuple-element.170), channel_id=1, source_target_pairs={{0,64},{32,96},{64,128},{96,160},{128,192},{160,224},{192,0},{224,... | collective-permute-start | bytes 1204232 | tf_op jit(solution)/shard_map/tick_a/ppermute | solution.py:293
  5.4 9.6 %collective-permute-start.3 = (bf16[112,1792]{1,0:T(8,128)(2,1)S(1)}, bf16[112,1792]{1,0:T(8,128)(2,1)S(1)}, u32[]{:S(2)}, u32[]{:S(2)}) collective-permute-start(bf16[112,1792]{1,0:T(8,128)(2,1)S(1)} %get-tuple-element.168), channel_id=1, source_target_pairs={{0,192},{32,224},{64,0},{96,32},{128,64},{160,96},{192,128},{224,1... | collective-permute-start | bytes 1204232 | tf_op jit(solution)/shard_map/tick_a/ppermute | solution.py:293
  6.9 17.8 %collective-permute-start.2 = (bf16[112,1792]{1,0:T(8,128)(2,1)S(1)}, bf16[112,1792]{1,0:T(8,128)(2,1)S(1)}, u32[]{:S(2)}, u32[]{:S(2)}) collective-permute-start(bf16[112,1792]{1,0:T(8,128)(2,1)S(1)} %get-tuple-element.169), channel_id=1, source_target_pairs={{0,128},{32,160},{64,192},{96,224},{128,0},{160,32},{192,64},{224,... | collective-permute-start | bytes 1204232 | tf_op jit(solution)/shard_map/tick_a/ppermute | solution.py:293
  28.6 8.5 %copy-start.40 = (bf16[1,128,1792]{2,1,0:T(8,128)(2,1)S(1)}, bf16[1,128,1792]{2,1,0:T(8,128)(2,1)}, u32[]{:S(2)}) copy-start(bf16[1,128,1792]{2,1,0:T(8,128)(2,1)} %param.10) | copy-start | bytes 1376260
  28.6 121.8 %all-to-all-start = ((bf16[16,448,128]{2,1,0:T(8,128)(2,1)}), bf16[16,448,128]{2,1,0:T(8,128)(2,1)}, u32[]{:S(2)}, u32[]{:S(2)}) async-start(bf16[16,448,128]{2,1,0:T(8,128)(2,1)} %bitcast.28), calls=%async_computation | async-start | bytes 3670016 | tf_op jit(solution)/shard_map/tick_b/all_to_all | solution.py:353
  37.1 4.3 %copy-start.28 = (s32[8]{0:T(128)S(1)}, s32[8]{0:T(128)}, u32[]{:S(2)}) copy-start(s32[8]{0:T(128)} %winner.17) | copy-start | bytes 100
  38.8 59.3 %collective-permute-start.5 = (bf16[256,1792]{1,0:T(8,128)(2,1)}, bf16[256,1792]{1,0:T(8,128)(2,1)}, u32[]{:S(2)}, u32[]{:S(2)}) collective-permute-start(bf16[256,1792]{1,0:T(8,128)(2,1)} %constant_dynamic-update-slice_fusion.refs_0_), channel_id=1, source_target_pairs={{4,0},{5,1},{6,2},{7,3},{8,4},{9,5},{10,6},{11,7},{12,8},{13,9},{1... | collective-permute-start | bytes 2752520 | tf_op jit(solution)/shard_map/tick_b/ppermute | solution.py:320
  41.3 57.2 %collective-permute-start.4 = (bf16[256,1792]{1,0:T(8,128)(2,1)}, bf16[256,1792]{1,0:T(8,128)(2,1)}, u32[]{:S(2)}, u32[]{:S(2)}) collective-permute-start(bf16[256,1792]{1,0:T(8,128)(2,1)} %constant_dynamic-update-slice_fusion.refs_0_), channel_id=1, source_target_pairs={{0,4},{1,5},{2,6},{3,7},{4,8},{5,9},{6,10},{7,11},{8,12},{9,13},{1... | collective-permute-start | bytes 2752520 | tf_op jit(solution)/shard_map/tick_b/ppermute | solution.py:320
  42.8 84.8 %copy-start.2 = (bf16[1,224,1792]{2,1,0:T(8,128)(2,1)S(1)}, bf16[1,224,1792]{2,1,0:T(8,128)(2,1)}, u32[]{:S(2)}) copy-start(bf16[1,224,1792]{2,1,0:T(8,128)(2,1)} %param.14) | copy-start | bytes 2408452
  42.9 24.6 %collective-permute-start.6 = (bf16[2,112,1792]{2,1,0:T(8,128)(2,1)S(1)}, bf16[2,112,1792]{2,1,0:T(8,128)(2,1)S(1)}, u32[]{:S(2)}, u32[]{:S(2)}) collective-permute-start(bf16[2,112,1792]{2,1,0:T(8,128)(2,1)S(1)} %tick_b.1), channel_id=1, source_target_pairs={{0,32},{32,0},{64,96},{96,64},{128,160},{160,128},{192,224},{224,1... | collective-permute-start | bytes 2408456 | tf_op jit(solution)/shard_map/tick_b/ppermute | solution.py:323
  45.7 21.7 %collective-permute-start.7 = (bf16[224,1792]{1,0:T(8,128)(2,1)}, bf16[224,1792]{1,0:T(8,128)(2,1)S(1)}, u32[]{:S(2)}, u32[]{:S(2)}) collective-permute-start(bf16[224,1792]{1,0:T(8,128)(2,1)} %bitcast.32), channel_id=1, source_target_pairs={{0,64},{32,96},{64,128},{96,160},{128,192},{160,224},{192,0},{224,... | collective-permute-start | bytes 2408456 | tf_op jit(solution)/shard_map/tick_b/ppermute | solution.py:349
  46.5 21.0 %collective-permute-start.8 = (bf16[224,1792]{1,0:T(8,128)(2,1)}, bf16[224,1792]{1,0:T(8,128)(2,1)S(1)}, u32[]{:S(2)}, u32[]{:S(2)}) collective-permute-start(bf16[224,1792]{1,0:T(8,128)(2,1)} %bitcast.33), channel_id=1, source_target_pairs={{0,192},{32,224},{64,0},{96,32},{128,64},{160,96},{192,128},{224,1... | collective-permute-start | bytes 2408456 | tf_op jit(solution)/shard_map/tick_b/ppermute | solution.py:349
  67.5 61.6 %copy-start.3 = (bf16[224,1792]{1,0:T(8,128)(2,1)}, bf16[224,1792]{1,0:T(8,128)(2,1)S(1)}, u32[]{:S(2)}) copy-start(bf16[224,1792]{1,0:T(8,128)(2,1)S(1)} %collective-permute-done.8.refs_3_) | copy-start | bytes 2408452
  98.5 21.2 %collective-permute-start.9 = (bf16[256,1792]{1,0:T(8,128)(2,1)}, bf16[256,1792]{1,0:T(8,128)(2,1)S(1)}, u32[]{:S(2)}, u32[]{:S(2)}) collective-permute-start(bf16[256,1792]{1,0:T(8,128)(2,1)} %collective-permute-done.4.refs_1_), channel_id=1, source_target_pairs={{0,4},{1,5},{2,6},{3,7},{4,8},{5,9},{6,10},{7,11},{8,12},{9,13},{1... | collective-permute-start | bytes 2752520 | tf_op jit(solution)/shard_map/tick_b/ppermute | solution.py:320
  99.2 20.5 %collective-permute-start.10 = (bf16[256,1792]{1,0:T(8,128)(2,1)}, bf16[256,1792]{1,0:T(8,128)(2,1)S(1)}, u32[]{:S(2)}, u32[]{:S(2)}) collective-permute-start(bf16[256,1792]{1,0:T(8,128)(2,1)} %collective-permute-done.5.refs_2_), channel_id=1, source_target_pairs={{4,0},{5,1},{6,2},{7,3},{8,4},{9,5},{10,6},{11,7},{12,8},{13,9},{1... | collective-permute-start | bytes 2752520 | tf_op jit(solution)/shard_map/tick_b/ppermute | solution.py:320
  101.2 18.5 %collective-permute-start.11 = (bf16[224,1792]{1,0:T(8,128)(2,1)}, bf16[224,1792]{1,0:T(8,128)(2,1)S(1)}, u32[]{:S(2)}, u32[]{:S(2)}) collective-permute-start(bf16[224,1792]{1,0:T(8,128)(2,1)} %bitcast.34), channel_id=1, source_target_pairs={{0,128},{32,160},{64,192},{96,224},{128,0},{160,32},{192,64},{224,... | collective-permute-start | bytes 2408456 | tf_op jit(solution)/shard_map/tick_b/ppermute | solution.py:357
  119.7 9.5 %copy-start.7 = (bf16[224,1792]{1,0:T(8,128)(2,1)}, bf16[224,1792]{1,0:T(8,128)(2,1)S(1)}, u32[]{:S(2)}) copy-start(bf16[224,1792]{1,0:T(8,128)(2,1)S(1)} %collective-permute-done.11.refs_2_) | copy-start | bytes 2408452
  119.7 29.8 %copy-start.41 = (bf16[256,1792]{1,0:T(8,128)(2,1)}, bf16[256,1792]{1,0:T(8,128)(2,1)S(1)}, u32[]{:S(2)}) copy-start(bf16[256,1792]{1,0:T(8,128)(2,1)S(1)} %collective-permute-done.9.refs_3_) | copy-start | bytes 2752516
  119.7 30.7 %copy-start.42 = (bf16[256,1792]{1,0:T(8,128)(2,1)}, bf16[256,1792]{1,0:T(8,128)(2,1)S(1)}, u32[]{:S(2)}) copy-start(bf16[256,1792]{1,0:T(8,128)(2,1)S(1)} %collective-permute-done.10.refs_4_) | copy-start | bytes 2752516
  119.7 30.7 %collective-permute-start.12 = (bf16[256,1792]{1,0:T(8,128)(2,1)S(1)}, bf16[256,1792]{1,0:T(8,128)(2,1)}, u32[]{:S(2)}, u32[]{:S(2)}) collective-permute-start(bf16[256,1792]{1,0:T(8,128)(2,1)S(1)} %collective-permute-done.9.refs_3_), channel_id=1, source_target_pairs={{0,4},{1,5},{2,6},{3,7},{4,8},{5,9},{6,10},{7,11},{8,12},{9,13},{1... | collective-permute-start | bytes 2752520 | tf_op jit(solution)/shard_map/tick_c/ppermute | solution.py:320
  123.8 26.6 %collective-permute-start.13 = (bf16[256,1792]{1,0:T(8,128)(2,1)S(1)}, bf16[256,1792]{1,0:T(8,128)(2,1)}, u32[]{:S(2)}, u32[]{:S(2)}) collective-permute-start(bf16[256,1792]{1,0:T(8,128)(2,1)S(1)} %collective-permute-done.10.refs_4_), channel_id=1, source_target_pairs={{4,0},{5,1},{6,2},{7,3},{8,4},{9,5},{10,6},{11,7},{12,8},{13,9},{1... | collective-permute-start | bytes 2752520 | tf_op jit(solution)/shard_map/tick_c/ppermute | solution.py:320
  126.9 9.4 %collective-permute-start.14 = (bf16[112,1792]{1,0:T(8,128)(2,1)S(1)}, bf16[112,1792]{1,0:T(8,128)(2,1)S(1)}, u32[]{:S(2)}, u32[]{:S(2)}) collective-permute-start(bf16[112,1792]{1,0:T(8,128)(2,1)S(1)} %get-tuple-element.116), channel_id=1, source_target_pairs={{0,64},{32,96},{64,128},{96,160},{128,192},{160,224},{192,0},{224,... | collective-permute-start | bytes 1204232 | tf_op jit(solution)/shard_map/tick_c/ppermute | solution.py:293
  129.1 20.4 %collective-permute-start.17 = (bf16[2,112,1792]{2,1,0:T(8,128)(2,1)S(1)}, bf16[2,112,1792]{2,1,0:T(8,128)(2,1)S(1)}, u32[]{:S(2)}, u32[]{:S(2)}) collective-permute-start(bf16[2,112,1792]{2,1,0:T(8,128)(2,1)S(1)} %tick_c.3), channel_id=1, source_target_pairs={{0,32},{32,0},{64,96},{96,64},{128,160},{160,128},{192,224},{224,1... | collective-permute-start | bytes 2408456 | tf_op jit(solution)/shard_map/tick_c/ppermute | solution.py:323
  132.0 12.9 %collective-permute-start.15 = (bf16[112,1792]{1,0:T(8,128)(2,1)S(1)}, bf16[112,1792]{1,0:T(8,128)(2,1)S(1)}, u32[]{:S(2)}, u32[]{:S(2)}) collective-permute-start(bf16[112,1792]{1,0:T(8,128)(2,1)S(1)} %get-tuple-element.117), channel_id=1, source_target_pairs={{0,128},{32,160},{64,192},{96,224},{128,0},{160,32},{192,64},{224,... | collective-permute-start | bytes 1204232 | tf_op jit(solution)/shard_map/tick_c/ppermute | solution.py:293
  137.0 11.7 %collective-permute-start.16 = (bf16[112,1792]{1,0:T(8,128)(2,1)S(1)}, bf16[112,1792]{1,0:T(8,128)(2,1)S(1)}, u32[]{:S(2)}, u32[]{:S(2)}) collective-permute-start(bf16[112,1792]{1,0:T(8,128)(2,1)S(1)} %get-tuple-element.118), channel_id=1, source_target_pairs={{0,192},{32,224},{64,0},{96,32},{128,64},{160,96},{192,128},{224,1... | collective-permute-start | bytes 1204232 | tf_op jit(solution)/shard_map/tick_c/ppermute | solution.py:293
  154.4 10.7 %copy-start.4 = (bf16[224,1792]{1,0:T(8,128)(2,1)S(1)}, bf16[224,1792]{1,0:T(8,128)(2,1)}, u32[]{:S(2)}) copy-start(bf16[224,1792]{1,0:T(8,128)(2,1)} %copy-done.3) | copy-start | bytes 2408452
  154.4 10.7 %copy-start.8 = (bf16[224,1792]{1,0:T(8,128)(2,1)S(1)}, bf16[224,1792]{1,0:T(8,128)(2,1)}, u32[]{:S(2)}) copy-start(bf16[224,1792]{1,0:T(8,128)(2,1)} %copy-done.7) | copy-start | bytes 2408452
  154.4 10.7 %copy-start.19 = (bf16[2,112,1792]{2,1,0:T(8,128)(2,1)S(1)}, bf16[2,112,1792]{2,1,0:T(8,128)(2,1)}, u32[]{:S(2)}) copy-start(bf16[2,112,1792]{2,1,0:T(8,128)(2,1)} %copy-done.18) | copy-start | bytes 2408452
  156.7 10.8 %copy-start = (bf16[4,112,1792]{2,1,0:T(8,128)(2,1)}, bf16[4,112,1792]{2,1,0:T(8,128)(2,1)S(1)}, u32[]{:S(2)}) copy-start(bf16[4,112,1792]{2,1,0:T(8,128)(2,1)S(1)} %tick_d.4) | copy-start | bytes 4816900
  156.7 26.7 %collective-permute-start.21 = (bf16[2,224,1792]{2,1,0:T(8,128)(2,1)S(1)}, bf16[2,224,1792]{2,1,0:T(8,128)(2,1)}, u32[]{:S(2)}, u32[]{:S(2)}) collective-permute-start(bf16[2,224,1792]{2,1,0:T(8,128)(2,1)S(1)} %bitcast.19), channel_id=1, source_target_pairs={{0,1},{1,0},{2,3},{3,2},{4,5},{5,4},{6,7},{7,6},{8,9},{9,8},{10,11... | collective-permute-start | bytes 4816904 | tf_op jit(solution)/shard_map/tick_d/ppermute | solution.py:320
  167.5 1.2 copy-start.11
  168.7 38.9 %all-to-all-start.1 = ((bf16[4,112,1792]{2,1,0:T(8,128)(2,1)}), bf16[4,112,1792]{2,1,0:T(8,128)(2,1)}, u32[]{:S(2)}, u32[]{:S(2)}) async-start(bf16[4,112,1792]{2,1,0:T(8,128)(2,1)} %copy-done.11), calls=%async_computation.1 | async-start | bytes 3211264 | tf_op jit(solution)/shard_map/tick_d/all_to_all | solution.py:330
  176.8 29.9 %collective-permute-start.20 = (bf16[2,112,1792]{2,1,0:T(8,128)(2,1)S(1)}, bf16[2,112,1792]{2,1,0:T(8,128)(2,1)S(1)}, u32[]{:S(2)}, u32[]{:S(2)}) collective-permute-start(bf16[2,112,1792]{2,1,0:T(8,128)(2,1)S(1)} %tick_d.5), channel_id=1, source_target_pairs={{0,32},{32,0},{64,96},{96,64},{128,160},{160,128},{192,224},{224,1... | collective-permute-start | bytes 2408456 | tf_op jit(solution)/shard_map/tick_d/ppermute | solution.py:323
  181.8 23.3 %collective-permute-start.19 = (bf16[128,1792]{1,0:T(8,128)(2,1)S(1)}, bf16[128,1792]{1,0:T(8,128)(2,1)S(1)}, u32[]{:S(2)}, u32[]{:S(2)}) collective-permute-start(bf16[128,1792]{1,0:T(8,128)(2,1)S(1)} %slice.23), channel_id=1, source_target_pairs={{4,0},{5,1},{6,2},{7,3},{8,4},{9,5},{10,6},{11,7},{12,8},{13,9},{1... | collective-permute-start | bytes 1376264 | tf_op jit(solution)/shard_map/tick_d/ppermute | solution.py:320
  181.9 24.0 %collective-permute-start.18 = (bf16[128,1792]{1,0:T(8,128)(2,1)S(1)}, bf16[128,1792]{1,0:T(8,128)(2,1)S(1)}, u32[]{:S(2)}, u32[]{:S(2)}) collective-permute-start(bf16[128,1792]{1,0:T(8,128)(2,1)S(1)} %slice.22), channel_id=1, source_target_pairs={{0,4},{1,5},{2,6},{3,7},{4,8},{5,9},{6,10},{7,11},{8,12},{9,13},{1... | collective-permute-start | bytes 1376264 | tf_op jit(solution)/shard_map/tick_d/ppermute | solution.py:320
  213.7 37.1 %all-to-all-start.2 = ((bf16[4,112,1792]{2,1,0:T(8,128)(2,1)}), bf16[4,112,1792]{2,1,0:T(8,128)(2,1)S(1)}, u32[]{:S(2)}, u32[]{:S(2)}) async-start(bf16[4,112,1792]{2,1,0:T(8,128)(2,1)} %tick_e.2), calls=%async_computation.2 | async-start | bytes 3211264 | tf_op jit(solution)/shard_map/tick_e/all_to_all | solution.py:330
  222.3 16.0 %copy-start.43 = (s32[8]{0:T(128)S(1)}, s32[8]{0:T(128)}, u32[]{:S(2)}) copy-start(s32[8]{0:T(128)} %param.19) | copy-start | bytes 100
  222.3 18.8 %copy-start.1 = (bf16[4,112,1792]{2,1,0:T(8,128)(2,1)S(1)}, bf16[4,112,1792]{2,1,0:T(8,128)(2,1)}, u32[]{:S(2)}) copy-start(bf16[4,112,1792]{2,1,0:T(8,128)(2,1)} %copy-done) | copy-start | bytes 4816900
  236.3 3.7 %collective-permute-start.24 = (f32[112,1792]{1,0:T(8,128)}, f32[112,1792]{1,0:T(8,128)}, u32[]{:S(2)}, u32[]{:S(2)}) collective-permute-start(f32[112,1792]{1,0:T(8,128)} %get-tuple-element.160), channel_id=1, source_target_pairs={{0,1},{1,0},{2,3},{3,2},{4,5},{5,4},{6,7},{7,6},{8,9},{9,8},{10,11... | collective-permute-start | bytes 2408456 | tf_op jit(solution)/shard_map/tick_e/ppermute | solution.py:320
  237.7 3.4 %collective-permute-start.25 = (f32[112,1792]{1,0:T(8,128)}, f32[112,1792]{1,0:T(8,128)}, u32[]{:S(2)}, u32[]{:S(2)}) collective-permute-start(f32[112,1792]{1,0:T(8,128)} %get-tuple-element.161), channel_id=1, source_target_pairs={{0,1},{1,0},{2,3},{3,2},{4,5},{5,4},{6,7},{7,6},{8,9},{9,8},{10,11... | collective-permute-start | bytes 2408456 | tf_op jit(solution)/shard_map/tick_e/ppermute | solution.py:320
  237.8 13.1 %collective-permute-start.22 = (f32[112,1792]{1,0:T(8,128)}, f32[112,1792]{1,0:T(8,128)}, u32[]{:S(2)}, u32[]{:S(2)}) collective-permute-start(f32[112,1792]{1,0:T(8,128)} %get-tuple-element.157), channel_id=1, source_target_pairs={{0,1},{1,0},{2,3},{3,2},{4,5},{5,4},{6,7},{7,6},{8,9},{9,8},{10,11... | collective-permute-start | bytes 2408456 | tf_op jit(solution)/shard_map/tick_e/ppermute | solution.py:320
  238.2 12.7 %collective-permute-start.23 = (f32[112,1792]{1,0:T(8,128)}, f32[112,1792]{1,0:T(8,128)}, u32[]{:S(2)}, u32[]{:S(2)}) collective-permute-start(f32[112,1792]{1,0:T(8,128)} %get-tuple-element.158), channel_id=1, source_target_pairs={{0,1},{1,0},{2,3},{3,2},{4,5},{5,4},{6,7},{7,6},{8,9},{9,8},{10,11... | collective-permute-start | bytes 2408456 | tf_op jit(solution)/shard_map/tick_e/ppermute | solution.py:320
  241.1 1.4 copy-start.12
  242.5 1.4 copy-start.14
  250.9 1.4 copy-start.13
  252.3 1.4 copy-start.15
  (25 other events, 23.9 us)

commit v4 on v3

--- a/solution.py
+++ b/solution.py
@@ -147,7 +147,7 @@
             pltpu.VMEM((4 * rows, total), jnp.bfloat16),
             pltpu.SemaphoreType.DMA((10 + len(blocks) + len(sources),)),
         ],
-        compiler_params=pltpu.CompilerParams(vmem_limit_bytes=48 * 2**20),
+        compiler_params=pltpu.CompilerParams(vmem_limit_bytes=60 * 2**20),
         cost_estimate=pl.CostEstimate(
             flops=16 * rows * width * total,
             bytes_accessed=20 * 2**20,
@@ -162,15 +162,18 @@
 
 
 def adam_kernel(scale, here, winner, rate, w_ref, *refs):
-    got, kept, came, outs = refs[0], refs[1:3], refs[3:5], refs[-6:]
+    got, kept, came, outs = refs[:2], refs[2:4], refs[4:8], refs[8:]
     learning = rate[0]
     column = winner[here[0]] // 2
+    early = pl.program_id(0) < pl.num_programs(0) // 2
 
     def moment(part):
-        return got[(column + part) % 4].astype(jnp.float32)
+        which = (column + part) % 4
+        return jnp.where(early, got[0][which], got[1][which]).astype(jnp.float32)
 
     for p in range(2):
-        grad = (kept[p][...] + came[p][...]) * scale
+        sent = jnp.where(early, came[2 * p][...], came[2 * p + 1][...])
+        grad = (kept[p][...] + sent) * scale
         first_new = 0.9 * moment(p) + 0.1 * grad
         second_new = 0.95 * moment(2 + p) + 0.05 * grad * grad
         update = learning * (first_new / bias_first) / (jnp.sqrt(second_new / bias_second) + 1e-08)
@@ -179,32 +182,40 @@
         outs[4 + p][0] = second_new.astype(jnp.bfloat16)
 
 
-def adam(here, winner, rate, weights, got, mine, other, scale, part, earlier):
+def adam(here, winner, rate, weights, got, mine, other, scale):
     hidden, width = weights.shape[1], weights.shape[2]
     rows = 16
-    steps = got.shape[1] // rows
-    off = part * steps
-    pair = pl.BlockSpec((2, rows, width), lambda i, *_: (0, i + off, 0))
-    four = pl.BlockSpec((4, rows, width), lambda i, *_: (0, i, 0))
-    flat = pl.BlockSpec((rows, width), lambda i, *_: (i + off, 0))
-    piece = pl.BlockSpec((rows, width), lambda i, *_: (i, 0))
-    one = pl.BlockSpec((1, rows, width), lambda i, *_: (0, i + off, 0))
-    whole = pl.BlockSpec(memory_space=pl.ANY)
+    steps = hidden // rows
+    middle = steps // 2
+
+    def first_half(i):
+        return jnp.minimum(i, middle - 1)
+
+    def second_half(i):
+        return jnp.maximum(i - middle, 0)
+
+    pair = pl.BlockSpec((2, rows, width), lambda i, *_: (0, i, 0))
+    flat = pl.BlockSpec((rows, width), lambda i, *_: (i, 0))
+    one = pl.BlockSpec((1, rows, width), lambda i, *_: (0, i, 0))
+    fours = [
+        pl.BlockSpec((4, rows, width), lambda i, *_: (0, first_half(i), 0)),
+        pl.BlockSpec((4, rows, width), lambda i, *_: (0, second_half(i), 0)),
+    ]
+    pieces = [
+        pl.BlockSpec((rows, width), lambda i, *_: (first_half(i), 0)),
+        pl.BlockSpec((rows, width), lambda i, *_: (second_half(i), 0)),
+    ]
     return pl.pallas_call(
         functools.partial(adam_kernel, scale),
         grid_spec=pltpu.PrefetchScalarGridSpec(
             num_scalar_prefetch=3,
             grid=(steps,),
-            in_specs=[pair, four] + [flat] * 2 + [piece] * 2 + [whole] * len(earlier),
+            in_specs=[pair, *fours, flat, flat, *pieces, *pieces],
             out_specs=[one] * 6,
         ),
         out_shape=[jax.ShapeDtypeStruct((1, hidden, width), jnp.bfloat16)] * 6,
-        input_output_aliases={9 + k: k for k in range(len(earlier))},
-        compiler_params=pltpu.CompilerParams(vmem_limit_bytes=32 * 2**20),
-        cost_estimate=pl.CostEstimate(
-            flops=40 * hidden * width, bytes_accessed=8 * 2**20, transcendentals=hidden * width
-        ),
-    )(here, winner, rate, weights, got, *mine, *other, *earlier)
+        compiler_params=pltpu.CompilerParams(vmem_limit_bytes=60 * 2**20),
+    )(here, winner, rate, weights, *got, *mine, *other)
 
 
 def losers(winner):
@@ -234,7 +245,7 @@
     return wanted
 
 
-def pick_kernel(mode, span, here, winner, *refs):
+def pick_kernel(mode, here, winner, *refs):
     count = 2 if mode == "cross" else 4
     stage, sems = refs[-2:]
     if mode == "gather":
@@ -245,7 +256,7 @@
     if mode in ("gather", "columns"):
         last = refs.pop()
         came = [last.at[0], last.at[1]]
-    choices = [ref.at[pl.ds(span[0], span[1])] for ref in refs] + came
+    choices = refs + came
     index = route(mode, here, winner)
     for k in range(count):
         for i, ref in enumerate(choices):
@@ -261,12 +272,10 @@
         pltpu.make_async_copy(stage.at[k], outs[k], sems.at[4 + k]).wait()
 
 
-def pick(mode, here, winner, arrays, span=None):
-    rows, width = arrays[0].shape
-    span = span or (0, rows)
+def pick(mode, here, winner, arrays):
+    shape = arrays[0].shape
     kind = arrays[0].dtype
     count = 2 if mode == "cross" else 4
-    shape = (span[1], width)
     smem = pl.BlockSpec(memory_space=pltpu.SMEM)
     anywhere = pl.BlockSpec(memory_space=pl.ANY)
     if mode == "gather":
@@ -274,7 +283,7 @@
     else:
         out_shape, out_specs = jax.ShapeDtypeStruct((count,) + shape, kind), anywhere
     return pl.pallas_call(
-        functools.partial(pick_kernel, mode, span),
+        functools.partial(pick_kernel, mode),
         in_specs=[smem, smem] + [anywhere] * len(arrays),
         out_specs=out_specs,
         out_shape=out_shape,
@@ -282,9 +291,9 @@
             pltpu.VMEM((count,) + shape, kind),
             pltpu.SemaphoreType.DMA((8,)),
         ],
-        compiler_params=pltpu.CompilerParams(vmem_limit_bytes=16 * 2**20),
+        compiler_params=pltpu.CompilerParams(vmem_limit_bytes=60 * 2**20),
         cost_estimate=pl.CostEstimate(
-            flops=0, bytes_accessed=4 * count * span[1] * width, transcendentals=0
+            flops=0, bytes_accessed=4 * count * arrays[0].size, transcendentals=0
         ),
     )(here, winner, *arrays)
 
@@ -319,16 +328,16 @@
     def fsdp(value, pairs):
         return lax.ppermute(value, "fsdp", pairs)
 
-    def exchange(held, span=None):
-        return lax.ppermute(pick("cross", here, winner, held, span), "member", row_swap)
+    def exchange(held):
+        return lax.ppermute(pick("cross", here, winner, held), "member", row_swap)
 
     def gathered(held, came):
         sent = pick("gather", here, winner, [*held, came])
         return [sent[0], *spread(sent)]
 
-    def columns(held, came, span):
+    def columns(held, came):
         return lax.all_to_all(
-            pick("columns", here, winner, [*held, came], span),
+            pick("columns", here, winner, [*held, came]),
             "member",
             0,
             0,
@@ -336,50 +345,57 @@
             tiled=True,
         )
 
-    half = hidden // 2
-    spans = [(0, half), (half, half)]
-    weights = [w[0, k * half : (k + 1) * half] for w in (gate_weight, up_weight) for k in range(2)]
-    moments = [m[0] for m in (gate_first, up_first, gate_second, up_second)]
+    def rows_of(array, k):
+        half = hidden // 2
+        return array[0, k * half : (k + 1) * half]
+
+    weights = [rows_of(w, k) for w in (gate_weight, up_weight) for k in range(2)]
+    moments = [
+        [rows_of(m, k) for m in (gate_first, up_first, gate_second, up_second)] for k in range(2)
+    ]
     with jax.named_scope("tick_a"):
-        held0 = [weights[0], *spread(weights)]
         partner = fsdp(own, low_swap)
-    partner, held0, own, turned, moments = sync((partner, held0, own, cotangent[0], moments))
-    with jax.named_scope("tick_b"):
-        came0 = exchange(held0)
-        near = [lax.ppermute(moments[j], "member", along_row(j)) for j in (1, 3)]
+        turned = cotangent[0].T
+    partner, turned, own, weights = sync((partner, turned, own, weights))
+    with jax.named_scope("tick_a"):
         start = jnp.concatenate([own, partner])
         up1, down1 = fsdp(start, z_up), fsdp(start, z_down)
-        turned = turned.T.reshape(16, 2 * hidden, count)
-        cots = lax.all_to_all(turned, "fsdp", 0, 0, axis_index_groups=same_core, tiled=True)
-    up1, down1, came0, held0, near, moments = sync((up1, down1, came0, held0, near, moments))
+        held0 = [weights[0], *spread(weights)]
+    up1, down1, held0, turned, moments[0] = sync((up1, down1, held0, turned, moments[0]))
     with jax.named_scope("tick_b"):
         up2, down2 = fsdp(up1, z_up), fsdp(down1, z_down)
-        far = lax.ppermute(moments[2], "member", along_row(2))
-        held1 = [moments[0], near[0], far, near[1]]
-    up2, down2, came0, held0, held1 = sync((up2, down2, came0, held0, held1))
+        came0 = exchange(held0)
+        turned = turned.reshape(16, 2 * hidden, count)
+        cots = lax.all_to_all(turned, "fsdp", 0, 0, axis_index_groups=same_core, tiled=True)
+        held1 = [moments[0][0], *spread(moments[0])]
+    came0, held0, held1, moments[1] = sync((came0, held0, held1, moments[1]))
     with jax.named_scope("tick_c"):
+        got0 = gathered(held0, came0)
+    got0, held1, moments[1] = sync((got0, held1, moments[1]))
+    with jax.named_scope("tick_c"):
+        came1 = exchange(held1)
+        held2 = [moments[1][0], *spread(moments[1])]
+    up2, down2, got0, came1, held1, held2, cots = sync(
+        (up2, down2, got0, came1, held1, held2, cots)
+    )
+    with jax.named_scope("tick_d"):
         up3, down3 = fsdp(up2, z_up), fsdp(down2, z_down)
-        got0 = gathered(held0, came0)
-        came1 = exchange(held1, spans[0])
-    up3, down3, got0, came1, held1, cots = sync((up3, down3, got0, came1, held1, cots))
-    with jax.named_scope("tick_d"):
         mine = pick("place", here, winner, got0).reshape(2, hidden, width)
         theirs = fsdp(mine, core_swap)
-        got1 = columns(held1, came1, spans[0])
-        came2 = exchange(held1, spans[1])
-        sides = [fsdp(up3[:count], z_up), fsdp(down3[count:], z_down)]
+        got1 = columns(held1, came1)
+        came2 = exchange(held2)
         blocks = [start, up1, down1, up2, down2]
         sources = [(d, b) for d in (0, -1, 1, -2, 2) for b in range(2)]
         totals = terms(here, mine, theirs, cots, blocks, sources, None, scale)
-    sides, came2, totals, got1, held1 = sync((sides, came2, totals, got1, held1))
+    up3, down3, came2, totals, got1, held2 = sync((up3, down3, came2, totals, got1, held2))
     with jax.named_scope("tick_e"):
-        got2 = columns(held1, came2, spans[1])
+        sides = [fsdp(up3[:count], z_up), fsdp(down3[count:], z_down)]
+        got2 = columns(held2, came2)
         sources = [(d, b) for d in (-3, 3, 4) for b in range(2)]
         sums = terms(here, mine, theirs, cots, [up3, down3, *sides], sources, totals, scale)
         other = [fsdp(part, core_swap) for part in sums[2:]]
     with jax.named_scope("adam"):
-        new = adam(here, winner, rate, mine, got1, sums[:2], other[0::2], scale, 0, [])
-        return tuple(adam(here, winner, rate, mine, got2, sums[:2], other[1::2], scale, 1, new))
+        return tuple(adam(here, winner, rate, mine, [got1, got2], sums[:2], other, scale))
 
 
 def solution(mesh):

time: 262 us -> 232 us (0.89)
  waiting for transfers between devices: 99 us -> 66.8 us
  local copies, waits for them, and re-layouts: 40.1 us -> 13.6 us
  starting transfers between devices: 59.7 us -> 81.8 us
  Pallas kernels: 59.5 us -> 66 us
    ppermute x6 -> x3, waiting for transfers between devices: 37 us -> 1.69 us  [exchange(): return lax.ppermute(pick('cross', here, winner, held), 'member', row_swap)]
    unnamed x89 -> x49, local copies, waits for them, and re-layouts: 31.6 us -> 4.16 us
    ppermute x6 -> x12, waiting for transfers between devices: 29.3 us -> 52.5 us  [spread(): return [lax.ppermute(pieces[j], 'member', along_row(j)) for j in (1, 2, 3)]]
    ppermute x14, waiting for transfers between devices: 32.6 us -> 12.7 us  [fsdp(): return lax.ppermute(value, 'fsdp', pairs)]
    ppermute x14, starting transfers between devices: 23.6 us -> 38.5 us  [fsdp(): return lax.ppermute(value, 'fsdp', pairs)]
    ppermute x6 -> x12, starting transfers between devices: 7.22 us -> 19.2 us  [spread(): return [lax.ppermute(pieces[j], 'member', along_row(j)) for j in (1, 2, 3)]]
    pallas_call x7, Pallas kernels: 14.2 us -> 19.9 us  [pick(): pl.pallas_call(functools.partial(pick_kernel, mode), in_specs=[smem, smem...]
    transpose x1 -> x0, local copies, waits for them, and re-layouts: 3.88 us -> none  [body(): turned = turned.T.reshape(16, 2 * hidden, count)]
  transfers between devices with their start and end apart: 29 -> 32, of which waited for: 12 -> 17; matrix products, arithmetic and copies ran while one was open for 2% -> 3% of each run, Pallas kernels for 18% -> 22%
where the time goes in v4:
time: 232 us; the launch traced here: 231 us
  starting transfers between devices  81.8 us (35%)
  waiting for transfers between devices  66.8 us (29%)
  Pallas kernels  66 us (28%)
  local copies, waits for them, and re-layouts  13.6 us (6%)
    ppermute x12, waiting for transfers between devices, spread(): return [lax.ppermute(pieces[j], 'member', along_row(j)) for j in (1, 2, 3)]  52.5 us
    ppermute x14, starting transfers between devices, fsdp(): return lax.ppermute(value, 'fsdp', pairs)  38.5 us
    pallas_call x2, Pallas kernels, terms(): pl.pallas_call(kernel, in_specs=[pl.BlockSpec(memory_space=pltpu.SMEM)] +...  33.3 us
    pallas_call x7, Pallas kernels, pick(): pl.pallas_call(functools.partial(pick_kernel, mode), in_specs=[smem, smem...  19.9 us
    ppermute x12, starting transfers between devices, spread(): return [lax.ppermute(pieces[j], 'member', along_row(j)) for j in (1, 2, 3)]  19.2 us
    pallas_call x1, Pallas kernels, adam(): pl.pallas_call(functools.partial(adam_kernel, scale), grid_spec=pltpu.Pre...  12.8 us
    ppermute x14, waiting for transfers between devices, fsdp(): return lax.ppermute(value, 'fsdp', pairs)  12.7 us
    ppermute x3, starting transfers between devices, exchange(): return lax.ppermute(pick('cross', here, winner, held), 'member', row_swap)  10.5 us
  transfers between devices with their start and end apart: 32, of which 17 were waited for; matrix products, arithmetic and copies ran while one was open for 3% of the time, Pallas kernels for 22%

profile of v4, /device:TPU:1, one launch (start us, length us, event | category | flops | bytes accessed | tf_op | source)
XLA Modules:
  0.0 230.7 jit_solution(10382692883034547632)
XLA Ops:
  0.6 2.2 collective-permute-start
  2.9 2.2 slice_bitcast_fusion.8
  5.1 7.1 %collective-permute-done = bf16[128,1792]{1,0:T(8,128)(2,1)S(1)} collective-permute-done((bf16[128,1792]{1,0:T(8,128)(2,1)}, bf16[128,1792]{1,0:T(8,128)(2,1)S(1)}, u32[]{:S(2)}, u32[]{:S(2)}) %collective-permute-start) | collective-permute-done | bytes 458784 | tf_op jit(solution)/shard_map/tick_a/ppermute | solution.py:329
  12.3 2.7 %collective-permute-start.1 = (bf16[256,1792]{1,0:T(8,128)(2,1)S(1)}, bf16[256,1792]{1,0:T(8,128)(2,1)S(1)}, u32[]{:S(2)}, u32[]{:S(2)}) collective-permute-start(bf16[256,1792]{1,0:T(8,128)(2,1)S(1)} %constant_dynamic-update-slice_fusion.refs_0_), channel_id=1, source_target_pairs={{0,4},{1,5},{2,6},{3,7},{4,8},{5,9},{6,10},{7,11},{8,12},{9,13},{1... | collective-permute-start | bytes 2752520 | tf_op jit(solution)/shard_map/tick_a/ppermute | solution.py:329
  15.0 4.0 %collective-permute-start.2 = (bf16[256,1792]{1,0:T(8,128)(2,1)S(1)}, bf16[256,1792]{1,0:T(8,128)(2,1)S(1)}, u32[]{:S(2)}, u32[]{:S(2)}) collective-permute-start(bf16[256,1792]{1,0:T(8,128)(2,1)S(1)} %constant_dynamic-update-slice_fusion.refs_0_), channel_id=1, source_target_pairs={{4,0},{5,1},{6,2},{7,3},{8,4},{9,5},{10,6},{11,7},{12,8},{13,9},{1... | collective-permute-start | bytes 2752520 | tf_op jit(solution)/shard_map/tick_a/ppermute | solution.py:329
  20.1 1.2 collective-permute-start.3
  21.3 2.5 %collective-permute-start.4 = (bf16[112,1792]{1,0:T(8,128)(2,1)S(1)}, bf16[112,1792]{1,0:T(8,128)(2,1)}, u32[]{:S(2)}, u32[]{:S(2)}) collective-permute-start(bf16[112,1792]{1,0:T(8,128)(2,1)S(1)} %get-tuple-element.99), channel_id=1, source_target_pairs={{0,128},{32,160},{64,192},{96,224},{128,0},{160,32},{192,64},{224,... | collective-permute-start | bytes 1204232 | tf_op jit(solution)/shard_map/tick_a/ppermute | solution.py:302
  23.7 1.2 collective-permute-start.5
  25.9 4.4 %collective-permute-done.3.refs_1_ = bf16[112,1792]{1,0:T(8,128)(2,1)} collective-permute-done((bf16[112,1792]{1,0:T(8,128)(2,1)S(1)}, bf16[112,1792]{1,0:T(8,128)(2,1)}, u32[]{:S(2)}, u32[]{:S(2)}) %collective-permute-start.3) | collective-permute-done | bytes 401440 | tf_op jit(solution)/shard_map/tick_a/ppermute | solution.py:302
  30.3 9.6 %collective-permute-done.4.refs_2_ = bf16[112,1792]{1,0:T(8,128)(2,1)} collective-permute-done((bf16[112,1792]{1,0:T(8,128)(2,1)S(1)}, bf16[112,1792]{1,0:T(8,128)(2,1)}, u32[]{:S(2)}, u32[]{:S(2)}) %collective-permute-start.4) | collective-permute-done | bytes 401440 | tf_op jit(solution)/shard_map/tick_a/ppermute | solution.py:302
  42.6 2.3 %copy.16 = bf16[7168,128]{1,0:T(8,128)(2,1)} copy(bf16[7168,128]{0,1:T(8,128)(2,1)S(1)} %bitcast.36) | data formatting | bytes 3670016 | tf_op jit(solution)/shard_map/optimization_barrier | solution.py:364
  44.9 6.3 %all-to-all-start = ((bf16[16,448,128]{2,1,0:T(8,128)(2,1)}), bf16[16,448,128]{2,1,0:T(8,128)(2,1)S(1)}, u32[]{:S(2)}, u32[]{:S(2)}) async-start(bf16[16,448,128]{2,1,0:T(8,128)(2,1)} %bitcast.17), calls=%async_computation | async-start | bytes 3670016 | tf_op jit(solution)/shard_map/tick_b/all_to_all | solution.py:369
  51.9 2.6 %tick_b.1 = bf16[2,112,1792]{2,1,0:T(8,128)(2,1)} custom-call(s32[2]{0:T(128)} %pad_add_fusion.here, s32[8]{0:T(128)} %winner.15, bf16[112,1792]{1,0:T(8,128)(2,1)} %get-tuple-element.112.refs_0_, bf16[112,1792]{1,0:T(8,128)(2,1)} %collective-permute-done.3.refs_1_, bf16[112,1792]{1,0:T(8,128)(2,1)} %collective-permute-done.4.refs_2_, ...), custom_call_target="tpu_custom_call" | custom-call | bytes 1605632 | tf_op jit(solution)/shard_map/tick_b/pallas_call | solution.py:285
  54.6 2.7 %collective-permute-start.8 = (bf16[2,112,1792]{2,1,0:T(8,128)(2,1)}, bf16[2,112,1792]{2,1,0:T(8,128)(2,1)}, u32[]{:S(2)}, u32[]{:S(2)}) collective-permute-start(bf16[2,112,1792]{2,1,0:T(8,128)(2,1)} %tick_b.1), channel_id=1, source_target_pairs={{0,32},{32,0},{64,96},{96,64},{128,160},{160,128},{192,224},{224,1... | collective-permute-start | bytes 2408456 | tf_op jit(solution)/shard_map/tick_b/ppermute | solution.py:332
  57.3 1.8 collective-permute-start.9
  59.1 2.9 %collective-permute-start.10 = (bf16[112,1792]{1,0:T(8,128)(2,1)}, bf16[112,1792]{1,0:T(8,128)(2,1)S(1)}, u32[]{:S(2)}, u32[]{:S(2)}) collective-permute-start(bf16[112,1792]{1,0:T(8,128)(2,1)} %get-tuple-element.110), channel_id=1, source_target_pairs={{0,128},{32,160},{64,192},{96,224},{128,0},{160,32},{192,64},{224,... | collective-permute-start | bytes 1204232 | tf_op jit(solution)/shard_map/tick_b/ppermute | solution.py:302
  62.0 1.4 collective-permute-start.6
  63.3 5.3 %collective-permute-done.9.refs_1_ = bf16[112,1792]{1,0:T(8,128)(2,1)S(1)} collective-permute-done((bf16[112,1792]{1,0:T(8,128)(2,1)}, bf16[112,1792]{1,0:T(8,128)(2,1)S(1)}, u32[]{:S(2)}, u32[]{:S(2)}) %collective-permute-start.9) | collective-permute-done | bytes 401440 | tf_op jit(solution)/shard_map/tick_b/ppermute | solution.py:302
  68.7 10.5 %collective-permute-done.10.refs_2_ = bf16[112,1792]{1,0:T(8,128)(2,1)S(1)} collective-permute-done((bf16[112,1792]{1,0:T(8,128)(2,1)}, bf16[112,1792]{1,0:T(8,128)(2,1)S(1)}, u32[]{:S(2)}, u32[]{:S(2)}) %collective-permute-start.10) | collective-permute-done | bytes 401440 | tf_op jit(solution)/shard_map/tick_b/ppermute | solution.py:302
  79.2 2.9 %tick_c.2 = (bf16[112,1792]{1,0:T(8,128)(2,1)}, bf16[112,1792]{1,0:T(8,128)(2,1)}, bf16[112,1792]{1,0:T(8,128)(2,1)}, bf16[112,1792]{1,0:T(8,128)(2,1)}) custom-call(s32[2]{0:T(128)} %pad_add_fusion.here, s32[8]{0:T(128)} %winner.15, bf16[112,1792]{1,0:T(8,128)(2,1)} %get-tuple-element.112.refs_0_, bf16[112,1792]{1,0:T(8,128)(2,1)} %collective-permute-done.3.refs_1_, ...), custom_call_target="tpu_custom_call" | custom-call | bytes 3211264 | tf_op jit(solution)/shard_map/tick_c/pallas_call | solution.py:285
  82.1 1.7 collective-permute-start.12
  83.8 2.9 %collective-permute-start.13 = (bf16[112,1792]{1,0:T(8,128)(2,1)}, bf16[112,1792]{1,0:T(8,128)(2,1)}, u32[]{:S(2)}, u32[]{:S(2)}) collective-permute-start(bf16[112,1792]{1,0:T(8,128)(2,1)} %get-tuple-element.119), channel_id=1, source_target_pairs={{0,128},{32,160},{64,192},{96,224},{128,0},{160,32},{192,64},{224,... | collective-permute-start | bytes 1204232 | tf_op jit(solution)/shard_map/tick_c/ppermute | solution.py:302
  86.6 9.2 %collective-permute-start.7 = (bf16[256,1792]{1,0:T(8,128)(2,1)}, bf16[256,1792]{1,0:T(8,128)(2,1)}, u32[]{:S(2)}, u32[]{:S(2)}) collective-permute-start(bf16[256,1792]{1,0:T(8,128)(2,1)} %copy-done.22), channel_id=1, source_target_pairs={{4,0},{5,1},{6,2},{7,3},{8,4},{9,5},{10,6},{11,7},{12,8},{13,9},{1... | collective-permute-start | bytes 2752520 | tf_op jit(solution)/shard_map/tick_b/ppermute | solution.py:329
  95.8 3.1 %collective-permute-done.13.refs_2_ = bf16[112,1792]{1,0:T(8,128)(2,1)} collective-permute-done((bf16[112,1792]{1,0:T(8,128)(2,1)}, bf16[112,1792]{1,0:T(8,128)(2,1)}, u32[]{:S(2)}, u32[]{:S(2)}) %collective-permute-start.13) | collective-permute-done | bytes 401440 | tf_op jit(solution)/shard_map/tick_c/ppermute | solution.py:302
  98.9 2.5 %collective-permute-done.14.refs_3_ = bf16[112,1792]{1,0:T(8,128)(2,1)} collective-permute-done((bf16[112,1792]{1,0:T(8,128)(2,1)}, bf16[112,1792]{1,0:T(8,128)(2,1)}, u32[]{:S(2)}, u32[]{:S(2)}) %collective-permute-start.14) | collective-permute-done | bytes 401440 | tf_op jit(solution)/shard_map/tick_c/ppermute | solution.py:302
  101.4 2.6 %tick_c.3 = bf16[2,112,1792]{2,1,0:T(8,128)(2,1)} custom-call(s32[2]{0:T(128)} %pad_add_fusion.here, s32[8]{0:T(128)} %winner.15, bf16[112,1792]{1,0:T(8,128)(2,1)} %get-tuple-element.159.refs_0_, bf16[112,1792]{1,0:T(8,128)(2,1)} %copy-done.4, bf16[112,1792]{1,0:T(8,128)(2,1)} %copy-done.5, bf16[112,1792]{1,0:T(8,128)(2,1)} %copy-done.6), custom_call_target="tpu_custom_call" | custom-call | bytes 1605632 | tf_op jit(solution)/shard_map/tick_c/pallas_call | solution.py:285
  104.1 7.6 %collective-permute-start.15 = (bf16[2,112,1792]{2,1,0:T(8,128)(2,1)}, bf16[2,112,1792]{2,1,0:T(8,128)(2,1)S(1)}, u32[]{:S(2)}, u32[]{:S(2)}) collective-permute-start(bf16[2,112,1792]{2,1,0:T(8,128)(2,1)} %tick_c.3), channel_id=1, source_target_pairs={{0,32},{32,0},{64,96},{96,64},{128,160},{160,128},{192,224},{224,1... | collective-permute-start | bytes 2408456 | tf_op jit(solution)/shard_map/tick_c/ppermute | solution.py:332
  112.2 4.1 %collective-permute-start.17 = (bf16[112,1792]{1,0:T(8,128)(2,1)}, bf16[112,1792]{1,0:T(8,128)(2,1)S(1)}, u32[]{:S(2)}, u32[]{:S(2)}) collective-permute-start(bf16[112,1792]{1,0:T(8,128)(2,1)} %get-tuple-element.139), channel_id=1, source_target_pairs={{0,128},{32,160},{64,192},{96,224},{128,0},{160,32},{192,64},{224,... | collective-permute-start | bytes 1204232 | tf_op jit(solution)/shard_map/tick_c/ppermute | solution.py:302
  116.8 5.4 %collective-permute-done.16.refs_1_ = bf16[112,1792]{1,0:T(8,128)(2,1)S(1)} collective-permute-done((bf16[112,1792]{1,0:T(8,128)(2,1)S(1)}, bf16[112,1792]{1,0:T(8,128)(2,1)S(1)}, u32[]{:S(2)}, u32[]{:S(2)}) %collective-permute-start.16) | collective-permute-done | bytes 401440 | tf_op jit(solution)/shard_map/tick_c/ppermute | solution.py:302
  122.3 10.6 %collective-permute-done.17.refs_2_ = bf16[112,1792]{1,0:T(8,128)(2,1)S(1)} collective-permute-done((bf16[112,1792]{1,0:T(8,128)(2,1)}, bf16[112,1792]{1,0:T(8,128)(2,1)S(1)}, u32[]{:S(2)}, u32[]{:S(2)}) %collective-permute-start.17) | collective-permute-done | bytes 401440 | tf_op jit(solution)/shard_map/tick_c/ppermute | solution.py:302
  134.4 3.1 %tick_d.4 = bf16[4,112,1792]{2,1,0:T(8,128)(2,1)} custom-call(s32[2]{0:T(128)} %pad_add_fusion.here, s32[8]{0:T(128)} %winner.15, bf16[112,1792]{1,0:T(8,128)(2,1)} %get-tuple-element.142.refs_0_, bf16[112,1792]{1,0:T(8,128)(2,1)} %collective-permute-done.12.refs_1_, bf16[112,1792]{1,0:T(8,128)(2,1)} %collective-permute-done.13.refs_2_, ...), custom_call_target="tpu_custom_call" | custom-call | bytes 3211264 | tf_op jit(solution)/shard_map/tick_d/pallas_call | solution.py:285
  137.5 2.3 %collective-permute-start.22 = (bf16[2,224,1792]{2,1,0:T(8,128)(2,1)}, bf16[2,224,1792]{2,1,0:T(8,128)(2,1)}, u32[]{:S(2)}, u32[]{:S(2)}) collective-permute-start(bf16[2,224,1792]{2,1,0:T(8,128)(2,1)} %bitcast.32), channel_id=1, source_target_pairs={{0,1},{1,0},{2,3},{3,2},{4,5},{5,4},{6,7},{7,6},{8,9},{9,8},{10,11... | collective-permute-start | bytes 4816904 | tf_op jit(solution)/shard_map/tick_d/ppermute | solution.py:329
  139.9 3.0 %tick_d.7 = bf16[4,112,1792]{2,1,0:T(8,128)(2,1)} custom-call(s32[2]{0:T(128)} %pad_add_fusion.here, s32[8]{0:T(128)} %winner.15, bf16[112,1792]{1,0:T(8,128)(2,1)} %get-tuple-element.159.refs_0_, bf16[112,1792]{1,0:T(8,128)(2,1)} %copy-done.4, bf16[112,1792]{1,0:T(8,128)(2,1)} %copy-done.5, bf16[112,1792]{1,0:T(8,128)(2,1)} %copy-done.6, ...), custom_call_target="tpu_custom_call" | custom-call | bytes 3211264 | tf_op jit(solution)/shard_map/tick_d/pallas_call | solution.py:285
  142.9 3.6 %all-to-all-start.1 = ((bf16[4,112,1792]{2,1,0:T(8,128)(2,1)}), bf16[4,112,1792]{2,1,0:T(8,128)(2,1)S(1)}, u32[]{:S(2)}, u32[]{:S(2)}) async-start(bf16[4,112,1792]{2,1,0:T(8,128)(2,1)} %tick_d.7), calls=%async_computation.1 | async-start | bytes 3211264 | tf_op jit(solution)/shard_map/tick_d/all_to_all | solution.py:339
  146.5 7.4 %collective-permute-start.19 = (bf16[256,1792]{1,0:T(8,128)(2,1)}, bf16[256,1792]{1,0:T(8,128)(2,1)S(1)}, u32[]{:S(2)}, u32[]{:S(2)}) collective-permute-start(bf16[256,1792]{1,0:T(8,128)(2,1)} %collective-permute-done.6.refs_3_), channel_id=1, source_target_pairs={{0,4},{1,5},{2,6},{3,7},{4,8},{5,9},{6,10},{7,11},{8,12},{9,13},{1... | collective-permute-start | bytes 2752520 | tf_op jit(solution)/shard_map/tick_d/ppermute | solution.py:329
  153.9 3.4 %collective-permute-start.20 = (bf16[256,1792]{1,0:T(8,128)(2,1)}, bf16[256,1792]{1,0:T(8,128)(2,1)}, u32[]{:S(2)}, u32[]{:S(2)}) collective-permute-start(bf16[256,1792]{1,0:T(8,128)(2,1)} %collective-permute-done.7.refs_4_), channel_id=1, source_target_pairs={{4,0},{5,1},{6,2},{7,3},{8,4},{9,5},{10,6},{11,7},{12,8},{13,9},{1... | collective-permute-start | bytes 2752520 | tf_op jit(solution)/shard_map/tick_d/ppermute | solution.py:329
  157.3 2.6 %tick_d.5 = bf16[2,112,1792]{2,1,0:T(8,128)(2,1)} custom-call(s32[2]{0:T(128)} %pad_add_fusion.here, s32[8]{0:T(128)} %winner.15, bf16[112,1792]{1,0:T(8,128)(2,1)} %get-tuple-element.165.refs_0_, bf16[112,1792]{1,0:T(8,128)(2,1)} %copy-done.7, bf16[112,1792]{1,0:T(8,128)(2,1)} %copy-done.8, bf16[112,1792]{1,0:T(8,128)(2,1)} %copy-done.9), custom_call_target="tpu_custom_call" | custom-call | bytes 1605632 | tf_op jit(solution)/shard_map/tick_d/pallas_call | solution.py:285
  160.1 19.1 %tick_d.6 = (f32[224,1792]{1,0:T(8,128)}, f32[224,1792]{1,0:T(8,128)}, f32[112,1792]{1,0:T(8,128)}, f32[112,1792]{1,0:T(8,128)}, f32[112,1792]{1,0:T(8,128)}, /*index=5*/f32[112,1792]{1,0:T(8,128)}) custom-call(s32[2]{0:T(128)} %pad_add_fusion.here, bf16[2,224,1792]{2,1,0:T(8,128)(2,1)} %bitcast.33, bf16[2,224,1792]{2,1,0:T(8,128)(2,1)} %collective-permute-done.22.theirs, ...), custom_call_target="tpu_custom_call" | custom-call | flops 8220835840 | bytes 20971520 | tf_op jit(solution)/shard_map/tick_d/pallas_call | solution.py:137
  179.2 1.7 collective-permute-done.21.refs_4_
  181.9 1.2 slice.54
  184.2 2.7 %collective-permute-start.24 = (bf16[128,1792]{1,0:T(8,128)(2,1)S(1)}, bf16[128,1792]{1,0:T(8,128)(2,1)}, u32[]{:S(2)}, u32[]{:S(2)}) collective-permute-start(bf16[128,1792]{1,0:T(8,128)(2,1)S(1)} %slice.55), channel_id=1, source_target_pairs={{4,0},{5,1},{6,2},{7,3},{8,4},{9,5},{10,6},{11,7},{12,8},{13,9},{1... | collective-permute-start | bytes 1376264 | tf_op jit(solution)/shard_map/tick_e/ppermute | solution.py:329
  187.0 2.9 %tick_e.2 = bf16[4,112,1792]{2,1,0:T(8,128)(2,1)} custom-call(s32[2]{0:T(128)} %pad_add_fusion.here, s32[8]{0:T(128)} %winner.15, bf16[112,1792]{1,0:T(8,128)(2,1)} %get-tuple-element.165.refs_0_, bf16[112,1792]{1,0:T(8,128)(2,1)} %copy-done.7, bf16[112,1792]{1,0:T(8,128)(2,1)} %copy-done.8, bf16[112,1792]{1,0:T(8,128)(2,1)} %copy-done.9, ...), custom_call_target="tpu_custom_call" | custom-call | bytes 3211264 | tf_op jit(solution)/shard_map/tick_e/pallas_call | solution.py:285
  189.9 3.7 %all-to-all-start.2 = ((bf16[4,112,1792]{2,1,0:T(8,128)(2,1)}), bf16[4,112,1792]{2,1,0:T(8,128)(2,1)S(1)}, u32[]{:S(2)}, u32[]{:S(2)}) async-start(bf16[4,112,1792]{2,1,0:T(8,128)(2,1)} %tick_e.2), calls=%async_computation.2 | async-start | bytes 3211264 | tf_op jit(solution)/shard_map/tick_e/all_to_all | solution.py:339
  193.7 1.7 collective-permute-done.23.refs_2_
  195.4 14.2 %tick_e.3 = (f32[224,1792]{1,0:T(8,128)}, f32[224,1792]{1,0:T(8,128)}, f32[112,1792]{1,0:T(8,128)}, f32[112,1792]{1,0:T(8,128)}, f32[112,1792]{1,0:T(8,128)}, /*index=5*/f32[112,1792]{1,0:T(8,128)}) custom-call(s32[2]{0:T(128)} %pad_add_fusion.here, bf16[2,224,1792]{2,1,0:T(8,128)(2,1)} %bitcast.34, bf16[2,224,1792]{2,1,0:T(8,128)(2,1)} %collective-permute-done.22.theirs, ...), custom_call_target="tpu_custom_call" | custom-call | flops 4932501504 | bytes 20971520 | tf_op jit(solution)/shard_map/tick_e/pallas_call | solution.py:137
  209.6 2.4 %collective-permute-start.25 = (f32[112,1792]{1,0:T(8,128)}, f32[112,1792]{1,0:T(8,128)S(1)}, u32[]{:S(2)}, u32[]{:S(2)}) collective-permute-start(f32[112,1792]{1,0:T(8,128)} %get-tuple-element.180), channel_id=1, source_target_pairs={{0,1},{1,0},{2,3},{3,2},{4,5},{5,4},{6,7},{7,6},{8,9},{9,8},{10,11... | collective-permute-start | bytes 2408456 | tf_op jit(solution)/shard_map/tick_e/ppermute | solution.py:329
  214.2 2.3 collective-permute-done.26.refs_5_
  217.7 12.8 %adam.1 = (bf16[1,224,1792]{2,1,0:T(8,128)(2,1)}, bf16[1,224,1792]{2,1,0:T(8,128)(2,1)}, bf16[1,224,1792]{2,1,0:T(8,128)(2,1)}, bf16[1,224,1792]{2,1,0:T(8,128)(...) custom-call(s32[2]{0:T(128)} %pad_add_fusion.here, s32[8]{0:T(128)} %winner.15, ...), custom_call_target="tpu_custom_call" | custom-call | tf_op jit(solution)/shard_map/adam/pallas_call | solution.py:208
  (84 shorter events, 13.1 us)
Async XLA Ops:
  0.6 11.5 %copy-start.18 = (bf16[1,128,1792]{2,1,0:T(8,128)(2,1)S(1)}, bf16[1,128,1792]{2,1,0:T(8,128)(2,1)}, u32[]{:S(2)}) copy-start(bf16[1,128,1792]{2,1,0:T(8,128)(2,1)} %param.10) | copy-start | bytes 1376260
  0.6 11.5 %collective-permute-start = (bf16[128,1792]{1,0:T(8,128)(2,1)}, bf16[128,1792]{1,0:T(8,128)(2,1)S(1)}, u32[]{:S(2)}, u32[]{:S(2)}) collective-permute-start(bf16[128,1792]{1,0:T(8,128)(2,1)} %bitcast.37), channel_id=1, source_target_pairs={{0,2},{1,3},{2,0},{3,1},{4,6},{5,7},{6,4},{7,5},{8,10},{9,11},{10,... | collective-permute-start | bytes 1376264 | tf_op jit(solution)/shard_map/tick_a/ppermute | solution.py:329
  5.1 13.9 %copy-start.12 = (bf16[1,224,1792]{2,1,0:T(8,128)(2,1)S(1)}, bf16[1,224,1792]{2,1,0:T(8,128)(2,1)}, u32[]{:S(2)}) copy-start(bf16[1,224,1792]{2,1,0:T(8,128)(2,1)} %param.15) | copy-start | bytes 2408452
  5.1 13.9 %copy-start.13 = (bf16[1,224,1792]{2,1,0:T(8,128)(2,1)S(1)}, bf16[1,224,1792]{2,1,0:T(8,128)(2,1)}, u32[]{:S(2)}) copy-start(bf16[1,224,1792]{2,1,0:T(8,128)(2,1)} %param.14) | copy-start | bytes 2408452
  12.2 7.8 %copy-start.20 = (bf16[256,1792]{1,0:T(8,128)(2,1)}, bf16[256,1792]{1,0:T(8,128)(2,1)S(1)}, u32[]{:S(2)}) copy-start(bf16[256,1792]{1,0:T(8,128)(2,1)S(1)} %constant_dynamic-update-slice_fusion.refs_0_) | copy-start | bytes 2752516
  12.3 12.6 %copy-start.14 = (bf16[1,224,1792]{2,1,0:T(8,128)(2,1)S(1)}, bf16[1,224,1792]{2,1,0:T(8,128)(2,1)}, u32[]{:S(2)}) copy-start(bf16[1,224,1792]{2,1,0:T(8,128)(2,1)} %param.17) | copy-start | bytes 2408452
  12.3 12.6 %copy-start.15 = (bf16[1,224,1792]{2,1,0:T(8,128)(2,1)S(1)}, bf16[1,224,1792]{2,1,0:T(8,128)(2,1)}, u32[]{:S(2)}) copy-start(bf16[1,224,1792]{2,1,0:T(8,128)(2,1)} %param.16) | copy-start | bytes 2408452
  12.3 28.4 %collective-permute-start.1 = (bf16[256,1792]{1,0:T(8,128)(2,1)S(1)}, bf16[256,1792]{1,0:T(8,128)(2,1)S(1)}, u32[]{:S(2)}, u32[]{:S(2)}) collective-permute-start(bf16[256,1792]{1,0:T(8,128)(2,1)S(1)} %constant_dynamic-update-slice_fusion.refs_0_), channel_id=1, source_target_pairs={{0,4},{1,5},{2,6},{3,7},{4,8},{5,9},{6,10},{7,11},{8,12},{9,13},{1... | collective-permute-start | bytes 2752520 | tf_op jit(solution)/shard_map/tick_a/ppermute | solution.py:329
  15.0 25.7 %collective-permute-start.2 = (bf16[256,1792]{1,0:T(8,128)(2,1)S(1)}, bf16[256,1792]{1,0:T(8,128)(2,1)S(1)}, u32[]{:S(2)}, u32[]{:S(2)}) collective-permute-start(bf16[256,1792]{1,0:T(8,128)(2,1)S(1)} %constant_dynamic-update-slice_fusion.refs_0_), channel_id=1, source_target_pairs={{4,0},{5,1},{6,2},{7,3},{8,4},{9,5},{10,6},{11,7},{12,8},{13,9},{1... | collective-permute-start | bytes 2752520 | tf_op jit(solution)/shard_map/tick_a/ppermute | solution.py:329
  20.0 22.6 %copy-start.2 = (bf16[1,128,7168]{2,1,0:T(8,128)(2,1)S(1)}, bf16[1,128,7168]{2,1,0:T(8,128)(2,1)}, u32[]{:S(2)}) copy-start(bf16[1,128,7168]{2,1,0:T(8,128)(2,1)} %param.11) | copy-start | bytes 5505028
  20.1 10.3 %collective-permute-start.3 = (bf16[112,1792]{1,0:T(8,128)(2,1)S(1)}, bf16[112,1792]{1,0:T(8,128)(2,1)}, u32[]{:S(2)}, u32[]{:S(2)}) collective-permute-start(bf16[112,1792]{1,0:T(8,128)(2,1)S(1)} %get-tuple-element.98), channel_id=1, source_target_pairs={{0,64},{32,96},{64,128},{96,160},{128,192},{160,224},{192,0},{224,... | collective-permute-start | bytes 1204232 | tf_op jit(solution)/shard_map/tick_a/ppermute | solution.py:302
  21.3 18.6 %collective-permute-start.4 = (bf16[112,1792]{1,0:T(8,128)(2,1)S(1)}, bf16[112,1792]{1,0:T(8,128)(2,1)}, u32[]{:S(2)}, u32[]{:S(2)}) collective-permute-start(bf16[112,1792]{1,0:T(8,128)(2,1)S(1)} %get-tuple-element.99), channel_id=1, source_target_pairs={{0,128},{32,160},{64,192},{96,224},{128,0},{160,32},{192,64},{224,... | collective-permute-start | bytes 1204232 | tf_op jit(solution)/shard_map/tick_a/ppermute | solution.py:302
  23.7 16.9 %collective-permute-start.5 = (bf16[112,1792]{1,0:T(8,128)(2,1)S(1)}, bf16[112,1792]{1,0:T(8,128)(2,1)}, u32[]{:S(2)}, u32[]{:S(2)}) collective-permute-start(bf16[112,1792]{1,0:T(8,128)(2,1)S(1)} %get-tuple-element.100), channel_id=1, source_target_pairs={{0,192},{32,224},{64,0},{96,32},{128,64},{160,96},{192,128},{224,1... | collective-permute-start | bytes 1204232 | tf_op jit(solution)/shard_map/tick_a/ppermute | solution.py:302
  44.9 89.5 %all-to-all-start = ((bf16[16,448,128]{2,1,0:T(8,128)(2,1)}), bf16[16,448,128]{2,1,0:T(8,128)(2,1)S(1)}, u32[]{:S(2)}, u32[]{:S(2)}) async-start(bf16[16,448,128]{2,1,0:T(8,128)(2,1)} %bitcast.17), calls=%async_computation | async-start | bytes 3670016 | tf_op jit(solution)/shard_map/tick_b/all_to_all | solution.py:369
  54.6 24.6 %collective-permute-start.8 = (bf16[2,112,1792]{2,1,0:T(8,128)(2,1)}, bf16[2,112,1792]{2,1,0:T(8,128)(2,1)}, u32[]{:S(2)}, u32[]{:S(2)}) collective-permute-start(bf16[2,112,1792]{2,1,0:T(8,128)(2,1)} %tick_b.1), channel_id=1, source_target_pairs={{0,32},{32,0},{64,96},{96,64},{128,160},{160,128},{192,224},{224,1... | collective-permute-start | bytes 2408456 | tf_op jit(solution)/shard_map/tick_b/ppermute | solution.py:332
  57.3 11.4 %collective-permute-start.9 = (bf16[112,1792]{1,0:T(8,128)(2,1)}, bf16[112,1792]{1,0:T(8,128)(2,1)S(1)}, u32[]{:S(2)}, u32[]{:S(2)}) collective-permute-start(bf16[112,1792]{1,0:T(8,128)(2,1)} %get-tuple-element.109), channel_id=1, source_target_pairs={{0,64},{32,96},{64,128},{96,160},{128,192},{160,224},{192,0},{224,... | collective-permute-start | bytes 1204232 | tf_op jit(solution)/shard_map/tick_b/ppermute | solution.py:302
  59.1 20.0 %collective-permute-start.10 = (bf16[112,1792]{1,0:T(8,128)(2,1)}, bf16[112,1792]{1,0:T(8,128)(2,1)S(1)}, u32[]{:S(2)}, u32[]{:S(2)}) collective-permute-start(bf16[112,1792]{1,0:T(8,128)(2,1)} %get-tuple-element.110), channel_id=1, source_target_pairs={{0,128},{32,160},{64,192},{96,224},{128,0},{160,32},{192,64},{224,... | collective-permute-start | bytes 1204232 | tf_op jit(solution)/shard_map/tick_b/ppermute | solution.py:302
  62.0 17.2 %collective-permute-start.11 = (bf16[112,1792]{1,0:T(8,128)(2,1)}, bf16[112,1792]{1,0:T(8,128)(2,1)S(1)}, u32[]{:S(2)}, u32[]{:S(2)}) collective-permute-start(bf16[112,1792]{1,0:T(8,128)(2,1)} %get-tuple-element.111), channel_id=1, source_target_pairs={{0,192},{32,224},{64,0},{96,32},{128,64},{160,96},{192,128},{224,1... | collective-permute-start | bytes 1204232 | tf_op jit(solution)/shard_map/tick_b/ppermute | solution.py:302
  62.0 54.3 %collective-permute-start.6 = (bf16[256,1792]{1,0:T(8,128)(2,1)}, bf16[256,1792]{1,0:T(8,128)(2,1)}, u32[]{:S(2)}, u32[]{:S(2)}) collective-permute-start(bf16[256,1792]{1,0:T(8,128)(2,1)} %copy-done.21), channel_id=1, source_target_pairs={{0,4},{1,5},{2,6},{3,7},{4,8},{5,9},{6,10},{7,11},{8,12},{9,13},{1... | collective-permute-start | bytes 2752520 | tf_op jit(solution)/shard_map/tick_b/ppermute | solution.py:329
  68.7 32.7 %copy-start.4 = (bf16[112,1792]{1,0:T(8,128)(2,1)}, bf16[112,1792]{1,0:T(8,128)(2,1)S(1)}, u32[]{:S(2)}) copy-start(bf16[112,1792]{1,0:T(8,128)(2,1)S(1)} %collective-permute-done.9.refs_1_) | copy-start | bytes 1204228
  79.2 22.2 %copy-start.5 = (bf16[112,1792]{1,0:T(8,128)(2,1)}, bf16[112,1792]{1,0:T(8,128)(2,1)S(1)}, u32[]{:S(2)}) copy-start(bf16[112,1792]{1,0:T(8,128)(2,1)S(1)} %collective-permute-done.10.refs_2_) | copy-start | bytes 1204228
  79.2 22.2 %copy-start.6 = (bf16[112,1792]{1,0:T(8,128)(2,1)}, bf16[112,1792]{1,0:T(8,128)(2,1)S(1)}, u32[]{:S(2)}) copy-start(bf16[112,1792]{1,0:T(8,128)(2,1)S(1)} %collective-permute-done.11.refs_3_) | copy-start | bytes 1204228
  82.1 13.7 %collective-permute-start.12 = (bf16[112,1792]{1,0:T(8,128)(2,1)}, bf16[112,1792]{1,0:T(8,128)(2,1)}, u32[]{:S(2)}, u32[]{:S(2)}) collective-permute-start(bf16[112,1792]{1,0:T(8,128)(2,1)} %get-tuple-element.118), channel_id=1, source_target_pairs={{0,64},{32,96},{64,128},{96,160},{128,192},{160,224},{192,0},{224,... | collective-permute-start | bytes 1204232 | tf_op jit(solution)/shard_map/tick_c/ppermute | solution.py:302
  83.8 15.1 %collective-permute-start.13 = (bf16[112,1792]{1,0:T(8,128)(2,1)}, bf16[112,1792]{1,0:T(8,128)(2,1)}, u32[]{:S(2)}, u32[]{:S(2)}) collective-permute-start(bf16[112,1792]{1,0:T(8,128)(2,1)} %get-tuple-element.119), channel_id=1, source_target_pairs={{0,128},{32,160},{64,192},{96,224},{128,0},{160,32},{192,64},{224,... | collective-permute-start | bytes 1204232 | tf_op jit(solution)/shard_map/tick_c/ppermute | solution.py:302
  86.6 14.8 %collective-permute-start.14 = (bf16[112,1792]{1,0:T(8,128)(2,1)}, bf16[112,1792]{1,0:T(8,128)(2,1)}, u32[]{:S(2)}, u32[]{:S(2)}) collective-permute-start(bf16[112,1792]{1,0:T(8,128)(2,1)} %get-tuple-element.120), channel_id=1, source_target_pairs={{0,192},{32,224},{64,0},{96,32},{128,64},{160,96},{192,128},{224,1... | collective-permute-start | bytes 1204232 | tf_op jit(solution)/shard_map/tick_c/ppermute | solution.py:302
  86.6 30.2 %collective-permute-start.7 = (bf16[256,1792]{1,0:T(8,128)(2,1)}, bf16[256,1792]{1,0:T(8,128)(2,1)}, u32[]{:S(2)}, u32[]{:S(2)}) collective-permute-start(bf16[256,1792]{1,0:T(8,128)(2,1)} %copy-done.22), channel_id=1, source_target_pairs={{4,0},{5,1},{6,2},{7,3},{8,4},{9,5},{10,6},{11,7},{12,8},{13,9},{1... | collective-permute-start | bytes 2752520 | tf_op jit(solution)/shard_map/tick_b/ppermute | solution.py:329
  104.1 30.3 %collective-permute-start.15 = (bf16[2,112,1792]{2,1,0:T(8,128)(2,1)}, bf16[2,112,1792]{2,1,0:T(8,128)(2,1)S(1)}, u32[]{:S(2)}, u32[]{:S(2)}) collective-permute-start(bf16[2,112,1792]{2,1,0:T(8,128)(2,1)} %tick_c.3), channel_id=1, source_target_pairs={{0,32},{32,0},{64,96},{96,64},{128,160},{160,128},{192,224},{224,1... | collective-permute-start | bytes 2408456 | tf_op jit(solution)/shard_map/tick_c/ppermute | solution.py:332
  111.7 10.6 %collective-permute-start.16 = (bf16[112,1792]{1,0:T(8,128)(2,1)S(1)}, bf16[112,1792]{1,0:T(8,128)(2,1)S(1)}, u32[]{:S(2)}, u32[]{:S(2)}) collective-permute-start(bf16[112,1792]{1,0:T(8,128)(2,1)S(1)} %get-tuple-element.138), channel_id=1, source_target_pairs={{0,64},{32,96},{64,128},{96,160},{128,192},{160,224},{192,0},{224,... | collective-permute-start | bytes 1204232 | tf_op jit(solution)/shard_map/tick_c/ppermute | solution.py:302
  112.2 20.7 %collective-permute-start.17 = (bf16[112,1792]{1,0:T(8,128)(2,1)}, bf16[112,1792]{1,0:T(8,128)(2,1)S(1)}, u32[]{:S(2)}, u32[]{:S(2)}) collective-permute-start(bf16[112,1792]{1,0:T(8,128)(2,1)} %get-tuple-element.139), channel_id=1, source_target_pairs={{0,128},{32,160},{64,192},{96,224},{128,0},{160,32},{192,64},{224,... | collective-permute-start | bytes 1204232 | tf_op jit(solution)/shard_map/tick_c/ppermute | solution.py:302
  116.3 16.9 %collective-permute-start.18 = (bf16[112,1792]{1,0:T(8,128)(2,1)S(1)}, bf16[112,1792]{1,0:T(8,128)(2,1)S(1)}, u32[]{:S(2)}, u32[]{:S(2)}) collective-permute-start(bf16[112,1792]{1,0:T(8,128)(2,1)S(1)} %get-tuple-element.140), channel_id=1, source_target_pairs={{0,192},{32,224},{64,0},{96,32},{128,64},{160,96},{192,128},{224,1... | collective-permute-start | bytes 1204232 | tf_op jit(solution)/shard_map/tick_c/ppermute | solution.py:302
  122.3 10.9 %copy-start.7 = (bf16[112,1792]{1,0:T(8,128)(2,1)}, bf16[112,1792]{1,0:T(8,128)(2,1)S(1)}, u32[]{:S(2)}) copy-start(bf16[112,1792]{1,0:T(8,128)(2,1)S(1)} %collective-permute-done.16.refs_1_) | copy-start | bytes 1204228
  137.5 22.6 %collective-permute-start.22 = (bf16[2,224,1792]{2,1,0:T(8,128)(2,1)}, bf16[2,224,1792]{2,1,0:T(8,128)(2,1)}, u32[]{:S(2)}, u32[]{:S(2)}) collective-permute-start(bf16[2,224,1792]{2,1,0:T(8,128)(2,1)} %bitcast.32), channel_id=1, source_target_pairs={{0,1},{1,0},{2,3},{3,2},{4,5},{5,4},{6,7},{7,6},{8,9},{9,8},{10,11... | collective-permute-start | bytes 4816904 | tf_op jit(solution)/shard_map/tick_d/ppermute | solution.py:329
  142.9 38.1 %all-to-all-start.1 = ((bf16[4,112,1792]{2,1,0:T(8,128)(2,1)}), bf16[4,112,1792]{2,1,0:T(8,128)(2,1)S(1)}, u32[]{:S(2)}, u32[]{:S(2)}) async-start(bf16[4,112,1792]{2,1,0:T(8,128)(2,1)} %tick_d.7), calls=%async_computation.1 | async-start | bytes 3211264 | tf_op jit(solution)/shard_map/tick_d/all_to_all | solution.py:339
  146.5 34.5 %collective-permute-start.19 = (bf16[256,1792]{1,0:T(8,128)(2,1)}, bf16[256,1792]{1,0:T(8,128)(2,1)S(1)}, u32[]{:S(2)}, u32[]{:S(2)}) collective-permute-start(bf16[256,1792]{1,0:T(8,128)(2,1)} %collective-permute-done.6.refs_3_), channel_id=1, source_target_pairs={{0,4},{1,5},{2,6},{3,7},{4,8},{5,9},{6,10},{7,11},{8,12},{9,13},{1... | collective-permute-start | bytes 2752520 | tf_op jit(solution)/shard_map/tick_d/ppermute | solution.py:329
  153.9 27.1 %collective-permute-start.20 = (bf16[256,1792]{1,0:T(8,128)(2,1)}, bf16[256,1792]{1,0:T(8,128)(2,1)}, u32[]{:S(2)}, u32[]{:S(2)}) collective-permute-start(bf16[256,1792]{1,0:T(8,128)(2,1)} %collective-permute-done.7.refs_4_), channel_id=1, source_target_pairs={{4,0},{5,1},{6,2},{7,3},{8,4},{9,5},{10,6},{11,7},{12,8},{13,9},{1... | collective-permute-start | bytes 2752520 | tf_op jit(solution)/shard_map/tick_d/ppermute | solution.py:329
  159.9 21.0 %collective-permute-start.21 = (bf16[2,112,1792]{2,1,0:T(8,128)(2,1)}, bf16[2,112,1792]{2,1,0:T(8,128)(2,1)S(1)}, u32[]{:S(2)}, u32[]{:S(2)}) collective-permute-start(bf16[2,112,1792]{2,1,0:T(8,128)(2,1)} %tick_d.5), channel_id=1, source_target_pairs={{0,32},{32,0},{64,96},{96,64},{128,160},{160,128},{192,224},{224,1... | collective-permute-start | bytes 2408456 | tf_op jit(solution)/shard_map/tick_d/ppermute | solution.py:332
  180.9 6.1 %copy-start.17 = (bf16[2,112,1792]{2,1,0:T(8,128)(2,1)}, bf16[2,112,1792]{2,1,0:T(8,128)(2,1)S(1)}, u32[]{:S(2)}) copy-start(bf16[2,112,1792]{2,1,0:T(8,128)(2,1)S(1)} %collective-permute-done.21.refs_4_) | copy-start | bytes 2408452
  180.9 9.0 %copy-start = (bf16[4,112,1792]{2,1,0:T(8,128)(2,1)}, bf16[4,112,1792]{2,1,0:T(8,128)(2,1)S(1)}, u32[]{:S(2)}) copy-start(bf16[4,112,1792]{2,1,0:T(8,128)(2,1)S(1)} %all-to-all-done.1.refs_0_) | copy-start | bytes 4816900
  183.1 12.3 %collective-permute-start.23 = (bf16[128,1792]{1,0:T(8,128)(2,1)S(1)}, bf16[128,1792]{1,0:T(8,128)(2,1)}, u32[]{:S(2)}, u32[]{:S(2)}) collective-permute-start(bf16[128,1792]{1,0:T(8,128)(2,1)S(1)} %slice.54), channel_id=1, source_target_pairs={{0,4},{1,5},{2,6},{3,7},{4,8},{5,9},{6,10},{7,11},{8,12},{9,13},{1... | collective-permute-start | bytes 1376264 | tf_op jit(solution)/shard_map/tick_e/ppermute | solution.py:329
  184.2 11.2 %collective-permute-start.24 = (bf16[128,1792]{1,0:T(8,128)(2,1)S(1)}, bf16[128,1792]{1,0:T(8,128)(2,1)}, u32[]{:S(2)}, u32[]{:S(2)}) collective-permute-start(bf16[128,1792]{1,0:T(8,128)(2,1)S(1)} %slice.55), channel_id=1, source_target_pairs={{4,0},{5,1},{6,2},{7,3},{8,4},{9,5},{10,6},{11,7},{12,8},{13,9},{1... | collective-permute-start | bytes 1376264 | tf_op jit(solution)/shard_map/tick_e/ppermute | solution.py:329
  189.9 24.0 %all-to-all-start.2 = ((bf16[4,112,1792]{2,1,0:T(8,128)(2,1)}), bf16[4,112,1792]{2,1,0:T(8,128)(2,1)S(1)}, u32[]{:S(2)}, u32[]{:S(2)}) async-start(bf16[4,112,1792]{2,1,0:T(8,128)(2,1)} %tick_e.2), calls=%async_computation.2 | async-start | bytes 3211264 | tf_op jit(solution)/shard_map/tick_e/all_to_all | solution.py:339
  193.7 19.0 %copy-start.23 = (s32[8]{0:T(128)S(1)}, s32[8]{0:T(128)}, u32[]{:S(2)}) copy-start(s32[8]{0:T(128)} %param.19) | copy-start | bytes 100
  209.6 4.5 %collective-permute-start.25 = (f32[112,1792]{1,0:T(8,128)}, f32[112,1792]{1,0:T(8,128)S(1)}, u32[]{:S(2)}, u32[]{:S(2)}) collective-permute-start(f32[112,1792]{1,0:T(8,128)} %get-tuple-element.180), channel_id=1, source_target_pairs={{0,1},{1,0},{2,3},{3,2},{4,5},{5,4},{6,7},{7,6},{8,9},{9,8},{10,11... | collective-permute-start | bytes 2408456 | tf_op jit(solution)/shard_map/tick_e/ppermute | solution.py:329
  212.0 4.4 %collective-permute-start.26 = (f32[112,1792]{1,0:T(8,128)}, f32[112,1792]{1,0:T(8,128)S(1)}, u32[]{:S(2)}, u32[]{:S(2)}) collective-permute-start(f32[112,1792]{1,0:T(8,128)} %get-tuple-element.181), channel_id=1, source_target_pairs={{0,1},{1,0},{2,3},{3,2},{4,5},{5,4},{6,7},{7,6},{8,9},{9,8},{10,11... | collective-permute-start | bytes 2408456 | tf_op jit(solution)/shard_map/tick_e/ppermute | solution.py:329
  212.1 4.5 %collective-permute-start.27 = (f32[112,1792]{1,0:T(8,128)}, f32[112,1792]{1,0:T(8,128)}, u32[]{:S(2)}, u32[]{:S(2)}) collective-permute-start(f32[112,1792]{1,0:T(8,128)} %get-tuple-element.182), channel_id=1, source_target_pairs={{0,1},{1,0},{2,3},{3,2},{4,5},{5,4},{6,7},{7,6},{8,9},{9,8},{10,11... | collective-permute-start | bytes 2408456 | tf_op jit(solution)/shard_map/tick_e/ppermute | solution.py:329
  212.5 5.2 %collective-permute-start.28 = (f32[112,1792]{1,0:T(8,128)}, f32[112,1792]{1,0:T(8,128)}, u32[]{:S(2)}, u32[]{:S(2)}) collective-permute-start(f32[112,1792]{1,0:T(8,128)} %get-tuple-element.183), channel_id=1, source_target_pairs={{0,1},{1,0},{2,3},{3,2},{4,5},{5,4},{6,7},{7,6},{8,9},{9,8},{10,11... | collective-permute-start | bytes 2408456 | tf_op jit(solution)/shard_map/tick_e/ppermute | solution.py:329
  213.9 3.8 %copy-start.1 = (bf16[4,112,1792]{2,1,0:T(8,128)(2,1)}, bf16[4,112,1792]{2,1,0:T(8,128)(2,1)S(1)}, u32[]{:S(2)}) copy-start(bf16[4,112,1792]{2,1,0:T(8,128)(2,1)S(1)} %all-to-all-done.2.refs_1_) | copy-start | bytes 4816900
  214.2 3.6 %copy-start.10 = (f32[112,1792]{1,0:T(8,128)}, f32[112,1792]{1,0:T(8,128)S(1)}, u32[]{:S(2)}) copy-start(f32[112,1792]{1,0:T(8,128)S(1)} %collective-permute-done.25.refs_4_) | copy-start | bytes 2408452
  (8 other events, 12.1 us)

commit v5 on v3

--- a/solution.py
+++ b/solution.py
@@ -58,7 +58,7 @@
     keep, send = refs[:2], refs[2:6]
     x, c, w, grad, cot, sems = refs[6:]
     rows, hidden = mine.shape[1], 2 * mine.shape[1]
-    half = rows // 2
+    half = mine.shape[2] // 2
     me = here[1]
     z, low, core = me // 4, (me // 2) % 2, me % 2
     mine_at = pl.multiple_of(core * rows, 32)
@@ -79,8 +79,8 @@
         for p in range(2):
             pairs.append((kept[p], grad.at[pl.ds(p * hidden + mine_at, rows)]))
             for h in range(2):
-                to = p * hidden + theirs_at + h * half
-                pairs.append((sent[2 * p + h], grad.at[pl.ds(to, half)]))
+                to = (pl.ds(p * hidden + theirs_at, rows), pl.ds(h * half, half))
+                pairs.append((sent[2 * p + h], grad.at[to]))
     copies = [pltpu.make_async_copy(a, b, sems.at[k]) for k, (a, b) in enumerate(pairs)]
     for copy in copies:
         copy.start()
@@ -117,8 +117,8 @@
     outs = []
     for p in range(2):
         for h in range(2):
-            to = p * hidden + theirs_at + h * half
-            outs.append((grad.at[pl.ds(to, half)], send[2 * p + h]))
+            to = (pl.ds(p * hidden + theirs_at, rows), pl.ds(h * half, half))
+            outs.append((grad.at[to], send[2 * p + h]))
         outs.append((grad.at[pl.ds(p * hidden + mine_at, rows)], keep[p]))
     launch([pltpu.make_async_copy(a, b, sems.at[k]) for k, (a, b) in enumerate(outs)])
 
@@ -130,7 +130,7 @@
     anywhere = pl.BlockSpec(memory_space=pl.ANY)
     args = [mine, theirs, cots, *blocks, *([] if first else totals)]
     sums = jax.ShapeDtypeStruct((rows, width), jnp.float32)
-    parts = jax.ShapeDtypeStruct((rows // 2, width), jnp.float32)
+    parts = jax.ShapeDtypeStruct((rows, width // 2), jnp.float32)
     kernel = functools.partial(
         terms_kernel, tuple(b.shape[0] for b in blocks), tuple(sources), first, scale
     )
@@ -147,7 +147,7 @@
             pltpu.VMEM((4 * rows, total), jnp.bfloat16),
             pltpu.SemaphoreType.DMA((10 + len(blocks) + len(sources),)),
         ],
-        compiler_params=pltpu.CompilerParams(vmem_limit_bytes=48 * 2**20),
+        compiler_params=pltpu.CompilerParams(vmem_limit_bytes=60 * 2**20),
         cost_estimate=pl.CostEstimate(
             flops=16 * rows * width * total,
             bytes_accessed=20 * 2**20,
@@ -162,15 +162,17 @@
 
 
 def adam_kernel(scale, here, winner, rate, w_ref, *refs):
-    got, kept, came, outs = refs[0], refs[1:3], refs[3:5], refs[-6:]
+    got, kept, came, outs = refs[:2], refs[2:4], refs[4:8], refs[8:]
     learning = rate[0]
     column = winner[here[0]] // 2
 
     def moment(part):
-        return got[(column + part) % 4].astype(jnp.float32)
+        which = (column + part) % 4
+        return jnp.concatenate([got[0][which], got[1][which]], axis=1).astype(jnp.float32)
 
     for p in range(2):
-        grad = (kept[p][...] + came[p][...]) * scale
+        sent = jnp.concatenate([came[2 * p][...], came[2 * p + 1][...]], axis=1)
+        grad = (kept[p][...] + sent) * scale
         first_new = 0.9 * moment(p) + 0.1 * grad
         second_new = 0.95 * moment(2 + p) + 0.05 * grad * grad
         update = learning * (first_new / bias_first) / (jnp.sqrt(second_new / bias_second) + 1e-08)
@@ -179,32 +181,25 @@
         outs[4 + p][0] = second_new.astype(jnp.bfloat16)
 
 
-def adam(here, winner, rate, weights, got, mine, other, scale, part, earlier):
+def adam(here, winner, rate, weights, got, mine, other, scale):
     hidden, width = weights.shape[1], weights.shape[2]
-    rows = 16
-    steps = got.shape[1] // rows
-    off = part * steps
-    pair = pl.BlockSpec((2, rows, width), lambda i, *_: (0, i + off, 0))
-    four = pl.BlockSpec((4, rows, width), lambda i, *_: (0, i, 0))
-    flat = pl.BlockSpec((rows, width), lambda i, *_: (i + off, 0))
-    piece = pl.BlockSpec((rows, width), lambda i, *_: (i, 0))
-    one = pl.BlockSpec((1, rows, width), lambda i, *_: (0, i + off, 0))
-    whole = pl.BlockSpec(memory_space=pl.ANY)
+    rows = 32
+    pair = pl.BlockSpec((2, rows, width), lambda i, *_: (0, i, 0))
+    four = pl.BlockSpec((4, rows, width // 2), lambda i, *_: (0, i, 0))
+    flat = pl.BlockSpec((rows, width), lambda i, *_: (i, 0))
+    piece = pl.BlockSpec((rows, width // 2), lambda i, *_: (i, 0))
+    one = pl.BlockSpec((1, rows, width), lambda i, *_: (0, i, 0))
     return pl.pallas_call(
         functools.partial(adam_kernel, scale),
         grid_spec=pltpu.PrefetchScalarGridSpec(
             num_scalar_prefetch=3,
-            grid=(steps,),
-            in_specs=[pair, four] + [flat] * 2 + [piece] * 2 + [whole] * len(earlier),
+            grid=(hidden // rows,),
+            in_specs=[pair] + [four] * 2 + [flat] * 2 + [piece] * 4,
             out_specs=[one] * 6,
         ),
         out_shape=[jax.ShapeDtypeStruct((1, hidden, width), jnp.bfloat16)] * 6,
-        input_output_aliases={9 + k: k for k in range(len(earlier))},
-        compiler_params=pltpu.CompilerParams(vmem_limit_bytes=32 * 2**20),
-        cost_estimate=pl.CostEstimate(
-            flops=40 * hidden * width, bytes_accessed=8 * 2**20, transcendentals=hidden * width
-        ),
-    )(here, winner, rate, weights, got, *mine, *other, *earlier)
+        compiler_params=pltpu.CompilerParams(vmem_limit_bytes=60 * 2**20),
+    )(here, winner, rate, weights, *got, *mine, *other)
 
 
 def losers(winner):
@@ -245,7 +240,7 @@
     if mode in ("gather", "columns"):
         last = refs.pop()
         came = [last.at[0], last.at[1]]
-    choices = [ref.at[pl.ds(span[0], span[1])] for ref in refs] + came
+    choices = [ref.at[:, pl.ds(span[0], span[1])] if span else ref for ref in refs] + came
     index = route(mode, here, winner)
     for k in range(count):
         for i, ref in enumerate(choices):
@@ -263,10 +258,9 @@
 
 def pick(mode, here, winner, arrays, span=None):
     rows, width = arrays[0].shape
-    span = span or (0, rows)
+    shape = (rows, span[1] if span else width)
     kind = arrays[0].dtype
     count = 2 if mode == "cross" else 4
-    shape = (span[1], width)
     smem = pl.BlockSpec(memory_space=pltpu.SMEM)
     anywhere = pl.BlockSpec(memory_space=pl.ANY)
     if mode == "gather":
@@ -282,9 +276,9 @@
             pltpu.VMEM((count,) + shape, kind),
             pltpu.SemaphoreType.DMA((8,)),
         ],
-        compiler_params=pltpu.CompilerParams(vmem_limit_bytes=16 * 2**20),
+        compiler_params=pltpu.CompilerParams(vmem_limit_bytes=60 * 2**20),
         cost_estimate=pl.CostEstimate(
-            flops=0, bytes_accessed=4 * count * span[1] * width, transcendentals=0
+            flops=0, bytes_accessed=4 * count * arrays[0].size, transcendentals=0
         ),
     )(here, winner, *arrays)
 
@@ -337,49 +331,46 @@
         )
 
     half = hidden // 2
-    spans = [(0, half), (half, half)]
+    spans = [(0, width // 2), (width // 2, width // 2)]
     weights = [w[0, k * half : (k + 1) * half] for w in (gate_weight, up_weight) for k in range(2)]
     moments = [m[0] for m in (gate_first, up_first, gate_second, up_second)]
+    turned = cotangent[0].T.reshape(16, 2 * hidden, count)
     with jax.named_scope("tick_a"):
+        cots = lax.all_to_all(turned, "fsdp", 0, 0, axis_index_groups=same_core, tiled=True)
+        start = jnp.concatenate([own, fsdp(own, low_swap)])
         held0 = [weights[0], *spread(weights)]
-        partner = fsdp(own, low_swap)
-    partner, held0, own, turned, moments = sync((partner, held0, own, cotangent[0], moments))
+    start, held0, moments = sync((start, held0, moments))
     with jax.named_scope("tick_b"):
+        up1, down1 = fsdp(start, z_up), fsdp(start, z_down)
         came0 = exchange(held0)
-        near = [lax.ppermute(moments[j], "member", along_row(j)) for j in (1, 3)]
-        start = jnp.concatenate([own, partner])
-        up1, down1 = fsdp(start, z_up), fsdp(start, z_down)
-        turned = turned.T.reshape(16, 2 * hidden, count)
-        cots = lax.all_to_all(turned, "fsdp", 0, 0, axis_index_groups=same_core, tiled=True)
-    up1, down1, came0, held0, near, moments = sync((up1, down1, came0, held0, near, moments))
-    with jax.named_scope("tick_b"):
+        held1 = [moments[0], *spread(moments)]
+    up1, down1, came0, held0, cots = sync((up1, down1, came0, held0, cots))
+    with jax.named_scope("tick_c"):
         up2, down2 = fsdp(up1, z_up), fsdp(down1, z_down)
-        far = lax.ppermute(moments[2], "member", along_row(2))
-        held1 = [moments[0], near[0], far, near[1]]
-    up2, down2, came0, held0, held1 = sync((up2, down2, came0, held0, held1))
-    with jax.named_scope("tick_c"):
+        got0 = gathered(held0, came0)
+    up2, down2, got0, held1 = sync((up2, down2, got0, held1))
+    with jax.named_scope("tick_d"):
         up3, down3 = fsdp(up2, z_up), fsdp(down2, z_down)
-        got0 = gathered(held0, came0)
         came1 = exchange(held1, spans[0])
-    up3, down3, got0, came1, held1, cots = sync((up3, down3, got0, came1, held1, cots))
-    with jax.named_scope("tick_d"):
         mine = pick("place", here, winner, got0).reshape(2, hidden, width)
         theirs = fsdp(mine, core_swap)
+        sources = [(d, b) for d in (0, -1, 1) for b in range(2)]
+        sums = terms(here, mine, theirs, cots, [start, up1, down1], sources, None, scale)
+    up3, down3, came1, sums, held1 = sync((up3, down3, came1, sums, held1))
+    with jax.named_scope("tick_e"):
+        sides = [fsdp(up3[:count], z_up), fsdp(down3[count:], z_down)]
         got1 = columns(held1, came1, spans[0])
         came2 = exchange(held1, spans[1])
-        sides = [fsdp(up3[:count], z_up), fsdp(down3[count:], z_down)]
-        blocks = [start, up1, down1, up2, down2]
-        sources = [(d, b) for d in (0, -1, 1, -2, 2) for b in range(2)]
-        totals = terms(here, mine, theirs, cots, blocks, sources, None, scale)
-    sides, came2, totals, got1, held1 = sync((sides, came2, totals, got1, held1))
-    with jax.named_scope("tick_e"):
+        sources = [(d, b) for d in (-2, 2, -3, 3) for b in range(2)]
+        sums = terms(here, mine, theirs, cots, [up2, down2, up3, down3], sources, sums, scale)
+    sides, came2, sums, got1, held1 = sync((sides, came2, sums, got1, held1))
+    with jax.named_scope("tick_f"):
         got2 = columns(held1, came2, spans[1])
-        sources = [(d, b) for d in (-3, 3, 4) for b in range(2)]
-        sums = terms(here, mine, theirs, cots, [up3, down3, *sides], sources, totals, scale)
+        sources = [(4, b) for b in range(2)]
+        sums = terms(here, mine, theirs, cots, sides, sources, sums, scale)
         other = [fsdp(part, core_swap) for part in sums[2:]]
     with jax.named_scope("adam"):
-        new = adam(here, winner, rate, mine, got1, sums[:2], other[0::2], scale, 0, [])
-        return tuple(adam(here, winner, rate, mine, got2, sums[:2], other[1::2], scale, 1, new))
+        return tuple(adam(here, winner, rate, mine, [got1, got2], sums[:2], other, scale))
 
 
 def solution(mesh):

time: 262 us -> 218 us (0.83)
  waiting for transfers between devices: 99 us -> 68.8 us
  local copies, waits for them, and re-layouts: 40.1 us -> 13.1 us
  Pallas kernels: 59.5 us -> 71.2 us
    unnamed x89 -> x46, local copies, waits for them, and re-layouts: 31.6 us -> 5.71 us
    ppermute x14, waiting for transfers between devices: 32.6 us -> 11.6 us  [fsdp(): return lax.ppermute(value, 'fsdp', pairs)]
    ppermute x3 -> x0, waiting for transfers between devices: 18 us -> none  [the longest x1 18 us: body(): far = lax.ppermute(moments[2], 'member', along_row(2))]
    ppermute x3, waiting for transfers between devices: 19.1 us -> 28.5 us  [exchange(): lax.ppermute(pick('cross', here, winner, held, span), 'member', row_swap)]
    pallas_call x2 -> x3, Pallas kernels: 32.1 us -> 40.6 us  [terms(): pl.pallas_call(kernel, in_specs=[pl.BlockSpec(memory_space=pltpu.SMEM)] +...]
    ppermute x6 -> x9, starting transfers between devices: 7.22 us -> 14.1 us  [spread(): return [lax.ppermute(pieces[j], 'member', along_row(j)) for j in (1, 2, 3)]]
    pallas_call x7, Pallas kernels: 14.2 us -> 20.2 us  [pick(): pl.pallas_call(functools.partial(pick_kernel, mode, span), in_specs=[smem...]
    ppermute x14, starting transfers between devices: 23.6 us -> 18.1 us  [fsdp(): return lax.ppermute(value, 'fsdp', pairs)]
  transfers between devices with their start and end apart: 29 -> 29, of which waited for: 12 -> 13; matrix products, arithmetic and copies ran while one was open for 2% -> 2% of each run, Pallas kernels for 18% -> 24%
where the time goes in v5:
time: 218 us; the launch traced here: 216 us
  Pallas kernels  71.2 us (33%)
  waiting for transfers between devices  68.8 us (32%)
  starting transfers between devices  59.2 us (27%)
  local copies, waits for them, and re-layouts  13.1 us (6%)
    pallas_call x3, Pallas kernels, terms(): pl.pallas_call(kernel, in_specs=[pl.BlockSpec(memory_space=pltpu.SMEM)] +...  40.6 us
    ppermute x9, waiting for transfers between devices, spread(): return [lax.ppermute(pieces[j], 'member', along_row(j)) for j in (1, 2, 3)]  28.6 us
    ppermute x3, waiting for transfers between devices, exchange(): lax.ppermute(pick('cross', here, winner, held, span), 'member', row_swap)  28.5 us
    pallas_call x7, Pallas kernels, pick(): pl.pallas_call(functools.partial(pick_kernel, mode, span), in_specs=[smem...  20.2 us
    ppermute x14, starting transfers between devices, fsdp(): return lax.ppermute(value, 'fsdp', pairs)  18.1 us
    ppermute x9, starting transfers between devices, spread(): return [lax.ppermute(pieces[j], 'member', along_row(j)) for j in (1, 2, 3)]  14.1 us
    ppermute x14, waiting for transfers between devices, fsdp(): return lax.ppermute(value, 'fsdp', pairs)  11.6 us
    pallas_call x1, Pallas kernels, adam(): pl.pallas_call(functools.partial(adam_kernel, scale), grid_spec=pltpu.Pre...  10.4 us
  transfers between devices with their start and end apart: 29, of which 13 were waited for; matrix products, arithmetic and copies ran while one was open for 2% of the time, Pallas kernels for 24%

profile of v5, /device:TPU:1, one launch (start us, length us, event | category | flops | bytes accessed | tf_op | source)
XLA Modules:
  0.0 215.8 jit_solution(2697358279624759687)
XLA Ops:
  0.6 3.9 %copy.16 = bf16[7168,128]{1,0:T(8,128)(2,1)} copy(bf16[7168,128]{0,1:T(8,128)(2,1)} %bitcast.29) | data formatting | bytes 3670016 | tf_op jit(solution)/shard_map/transpose | solution.py:337
  4.5 10.3 %all-to-all-start = ((bf16[16,448,128]{2,1,0:T(8,128)(2,1)}), bf16[16,448,128]{2,1,0:T(8,128)(2,1)}, u32[]{:S(2)}, u32[]{:S(2)}) async-start(bf16[16,448,128]{2,1,0:T(8,128)(2,1)} %bitcast.13), calls=%async_computation | async-start | bytes 3670016 | tf_op jit(solution)/shard_map/tick_a/all_to_all | solution.py:339
  14.8 1.4 collective-permute-start
  17.0 1.2 collective-permute-start.1
  18.3 1.5 collective-permute-start.3
  19.9 1.5 collective-permute-start.2
  22.0 6.5 %collective-permute-done = bf16[128,1792]{1,0:T(8,128)(2,1)S(1)} collective-permute-done((bf16[128,1792]{1,0:T(8,128)(2,1)S(1)}, bf16[128,1792]{1,0:T(8,128)(2,1)S(1)}, u32[]{:S(2)}, u32[]{:S(2)}) %collective-permute-start) | collective-permute-done | bytes 458784 | tf_op jit(solution)/shard_map/tick_a/ppermute | solution.py:314
  28.5 1.0 pad_maximum_fusion.refs_0_
  29.6 7.6 %collective-permute-done.2.refs_2_ = bf16[112,1792]{1,0:T(8,128)(2,1)S(1)} collective-permute-done((bf16[112,1792]{1,0:T(8,128)(2,1)S(1)}, bf16[112,1792]{1,0:T(8,128)(2,1)S(1)}, u32[]{:S(2)}, u32[]{:S(2)}) %collective-permute-start.2) | collective-permute-done | bytes 401440 | tf_op jit(solution)/shard_map/tick_a/ppermute | solution.py:287
  38.0 2.6 %tick_b.1 = bf16[2,112,1792]{2,1,0:T(8,128)(2,1)} custom-call(s32[2]{0:T(128)} %pad_add_fusion.here, s32[8]{0:T(128)} %winner.15, bf16[112,1792]{1,0:T(8,128)(2,1)} %get-tuple-element.89.refs_0_, bf16[112,1792]{1,0:T(8,128)(2,1)} %copy-done.6, bf16[112,1792]{1,0:T(8,128)(2,1)} %copy-done.8, bf16[112,1792]{1,0:T(8,128)(2,1)} %copy-done.7), custom_call_target="tpu_custom_call" | custom-call | bytes 1605632 | tf_op jit(solution)/shard_map/tick_b/pallas_call | solution.py:270
  40.6 2.7 %collective-permute-start.6 = (bf16[2,112,1792]{2,1,0:T(8,128)(2,1)}, bf16[2,112,1792]{2,1,0:T(8,128)(2,1)S(1)}, u32[]{:S(2)}, u32[]{:S(2)}) collective-permute-start(bf16[2,112,1792]{2,1,0:T(8,128)(2,1)} %tick_b.1), channel_id=1, source_target_pairs={{0,32},{32,0},{64,96},{96,64},{128,160},{160,128},{192,224},{224,1... | collective-permute-start | bytes 2408456 | tf_op jit(solution)/shard_map/tick_b/ppermute | solution.py:317
  43.3 2.3 %collective-permute-start.5 = (bf16[256,1792]{1,0:T(8,128)(2,1)}, bf16[256,1792]{1,0:T(8,128)(2,1)}, u32[]{:S(2)}, u32[]{:S(2)}) collective-permute-start(bf16[256,1792]{1,0:T(8,128)(2,1)} %pad_maximum_fusion.refs_0_), channel_id=1, source_target_pairs={{4,0},{5,1},{6,2},{7,3},{8,4},{9,5},{10,6},{11,7},{12,8},{13,9},{1... | collective-permute-start | bytes 2752520 | tf_op jit(solution)/shard_map/tick_b/ppermute | solution.py:314
  46.4 1.7 collective-permute-start.13
  48.1 26.0 %collective-permute-done.6.refs_4_ = bf16[2,112,1792]{2,1,0:T(8,128)(2,1)S(1)} collective-permute-done((bf16[2,112,1792]{2,1,0:T(8,128)(2,1)}, bf16[2,112,1792]{2,1,0:T(8,128)(2,1)S(1)}, u32[]{:S(2)}, u32[]{:S(2)}) %collective-permute-start.6) | collective-permute-done | bytes 802848 | tf_op jit(solution)/shard_map/tick_b/ppermute | solution.py:317
  74.1 1.5 collective-permute-start.14
  75.9 0.9 collective-permute-done.4.refs_1_
  76.9 2.6 %collective-permute-start.8 = (bf16[256,1792]{1,0:T(8,128)(2,1)}, bf16[256,1792]{1,0:T(8,128)(2,1)}, u32[]{:S(2)}, u32[]{:S(2)}) collective-permute-start(bf16[256,1792]{1,0:T(8,128)(2,1)} %collective-permute-done.5.refs_2_), channel_id=1, source_target_pairs={{4,0},{5,1},{6,2},{7,3},{8,4},{9,5},{10,6},{11,7},{12,8},{13,9},{1... | collective-permute-start | bytes 2752520 | tf_op jit(solution)/shard_map/tick_c/ppermute | solution.py:314
  79.5 3.3 %tick_c.1 = (bf16[112,1792]{1,0:T(8,128)(2,1)}, bf16[112,1792]{1,0:T(8,128)(2,1)}, bf16[112,1792]{1,0:T(8,128)(2,1)}, bf16[112,1792]{1,0:T(8,128)(2,1)}) custom-call(s32[2]{0:T(128)} %pad_add_fusion.here, s32[8]{0:T(128)} %winner.15, bf16[112,1792]{1,0:T(8,128)(2,1)} %get-tuple-element.89.refs_0_, bf16[112,1792]{1,0:T(8,128)(2,1)} %copy-done.6, ...), custom_call_target="tpu_custom_call" | custom-call | bytes 3211264 | tf_op jit(solution)/shard_map/tick_c/pallas_call | solution.py:270
  83.8 2.7 %collective-permute-start.10 = (bf16[112,1792]{1,0:T(8,128)(2,1)}, bf16[112,1792]{1,0:T(8,128)(2,1)S(1)}, u32[]{:S(2)}, u32[]{:S(2)}) collective-permute-start(bf16[112,1792]{1,0:T(8,128)(2,1)} %get-tuple-element.96), channel_id=1, source_target_pairs={{0,128},{32,160},{64,192},{96,224},{128,0},{160,32},{192,64},{224,... | collective-permute-start | bytes 1204232 | tf_op jit(solution)/shard_map/tick_c/ppermute | solution.py:287
  86.5 6.2 %collective-permute-done.14.refs_3_ = bf16[224,1792]{1,0:T(8,128)(2,1)S(1)} collective-permute-done((bf16[224,1792]{1,0:T(8,128)(2,1)}, bf16[224,1792]{1,0:T(8,128)(2,1)S(1)}, u32[]{:S(2)}, u32[]{:S(2)}) %collective-permute-start.14) | collective-permute-done | bytes 802848 | tf_op jit(solution)/shard_map/tick_b/ppermute | solution.py:287
  92.7 2.3 %collective-permute-start.11 = (bf16[112,1792]{1,0:T(8,128)(2,1)}, bf16[112,1792]{1,0:T(8,128)(2,1)S(1)}, u32[]{:S(2)}, u32[]{:S(2)}) collective-permute-start(bf16[112,1792]{1,0:T(8,128)(2,1)} %get-tuple-element.97), channel_id=1, source_target_pairs={{0,192},{32,224},{64,0},{96,32},{128,64},{160,96},{192,128},{224,1... | collective-permute-start | bytes 1204232 | tf_op jit(solution)/shard_map/tick_c/ppermute | solution.py:287
  95.0 7.6 %collective-permute-done.10.refs_2_ = bf16[112,1792]{1,0:T(8,128)(2,1)S(1)} collective-permute-done((bf16[112,1792]{1,0:T(8,128)(2,1)}, bf16[112,1792]{1,0:T(8,128)(2,1)S(1)}, u32[]{:S(2)}, u32[]{:S(2)}) %collective-permute-start.10) | collective-permute-done | bytes 401440 | tf_op jit(solution)/shard_map/tick_c/ppermute | solution.py:287
  102.6 7.2 %collective-permute-done.11.refs_3_ = bf16[112,1792]{1,0:T(8,128)(2,1)S(1)} collective-permute-done((bf16[112,1792]{1,0:T(8,128)(2,1)}, bf16[112,1792]{1,0:T(8,128)(2,1)S(1)}, u32[]{:S(2)}, u32[]{:S(2)}) %collective-permute-start.11) | collective-permute-done | bytes 401440 | tf_op jit(solution)/shard_map/tick_c/ppermute | solution.py:287
  110.5 2.9 %tick_d.3 = bf16[4,112,1792]{2,1,0:T(8,128)(2,1)} custom-call(s32[2]{0:T(128)} %pad_add_fusion.here, s32[8]{0:T(128)} %winner.15, bf16[112,1792]{1,0:T(8,128)(2,1)} %get-tuple-element.102.refs_0_, bf16[112,1792]{1,0:T(8,128)(2,1)} %copy-done.18, bf16[112,1792]{1,0:T(8,128)(2,1)} %copy-done.19, bf16[112,1792]{1,0:T(8,128)(2,1)} %copy-done.20), custom_call_target="tpu_custom_call" | custom-call | bytes 3211264 | tf_op jit(solution)/shard_map/tick_d/pallas_call | solution.py:270
  113.5 2.2 %collective-permute-start.18 = (bf16[2,224,1792]{2,1,0:T(8,128)(2,1)}, bf16[2,224,1792]{2,1,0:T(8,128)(2,1)S(1)}, u32[]{:S(2)}, u32[]{:S(2)}) collective-permute-start(bf16[2,224,1792]{2,1,0:T(8,128)(2,1)} %bitcast.20), channel_id=1, source_target_pairs={{0,1},{1,0},{2,3},{3,2},{4,5},{5,4},{6,7},{7,6},{8,9},{9,8},{10,11... | collective-permute-start | bytes 4816904 | tf_op jit(solution)/shard_map/tick_d/ppermute | solution.py:314
  115.7 2.7 %collective-permute-start.16 = (bf16[256,1792]{1,0:T(8,128)(2,1)}, bf16[256,1792]{1,0:T(8,128)(2,1)}, u32[]{:S(2)}, u32[]{:S(2)}) collective-permute-start(bf16[256,1792]{1,0:T(8,128)(2,1)} %collective-permute-done.8.refs_1_), channel_id=1, source_target_pairs={{4,0},{5,1},{6,2},{7,3},{8,4},{9,5},{10,6},{11,7},{12,8},{13,9},{1... | collective-permute-start | bytes 2752520 | tf_op jit(solution)/shard_map/tick_d/ppermute | solution.py:314
  118.4 2.6 %tick_d.4 = bf16[2,224,896]{2,1,0:T(8,128)(2,1)} custom-call(s32[2]{0:T(128)} %pad_add_fusion.here, s32[8]{0:T(128)} %winner.15, bf16[224,1792]{1,0:T(8,128)(2,1)} %bitcast.25, bf16[224,1792]{1,0:T(8,128)(2,1)} %copy-done, bf16[224,1792]{1,0:T(8,128)(2,1)} %copy-done.1, bf16[224,1792]{1,0:T(8,128)(2,1)} %copy-done.2), custom_call_target="tpu_custom_call" | custom-call | bytes 3211264 | tf_op jit(solution)/shard_map/tick_d/pallas_call | solution.py:270
  121.0 2.6 %collective-permute-start.17 = (bf16[2,224,896]{2,1,0:T(8,128)(2,1)}, bf16[2,224,896]{2,1,0:T(8,128)(2,1)S(1)}, u32[]{:S(2)}, u32[]{:S(2)}) collective-permute-start(bf16[2,224,896]{2,1,0:T(8,128)(2,1)} %tick_d.4), channel_id=1, source_target_pairs={{0,32},{32,0},{64,96},{96,64},{128,160},{160,128},{192,224},{224,1... | collective-permute-start | bytes 2408456 | tf_op jit(solution)/shard_map/tick_d/ppermute | solution.py:317
  123.6 1.2 copy-done.5
  124.8 14.1 %tick_d.5 = (f32[224,1792]{1,0:T(8,128)}, f32[224,1792]{1,0:T(8,128)}, f32[224,896]{1,0:T(8,128)}, f32[224,896]{1,0:T(8,128)}, f32[224,896]{1,0:T(8,128)}, /*index=5*/f32[224,896]{1,0:T(8,128)}) custom-call(s32[2]{0:T(128)} %pad_add_fusion.here, bf16[2,224,1792]{2,1,0:T(8,128)(2,1)} %bitcast.21, bf16[2,224,1792]{2,1,0:T(8,128)(2,1)} %copy-done.5, ...), custom_call_target="tpu_custom_call" | custom-call | flops 4932501504 | bytes 20971520 | tf_op jit(solution)/shard_map/tick_d/pallas_call | solution.py:137
  138.8 2.6 %collective-permute-done.17.refs_4_ = bf16[2,224,896]{2,1,0:T(8,128)(2,1)S(1)} collective-permute-done((bf16[2,224,896]{2,1,0:T(8,128)(2,1)}, bf16[2,224,896]{2,1,0:T(8,128)(2,1)S(1)}, u32[]{:S(2)}, u32[]{:S(2)}) %collective-permute-start.17) | collective-permute-done | bytes 802848 | tf_op jit(solution)/shard_map/tick_d/ppermute | solution.py:317
  142.3 3.0 %tick_e.5 = bf16[4,224,896]{2,1,0:T(8,128)(2,1)} custom-call(s32[2]{0:T(128)} %pad_add_fusion.here, s32[8]{0:T(128)} %winner.15, bf16[224,1792]{1,0:T(8,128)(2,1)} %bitcast.26, bf16[224,1792]{1,0:T(8,128)(2,1)} %copy-done, bf16[224,1792]{1,0:T(8,128)(2,1)} %copy-done.1, bf16[224,1792]{1,0:T(8,128)(2,1)} %copy-done.2, bf16[2,224,896]{2,1,0:T(8,128)(2,1)} %copy-done.12), custom_call_target="tpu_custom_call" | custom-call | bytes 6422528 | tf_op jit(solution)/shard_map/tick_e/pallas_call | solution.py:270
  145.3 4.4 %all-to-all-start.1 = ((bf16[4,224,896]{2,1,0:T(8,128)(2,1)}), bf16[4,224,896]{2,1,0:T(8,128)(2,1)S(1)}, u32[]{:S(2)}, u32[]{:S(2)}) async-start(bf16[4,224,896]{2,1,0:T(8,128)(2,1)} %tick_e.5), calls=%async_computation.1 | async-start | bytes 3211264 | tf_op jit(solution)/shard_map/tick_e/all_to_all | solution.py:324
  149.7 2.6 %tick_e.3 = bf16[2,224,896]{2,1,0:T(8,128)(2,1)} custom-call(s32[2]{0:T(128)} %pad_add_fusion.here, s32[8]{0:T(128)} %winner.15, bf16[224,1792]{1,0:T(8,128)(2,1)} %bitcast.27, bf16[224,1792]{1,0:T(8,128)(2,1)} %copy-done, bf16[224,1792]{1,0:T(8,128)(2,1)} %copy-done.1, bf16[224,1792]{1,0:T(8,128)(2,1)} %copy-done.2), custom_call_target="tpu_custom_call" | custom-call | bytes 3211264 | tf_op jit(solution)/shard_map/tick_e/pallas_call | solution.py:270
  152.4 2.7 %collective-permute-start.21 = (bf16[2,224,896]{2,1,0:T(8,128)(2,1)}, bf16[2,224,896]{2,1,0:T(8,128)(2,1)S(1)}, u32[]{:S(2)}, u32[]{:S(2)}) collective-permute-start(bf16[2,224,896]{2,1,0:T(8,128)(2,1)} %tick_e.3), channel_id=1, source_target_pairs={{0,32},{32,0},{64,96},{96,64},{128,160},{160,128},{192,224},{224,1... | collective-permute-start | bytes 2408456 | tf_op jit(solution)/shard_map/tick_e/ppermute | solution.py:317
  155.1 1.0 slice.23
  156.2 1.0 slice.22
  157.3 2.7 %collective-permute-start.20 = (bf16[128,1792]{1,0:T(8,128)(2,1)S(1)}, bf16[128,1792]{1,0:T(8,128)(2,1)}, u32[]{:S(2)}, u32[]{:S(2)}) collective-permute-start(bf16[128,1792]{1,0:T(8,128)(2,1)S(1)} %slice.23), channel_id=1, source_target_pairs={{4,0},{5,1},{6,2},{7,3},{8,4},{9,5},{10,6},{11,7},{12,8},{13,9},{1... | collective-permute-start | bytes 1376264 | tf_op jit(solution)/shard_map/tick_e/ppermute | solution.py:314
  160.0 16.7 %tick_e.4 = (f32[224,1792]{1,0:T(8,128)}, f32[224,1792]{1,0:T(8,128)}, f32[224,896]{1,0:T(8,128)}, f32[224,896]{1,0:T(8,128)}, f32[224,896]{1,0:T(8,128)}, /*index=5*/f32[224,896]{1,0:T(8,128)}) custom-call(s32[2]{0:T(128)} %pad_add_fusion.here, bf16[2,224,1792]{2,1,0:T(8,128)(2,1)} %bitcast.22, bf16[2,224,1792]{2,1,0:T(8,128)(2,1)} %copy-done.5, ...), custom_call_target="tpu_custom_call" | custom-call | flops 6576668672 | bytes 20971520 | tf_op jit(solution)/shard_map/tick_e/pallas_call | solution.py:137
  176.7 0.9 copy-done.11
  177.7 3.0 %tick_f.2 = bf16[4,224,896]{2,1,0:T(8,128)(2,1)} custom-call(s32[2]{0:T(128)} %pad_add_fusion.here, s32[8]{0:T(128)} %winner.15, bf16[224,1792]{1,0:T(8,128)(2,1)} %bitcast.28, bf16[224,1792]{1,0:T(8,128)(2,1)} %copy-done, bf16[224,1792]{1,0:T(8,128)(2,1)} %copy-done.1, bf16[224,1792]{1,0:T(8,128)(2,1)} %copy-done.2, bf16[2,224,896]{2,1,0:T(8,128)(2,1)} %copy-done.11), custom_call_target="tpu_custom_call" | custom-call | bytes 6422528 | tf_op jit(solution)/shard_map/tick_f/pallas_call | solution.py:270
  180.6 4.3 %all-to-all-start.2 = ((bf16[4,224,896]{2,1,0:T(8,128)(2,1)}), bf16[4,224,896]{2,1,0:T(8,128)(2,1)S(1)}, u32[]{:S(2)}, u32[]{:S(2)}) async-start(bf16[4,224,896]{2,1,0:T(8,128)(2,1)} %tick_f.2), calls=%async_computation.2 | async-start | bytes 3211264 | tf_op jit(solution)/shard_map/tick_f/all_to_all | solution.py:324
  185.0 9.9 %tick_f.3 = (f32[224,1792]{1,0:T(8,128)}, f32[224,1792]{1,0:T(8,128)}, f32[224,896]{1,0:T(8,128)}, f32[224,896]{1,0:T(8,128)}, f32[224,896]{1,0:T(8,128)}, /*index=5*/f32[224,896]{1,0:T(8,128)}) custom-call(s32[2]{0:T(128)} %pad_add_fusion.here, bf16[2,224,1792]{2,1,0:T(8,128)(2,1)} %bitcast.23, bf16[2,224,1792]{2,1,0:T(8,128)(2,1)} %copy-done.5, ...), custom_call_target="tpu_custom_call" | custom-call | flops 1644167168 | bytes 20971520 | tf_op jit(solution)/shard_map/tick_f/pallas_call | solution.py:137
  194.9 3.4 %collective-permute-start.22 = (f32[224,896]{1,0:T(8,128)}, f32[224,896]{1,0:T(8,128)S(1)}, u32[]{:S(2)}, u32[]{:S(2)}) collective-permute-start(f32[224,896]{1,0:T(8,128)} %get-tuple-element.154), channel_id=1, source_target_pairs={{0,1},{1,0},{2,3},{3,2},{4,5},{5,4},{6,7},{7,6},{8,9},{9,8},{10,11... | collective-permute-start | bytes 2408456 | tf_op jit(solution)/shard_map/tick_f/ppermute | solution.py:314
  200.5 2.3 %collective-permute-done.23.refs_5_ = f32[224,896]{1,0:T(8,128)S(1)} collective-permute-done((f32[224,896]{1,0:T(8,128)}, f32[224,896]{1,0:T(8,128)S(1)}, u32[]{:S(2)}, u32[]{:S(2)}) %collective-permute-start.23) | collective-permute-done | bytes 802848 | tf_op jit(solution)/shard_map/tick_f/ppermute | solution.py:314
  202.9 1.1 collective-permute-done.25.refs_7_
  204.1 1.2 copy-done.4
  205.2 10.4 %adam.1 = (bf16[1,224,1792]{2,1,0:T(8,128)(2,1)}, bf16[1,224,1792]{2,1,0:T(8,128)(2,1)}, bf16[1,224,1792]{2,1,0:T(8,128)(2,1)}, bf16[1,224,1792]{2,1,0:T(8,128)(...) custom-call(s32[2]{0:T(128)} %pad_add_fusion.here, s32[8]{0:T(128)} %winner.15, ...), custom_call_target="tpu_custom_call" | custom-call | tf_op jit(solution)/shard_map/adam/pallas_call | solution.py:192
  (75 shorter events, 7.6 us)
Async XLA Ops:
  4.5 10.3 %copy-start.16 = (bf16[1,128,1792]{2,1,0:T(8,128)(2,1)S(1)}, bf16[1,128,1792]{2,1,0:T(8,128)(2,1)}, u32[]{:S(2)}) copy-start(bf16[1,128,1792]{2,1,0:T(8,128)(2,1)} %param.10) | copy-start | bytes 1376260
  4.5 11.7 %copy-start.13 = (bf16[1,224,1792]{2,1,0:T(8,128)(2,1)S(1)}, bf16[1,224,1792]{2,1,0:T(8,128)(2,1)}, u32[]{:S(2)}) copy-start(bf16[1,224,1792]{2,1,0:T(8,128)(2,1)} %param.12) | copy-start | bytes 2408452
  4.5 72.3 %all-to-all-start = ((bf16[16,448,128]{2,1,0:T(8,128)(2,1)}), bf16[16,448,128]{2,1,0:T(8,128)(2,1)}, u32[]{:S(2)}, u32[]{:S(2)}) async-start(bf16[16,448,128]{2,1,0:T(8,128)(2,1)} %bitcast.13), calls=%async_computation | async-start | bytes 3670016 | tf_op jit(solution)/shard_map/tick_a/all_to_all | solution.py:339
  14.8 3.4 %copy-start.14 = (bf16[1,224,1792]{2,1,0:T(8,128)(2,1)S(1)}, bf16[1,224,1792]{2,1,0:T(8,128)(2,1)}, u32[]{:S(2)}) copy-start(bf16[1,224,1792]{2,1,0:T(8,128)(2,1)} %param.13) | copy-start | bytes 2408452
  14.8 13.7 %collective-permute-start = (bf16[128,1792]{1,0:T(8,128)(2,1)S(1)}, bf16[128,1792]{1,0:T(8,128)(2,1)S(1)}, u32[]{:S(2)}, u32[]{:S(2)}) collective-permute-start(bf16[128,1792]{1,0:T(8,128)(2,1)S(1)} %bitcast.30), channel_id=1, source_target_pairs={{0,2},{1,3},{2,0},{3,1},{4,6},{5,7},{6,4},{7,5},{8,10},{9,11},{10,... | collective-permute-start | bytes 1376264 | tf_op jit(solution)/shard_map/tick_a/ppermute | solution.py:314
  17.0 12.5 %collective-permute-start.1 = (bf16[112,1792]{1,0:T(8,128)(2,1)S(1)}, bf16[112,1792]{1,0:T(8,128)(2,1)S(1)}, u32[]{:S(2)}, u32[]{:S(2)}) collective-permute-start(bf16[112,1792]{1,0:T(8,128)(2,1)S(1)} %get-tuple-element.160), channel_id=1, source_target_pairs={{0,64},{32,96},{64,128},{96,160},{128,192},{160,224},{192,0},{224,... | collective-permute-start | bytes 1204232 | tf_op jit(solution)/shard_map/tick_a/ppermute | solution.py:287
  18.3 11.3 %collective-permute-start.3 = (bf16[112,1792]{1,0:T(8,128)(2,1)S(1)}, bf16[112,1792]{1,0:T(8,128)(2,1)S(1)}, u32[]{:S(2)}, u32[]{:S(2)}) collective-permute-start(bf16[112,1792]{1,0:T(8,128)(2,1)S(1)} %get-tuple-element.158), channel_id=1, source_target_pairs={{0,192},{32,224},{64,0},{96,32},{128,64},{160,96},{192,128},{224,1... | collective-permute-start | bytes 1204232 | tf_op jit(solution)/shard_map/tick_a/ppermute | solution.py:287
  19.9 17.4 %collective-permute-start.2 = (bf16[112,1792]{1,0:T(8,128)(2,1)S(1)}, bf16[112,1792]{1,0:T(8,128)(2,1)S(1)}, u32[]{:S(2)}, u32[]{:S(2)}) collective-permute-start(bf16[112,1792]{1,0:T(8,128)(2,1)S(1)} %get-tuple-element.159), channel_id=1, source_target_pairs={{0,128},{32,160},{64,192},{96,224},{128,0},{160,32},{192,64},{224,... | collective-permute-start | bytes 1204232 | tf_op jit(solution)/shard_map/tick_a/ppermute | solution.py:287
  29.6 7.7 %copy-start.6 = (bf16[112,1792]{1,0:T(8,128)(2,1)}, bf16[112,1792]{1,0:T(8,128)(2,1)S(1)}, u32[]{:S(2)}) copy-start(bf16[112,1792]{1,0:T(8,128)(2,1)S(1)} %collective-permute-done.1.refs_1_) | copy-start | bytes 1204228
  29.6 7.6 %copy-start.7 = (bf16[112,1792]{1,0:T(8,128)(2,1)}, bf16[112,1792]{1,0:T(8,128)(2,1)S(1)}, u32[]{:S(2)}) copy-start(bf16[112,1792]{1,0:T(8,128)(2,1)S(1)} %collective-permute-done.3.refs_3_) | copy-start | bytes 1204228
  40.6 33.5 %collective-permute-start.6 = (bf16[2,112,1792]{2,1,0:T(8,128)(2,1)}, bf16[2,112,1792]{2,1,0:T(8,128)(2,1)S(1)}, u32[]{:S(2)}, u32[]{:S(2)}) collective-permute-start(bf16[2,112,1792]{2,1,0:T(8,128)(2,1)} %tick_b.1), channel_id=1, source_target_pairs={{0,32},{32,0},{64,96},{96,64},{128,160},{160,128},{192,224},{224,1... | collective-permute-start | bytes 2408456 | tf_op jit(solution)/shard_map/tick_b/ppermute | solution.py:317
  43.3 32.6 %collective-permute-start.5 = (bf16[256,1792]{1,0:T(8,128)(2,1)}, bf16[256,1792]{1,0:T(8,128)(2,1)}, u32[]{:S(2)}, u32[]{:S(2)}) collective-permute-start(bf16[256,1792]{1,0:T(8,128)(2,1)} %pad_maximum_fusion.refs_0_), channel_id=1, source_target_pairs={{4,0},{5,1},{6,2},{7,3},{8,4},{9,5},{10,6},{11,7},{12,8},{13,9},{1... | collective-permute-start | bytes 2752520 | tf_op jit(solution)/shard_map/tick_b/ppermute | solution.py:314
  45.6 31.2 %collective-permute-start.4 = (bf16[256,1792]{1,0:T(8,128)(2,1)}, bf16[256,1792]{1,0:T(8,128)(2,1)}, u32[]{:S(2)}, u32[]{:S(2)}) collective-permute-start(bf16[256,1792]{1,0:T(8,128)(2,1)} %pad_maximum_fusion.refs_0_), channel_id=1, source_target_pairs={{0,4},{1,5},{2,6},{3,7},{4,8},{5,9},{6,10},{7,11},{8,12},{9,13},{1... | collective-permute-start | bytes 2752520 | tf_op jit(solution)/shard_map/tick_b/ppermute | solution.py:314
  45.6 37.3 %collective-permute-start.12 = (bf16[224,1792]{1,0:T(8,128)(2,1)}, bf16[224,1792]{1,0:T(8,128)(2,1)S(1)}, u32[]{:S(2)}, u32[]{:S(2)}) collective-permute-start(bf16[224,1792]{1,0:T(8,128)(2,1)} %bitcast.8), channel_id=1, source_target_pairs={{0,64},{32,96},{64,128},{96,160},{128,192},{160,224},{192,0},{224,... | collective-permute-start | bytes 2408456 | tf_op jit(solution)/shard_map/tick_b/ppermute | solution.py:287
  46.4 37.3 %collective-permute-start.13 = (bf16[224,1792]{1,0:T(8,128)(2,1)}, bf16[224,1792]{1,0:T(8,128)(2,1)S(1)}, u32[]{:S(2)}, u32[]{:S(2)}) collective-permute-start(bf16[224,1792]{1,0:T(8,128)(2,1)} %bitcast.9), channel_id=1, source_target_pairs={{0,128},{32,160},{64,192},{96,224},{128,0},{160,32},{192,64},{224,... | collective-permute-start | bytes 2408456 | tf_op jit(solution)/shard_map/tick_b/ppermute | solution.py:287
  74.1 5.4 %copy-start.15 = (bf16[2,112,1792]{2,1,0:T(8,128)(2,1)}, bf16[2,112,1792]{2,1,0:T(8,128)(2,1)S(1)}, u32[]{:S(2)}) copy-start(bf16[2,112,1792]{2,1,0:T(8,128)(2,1)S(1)} %collective-permute-done.6.refs_4_) | copy-start | bytes 2408452
  74.1 18.6 %collective-permute-start.14 = (bf16[224,1792]{1,0:T(8,128)(2,1)}, bf16[224,1792]{1,0:T(8,128)(2,1)S(1)}, u32[]{:S(2)}, u32[]{:S(2)}) collective-permute-start(bf16[224,1792]{1,0:T(8,128)(2,1)} %bitcast.32), channel_id=1, source_target_pairs={{0,192},{32,224},{64,0},{96,32},{128,64},{160,96},{192,128},{224,1... | collective-permute-start | bytes 2408456 | tf_op jit(solution)/shard_map/tick_b/ppermute | solution.py:287
  76.8 32.9 %collective-permute-start.7 = (bf16[256,1792]{1,0:T(8,128)(2,1)}, bf16[256,1792]{1,0:T(8,128)(2,1)}, u32[]{:S(2)}, u32[]{:S(2)}) collective-permute-start(bf16[256,1792]{1,0:T(8,128)(2,1)} %collective-permute-done.4.refs_1_), channel_id=1, source_target_pairs={{0,4},{1,5},{2,6},{3,7},{4,8},{5,9},{6,10},{7,11},{8,12},{9,13},{1... | collective-permute-start | bytes 2752520 | tf_op jit(solution)/shard_map/tick_c/ppermute | solution.py:314
  76.9 32.8 %collective-permute-start.8 = (bf16[256,1792]{1,0:T(8,128)(2,1)}, bf16[256,1792]{1,0:T(8,128)(2,1)}, u32[]{:S(2)}, u32[]{:S(2)}) collective-permute-start(bf16[256,1792]{1,0:T(8,128)(2,1)} %collective-permute-done.5.refs_2_), channel_id=1, source_target_pairs={{4,0},{5,1},{6,2},{7,3},{8,4},{9,5},{10,6},{11,7},{12,8},{13,9},{1... | collective-permute-start | bytes 2752520 | tf_op jit(solution)/shard_map/tick_c/ppermute | solution.py:314
  82.9 30.6 %copy-start = (bf16[224,1792]{1,0:T(8,128)(2,1)}, bf16[224,1792]{1,0:T(8,128)(2,1)S(1)}, u32[]{:S(2)}) copy-start(bf16[224,1792]{1,0:T(8,128)(2,1)S(1)} %collective-permute-done.12.refs_1_) | copy-start | bytes 2408452
  82.9 12.1 %collective-permute-start.9 = (bf16[112,1792]{1,0:T(8,128)(2,1)}, bf16[112,1792]{1,0:T(8,128)(2,1)S(1)}, u32[]{:S(2)}, u32[]{:S(2)}) collective-permute-start(bf16[112,1792]{1,0:T(8,128)(2,1)} %get-tuple-element.95), channel_id=1, source_target_pairs={{0,64},{32,96},{64,128},{96,160},{128,192},{160,224},{192,0},{224,... | collective-permute-start | bytes 1204232 | tf_op jit(solution)/shard_map/tick_c/ppermute | solution.py:287
  83.8 29.7 %copy-start.1 = (bf16[224,1792]{1,0:T(8,128)(2,1)}, bf16[224,1792]{1,0:T(8,128)(2,1)S(1)}, u32[]{:S(2)}) copy-start(bf16[224,1792]{1,0:T(8,128)(2,1)S(1)} %collective-permute-done.13.refs_2_) | copy-start | bytes 2408452
  83.8 18.8 %collective-permute-start.10 = (bf16[112,1792]{1,0:T(8,128)(2,1)}, bf16[112,1792]{1,0:T(8,128)(2,1)S(1)}, u32[]{:S(2)}, u32[]{:S(2)}) collective-permute-start(bf16[112,1792]{1,0:T(8,128)(2,1)} %get-tuple-element.96), channel_id=1, source_target_pairs={{0,128},{32,160},{64,192},{96,224},{128,0},{160,32},{192,64},{224,... | collective-permute-start | bytes 1204232 | tf_op jit(solution)/shard_map/tick_c/ppermute | solution.py:287
  92.7 20.8 %copy-start.2 = (bf16[224,1792]{1,0:T(8,128)(2,1)}, bf16[224,1792]{1,0:T(8,128)(2,1)S(1)}, u32[]{:S(2)}) copy-start(bf16[224,1792]{1,0:T(8,128)(2,1)S(1)} %collective-permute-done.14.refs_3_) | copy-start | bytes 2408452
  92.7 17.1 %collective-permute-start.11 = (bf16[112,1792]{1,0:T(8,128)(2,1)}, bf16[112,1792]{1,0:T(8,128)(2,1)S(1)}, u32[]{:S(2)}, u32[]{:S(2)}) collective-permute-start(bf16[112,1792]{1,0:T(8,128)(2,1)} %get-tuple-element.97), channel_id=1, source_target_pairs={{0,192},{32,224},{64,0},{96,32},{128,64},{160,96},{192,128},{224,1... | collective-permute-start | bytes 1204232 | tf_op jit(solution)/shard_map/tick_c/ppermute | solution.py:287
  95.0 14.8 %copy-start.18 = (bf16[112,1792]{1,0:T(8,128)(2,1)}, bf16[112,1792]{1,0:T(8,128)(2,1)S(1)}, u32[]{:S(2)}) copy-start(bf16[112,1792]{1,0:T(8,128)(2,1)S(1)} %collective-permute-done.9.refs_1_) | copy-start | bytes 1204228
  102.6 7.2 %copy-start.19 = (bf16[112,1792]{1,0:T(8,128)(2,1)}, bf16[112,1792]{1,0:T(8,128)(2,1)S(1)}, u32[]{:S(2)}) copy-start(bf16[112,1792]{1,0:T(8,128)(2,1)S(1)} %collective-permute-done.10.refs_2_) | copy-start | bytes 1204228
  113.5 10.1 %collective-permute-start.18 = (bf16[2,224,1792]{2,1,0:T(8,128)(2,1)}, bf16[2,224,1792]{2,1,0:T(8,128)(2,1)S(1)}, u32[]{:S(2)}, u32[]{:S(2)}) collective-permute-start(bf16[2,224,1792]{2,1,0:T(8,128)(2,1)} %bitcast.20), channel_id=1, source_target_pairs={{0,1},{1,0},{2,3},{3,2},{4,5},{5,4},{6,7},{7,6},{8,9},{9,8},{10,11... | collective-permute-start | bytes 4816904 | tf_op jit(solution)/shard_map/tick_d/ppermute | solution.py:314
  115.7 25.7 %collective-permute-start.15 = (bf16[256,1792]{1,0:T(8,128)(2,1)}, bf16[256,1792]{1,0:T(8,128)(2,1)S(1)}, u32[]{:S(2)}, u32[]{:S(2)}) collective-permute-start(bf16[256,1792]{1,0:T(8,128)(2,1)} %collective-permute-done.7.refs_0_), channel_id=1, source_target_pairs={{0,4},{1,5},{2,6},{3,7},{4,8},{5,9},{6,10},{7,11},{8,12},{9,13},{1... | collective-permute-start | bytes 2752520 | tf_op jit(solution)/shard_map/tick_d/ppermute | solution.py:314
  115.7 25.7 %collective-permute-start.16 = (bf16[256,1792]{1,0:T(8,128)(2,1)}, bf16[256,1792]{1,0:T(8,128)(2,1)}, u32[]{:S(2)}, u32[]{:S(2)}) collective-permute-start(bf16[256,1792]{1,0:T(8,128)(2,1)} %collective-permute-done.8.refs_1_), channel_id=1, source_target_pairs={{4,0},{5,1},{6,2},{7,3},{8,4},{9,5},{10,6},{11,7},{12,8},{13,9},{1... | collective-permute-start | bytes 2752520 | tf_op jit(solution)/shard_map/tick_d/ppermute | solution.py:314
  121.0 20.4 %collective-permute-start.17 = (bf16[2,224,896]{2,1,0:T(8,128)(2,1)}, bf16[2,224,896]{2,1,0:T(8,128)(2,1)S(1)}, u32[]{:S(2)}, u32[]{:S(2)}) collective-permute-start(bf16[2,224,896]{2,1,0:T(8,128)(2,1)} %tick_d.4), channel_id=1, source_target_pairs={{0,32},{32,0},{64,96},{96,64},{128,160},{160,128},{192,224},{224,1... | collective-permute-start | bytes 2408456 | tf_op jit(solution)/shard_map/tick_d/ppermute | solution.py:317
  123.6 1.2 copy-start.5
  141.4 3.9 %copy-start.21 = (bf16[256,1792]{1,0:T(8,128)(2,1)}, bf16[256,1792]{1,0:T(8,128)(2,1)S(1)}, u32[]{:S(2)}) copy-start(bf16[256,1792]{1,0:T(8,128)(2,1)S(1)} %collective-permute-done.15.refs_2_) | copy-start | bytes 2752516
  145.3 31.4 %all-to-all-start.1 = ((bf16[4,224,896]{2,1,0:T(8,128)(2,1)}), bf16[4,224,896]{2,1,0:T(8,128)(2,1)S(1)}, u32[]{:S(2)}, u32[]{:S(2)}) async-start(bf16[4,224,896]{2,1,0:T(8,128)(2,1)} %tick_e.5), calls=%async_computation.1 | async-start | bytes 3211264 | tf_op jit(solution)/shard_map/tick_e/all_to_all | solution.py:324
  152.4 24.4 %collective-permute-start.21 = (bf16[2,224,896]{2,1,0:T(8,128)(2,1)}, bf16[2,224,896]{2,1,0:T(8,128)(2,1)S(1)}, u32[]{:S(2)}, u32[]{:S(2)}) collective-permute-start(bf16[2,224,896]{2,1,0:T(8,128)(2,1)} %tick_e.3), channel_id=1, source_target_pairs={{0,32},{32,0},{64,96},{96,64},{128,160},{160,128},{192,224},{224,1... | collective-permute-start | bytes 2408456 | tf_op jit(solution)/shard_map/tick_e/ppermute | solution.py:317
  157.2 19.5 %collective-permute-start.19 = (bf16[128,1792]{1,0:T(8,128)(2,1)S(1)}, bf16[128,1792]{1,0:T(8,128)(2,1)S(1)}, u32[]{:S(2)}, u32[]{:S(2)}) collective-permute-start(bf16[128,1792]{1,0:T(8,128)(2,1)S(1)} %slice.22), channel_id=1, source_target_pairs={{0,4},{1,5},{2,6},{3,7},{4,8},{5,9},{6,10},{7,11},{8,12},{9,13},{1... | collective-permute-start | bytes 1376264 | tf_op jit(solution)/shard_map/tick_e/ppermute | solution.py:314
  157.3 19.4 %collective-permute-start.20 = (bf16[128,1792]{1,0:T(8,128)(2,1)S(1)}, bf16[128,1792]{1,0:T(8,128)(2,1)}, u32[]{:S(2)}, u32[]{:S(2)}) collective-permute-start(bf16[128,1792]{1,0:T(8,128)(2,1)S(1)} %slice.23), channel_id=1, source_target_pairs={{4,0},{5,1},{6,2},{7,3},{8,4},{9,5},{10,6},{11,7},{12,8},{13,9},{1... | collective-permute-start | bytes 1376264 | tf_op jit(solution)/shard_map/tick_e/ppermute | solution.py:314
  176.7 8.3 %copy-start.17 = (bf16[128,1792]{1,0:T(8,128)(2,1)}, bf16[128,1792]{1,0:T(8,128)(2,1)S(1)}, u32[]{:S(2)}) copy-start(bf16[128,1792]{1,0:T(8,128)(2,1)S(1)} %collective-permute-done.19.refs_0_) | copy-start | bytes 1376260
  176.7 3.9 %copy-start.3 = (bf16[4,224,896]{2,1,0:T(8,128)(2,1)}, bf16[4,224,896]{2,1,0:T(8,128)(2,1)S(1)}, u32[]{:S(2)}) copy-start(bf16[4,224,896]{2,1,0:T(8,128)(2,1)S(1)} %all-to-all-done.1.refs_0_) | copy-start | bytes 4816900
  180.6 23.4 %all-to-all-start.2 = ((bf16[4,224,896]{2,1,0:T(8,128)(2,1)}), bf16[4,224,896]{2,1,0:T(8,128)(2,1)S(1)}, u32[]{:S(2)}, u32[]{:S(2)}) async-start(bf16[4,224,896]{2,1,0:T(8,128)(2,1)} %tick_f.2), calls=%async_computation.2 | async-start | bytes 3211264 | tf_op jit(solution)/shard_map/tick_f/all_to_all | solution.py:324
  185.0 14.0 %copy-start.22 = (s32[8]{0:T(128)S(1)}, s32[8]{0:T(128)}, u32[]{:S(2)}) copy-start(s32[8]{0:T(128)} %param.19) | copy-start | bytes 100
  194.9 5.6 %collective-permute-start.22 = (f32[224,896]{1,0:T(8,128)}, f32[224,896]{1,0:T(8,128)S(1)}, u32[]{:S(2)}, u32[]{:S(2)}) collective-permute-start(f32[224,896]{1,0:T(8,128)} %get-tuple-element.154), channel_id=1, source_target_pairs={{0,1},{1,0},{2,3},{3,2},{4,5},{5,4},{6,7},{7,6},{8,9},{9,8},{10,11... | collective-permute-start | bytes 2408456 | tf_op jit(solution)/shard_map/tick_f/ppermute | solution.py:314
  198.3 4.4 %collective-permute-start.23 = (f32[224,896]{1,0:T(8,128)}, f32[224,896]{1,0:T(8,128)S(1)}, u32[]{:S(2)}, u32[]{:S(2)}) collective-permute-start(f32[224,896]{1,0:T(8,128)} %get-tuple-element.155), channel_id=1, source_target_pairs={{0,1},{1,0},{2,3},{3,2},{4,5},{5,4},{6,7},{7,6},{8,9},{9,8},{10,11... | collective-permute-start | bytes 2408456 | tf_op jit(solution)/shard_map/tick_f/ppermute | solution.py:314
  198.4 4.5 %collective-permute-start.24 = (f32[224,896]{1,0:T(8,128)}, f32[224,896]{1,0:T(8,128)}, u32[]{:S(2)}, u32[]{:S(2)}) collective-permute-start(f32[224,896]{1,0:T(8,128)} %get-tuple-element.156), channel_id=1, source_target_pairs={{0,1},{1,0},{2,3},{3,2},{4,5},{5,4},{6,7},{7,6},{8,9},{9,8},{10,11... | collective-permute-start | bytes 2408456 | tf_op jit(solution)/shard_map/tick_f/ppermute | solution.py:314
  198.8 5.2 %collective-permute-start.25 = (f32[224,896]{1,0:T(8,128)}, f32[224,896]{1,0:T(8,128)}, u32[]{:S(2)}, u32[]{:S(2)}) collective-permute-start(f32[224,896]{1,0:T(8,128)} %get-tuple-element.157), channel_id=1, source_target_pairs={{0,1},{1,0},{2,3},{3,2},{4,5},{5,4},{6,7},{7,6},{8,9},{9,8},{10,11... | collective-permute-start | bytes 2408456 | tf_op jit(solution)/shard_map/tick_f/ppermute | solution.py:314
  200.5 3.6 %copy-start.9 = (f32[224,896]{1,0:T(8,128)}, f32[224,896]{1,0:T(8,128)S(1)}, u32[]{:S(2)}) copy-start(f32[224,896]{1,0:T(8,128)S(1)} %collective-permute-done.22.refs_4_) | copy-start | bytes 2408452
  202.8 1.3 copy-start.10
  204.1 1.2 copy-start.4
  (4 other events, 3.3 us)

commit v6 on v5

--- a/solution.py
+++ b/solution.py
@@ -175,7 +175,7 @@
         grad = (kept[p][...] + sent) * scale
         first_new = 0.9 * moment(p) + 0.1 * grad
         second_new = 0.95 * moment(2 + p) + 0.05 * grad * grad
-        update = learning * (first_new / bias_first) / (jnp.sqrt(second_new / bias_second) + 1e-08)
+        update = learning * first_new / (jnp.sqrt(second_new * (1.0 / bias_second)) + 1e-08)
         outs[p][0] = (w_ref[p].astype(jnp.float32) - update).astype(jnp.bfloat16)
         outs[2 + p][0] = first_new.astype(jnp.bfloat16)
         outs[4 + p][0] = second_new.astype(jnp.bfloat16)
@@ -308,7 +308,7 @@
     learning = 0.2 * jnp.exp2(
         (rate_index[lax.axis_index("member")].astype(jnp.float32) - 2.0) * 0.5
     )
-    rate = jnp.full((1,), learning, jnp.float32)
+    rate = jnp.full((1,), learning / bias_first, jnp.float32)
 
     def fsdp(value, pairs):
         return lax.ppermute(value, "fsdp", pairs)
@@ -334,8 +334,8 @@
     spans = [(0, width // 2), (width // 2, width // 2)]
     weights = [w[0, k * half : (k + 1) * half] for w in (gate_weight, up_weight) for k in range(2)]
     moments = [m[0] for m in (gate_first, up_first, gate_second, up_second)]
-    turned = cotangent[0].T.reshape(16, 2 * hidden, count)
     with jax.named_scope("tick_a"):
+        turned = cotangent[0].T.reshape(16, 2 * hidden, count)
         cots = lax.all_to_all(turned, "fsdp", 0, 0, axis_index_groups=same_core, tiled=True)
         start = jnp.concatenate([own, fsdp(own, low_swap)])
         held0 = [weights[0], *spread(weights)]
@@ -348,19 +348,21 @@
     with jax.named_scope("tick_c"):
         up2, down2 = fsdp(up1, z_up), fsdp(down1, z_down)
         got0 = gathered(held0, came0)
-    up2, down2, got0, held1 = sync((up2, down2, got0, held1))
+        sent1 = pick("cross", here, winner, held1, spans[0])
+    up2, down2, got0, held1, sent1 = sync((up2, down2, got0, held1, sent1))
     with jax.named_scope("tick_d"):
         up3, down3 = fsdp(up2, z_up), fsdp(down2, z_down)
-        came1 = exchange(held1, spans[0])
+        came1 = lax.ppermute(sent1, "member", row_swap)
+        sent2 = pick("cross", here, winner, held1, spans[1])
         mine = pick("place", here, winner, got0).reshape(2, hidden, width)
         theirs = fsdp(mine, core_swap)
         sources = [(d, b) for d in (0, -1, 1) for b in range(2)]
         sums = terms(here, mine, theirs, cots, [start, up1, down1], sources, None, scale)
-    up3, down3, came1, sums, held1 = sync((up3, down3, came1, sums, held1))
+    up3, down3, came1, sums, held1, sent2 = sync((up3, down3, came1, sums, held1, sent2))
     with jax.named_scope("tick_e"):
         sides = [fsdp(up3[:count], z_up), fsdp(down3[count:], z_down)]
         got1 = columns(held1, came1, spans[0])
-        came2 = exchange(held1, spans[1])
+        came2 = lax.ppermute(sent2, "member", row_swap)
         sources = [(d, b) for d in (-2, 2, -3, 3) for b in range(2)]
         sums = terms(here, mine, theirs, cots, [up2, down2, up3, down3], sources, sums, scale)
     sides, came2, sums, got1, held1 = sync((sides, came2, sums, got1, held1))

time: 218 us -> 215 us (0.986)
  waiting for transfers between devices: 68.8 us -> 64.1 us
    ppermute x3 -> x1, starting transfers between devices: 8.01 us -> 2.71 us  [exchange(): lax.ppermute(pick('cross', here, winner, held, span), 'member', row_swap)]
    ppermute x0 -> x2, starting transfers between devices: none -> 4.79 us  [the longest x1 2.47 us: body(): came1 = lax.ppermute(sent1, 'member', row_swap)]
    ppermute x9, waiting for transfers between devices: 28.6 us -> 25.9 us  [spread(): return [lax.ppermute(pieces[j], 'member', along_row(j)) for j in (1, 2, 3)]]
    ppermute x3 -> x1, waiting for transfers between devices: 28.5 us -> 26 us  [exchange(): lax.ppermute(pick('cross', here, winner, held, span), 'member', row_swap)]
    unnamed x46 -> x48, local copies, waits for them, and re-layouts: 5.71 us -> 5.77 us
  transfers between devices with their start and end apart: 29 -> 29, of which waited for: 13 -> 14; matrix products, arithmetic and copies ran while one was open for 2% -> 3% of each run, Pallas kernels for 24% -> 25%
where the time goes in v6:
time: 215 us; the launch traced here: 211 us
  Pallas kernels  71.1 us (33%)
  waiting for transfers between devices  64.1 us (30%)
  starting transfers between devices  58.4 us (27%)
  local copies, waits for them, and re-layouts  13.9 us (6%)
    pallas_call x3, Pallas kernels, terms(): pl.pallas_call(kernel, in_specs=[pl.BlockSpec(memory_space=pltpu.SMEM)] +...  40.6 us
    ppermute x1, waiting for transfers between devices, exchange(): lax.ppermute(pick('cross', here, winner, held, span), 'member', row_swap)  26 us
    ppermute x9, waiting for transfers between devices, spread(): return [lax.ppermute(pieces[j], 'member', along_row(j)) for j in (1, 2, 3)]  25.9 us
    pallas_call x7, Pallas kernels, pick(): pl.pallas_call(functools.partial(pick_kernel, mode, span), in_specs=[smem...  20.3 us
    ppermute x14, starting transfers between devices, fsdp(): return lax.ppermute(value, 'fsdp', pairs)  17.4 us
    ppermute x9, starting transfers between devices, spread(): return [lax.ppermute(pieces[j], 'member', along_row(j)) for j in (1, 2, 3)]  14.2 us
    ppermute x14, waiting for transfers between devices, fsdp(): return lax.ppermute(value, 'fsdp', pairs)  11.8 us
    all_to_all x1, starting transfers between devices, body(): lax.all_to_all(turned, 'fsdp', 0, 0, axis_index_groups=same_core, tiled=T...  10.3 us
  transfers between devices with their start and end apart: 29, of which 14 were waited for; matrix products, arithmetic and copies ran while one was open for 3% of the time, Pallas kernels for 25%

profile of v6, /device:TPU:1, one launch (start us, length us, event | category | flops | bytes accessed | tf_op | source)
XLA Modules:
  0.0 211.0 jit_solution(9565108705779141684)
XLA Ops:
  0.6 3.9 %copy.16 = bf16[7168,128]{1,0:T(8,128)(2,1)} copy(bf16[7168,128]{0,1:T(8,128)(2,1)} %bitcast.29) | data formatting | bytes 3670016 | tf_op jit(solution)/shard_map/tick_a/transpose | solution.py:338
  4.5 10.3 %all-to-all-start = ((bf16[16,448,128]{2,1,0:T(8,128)(2,1)}), bf16[16,448,128]{2,1,0:T(8,128)(2,1)}, u32[]{:S(2)}, u32[]{:S(2)}) async-start(bf16[16,448,128]{2,1,0:T(8,128)(2,1)} %bitcast.13), calls=%async_computation | async-start | bytes 3670016 | tf_op jit(solution)/shard_map/tick_a/all_to_all | solution.py:339
  14.8 1.4 collective-permute-start
  17.1 1.2 collective-permute-start.1
  18.3 1.5 collective-permute-start.3
  19.9 1.5 collective-permute-start.2
  22.1 6.5 %collective-permute-done = bf16[128,1792]{1,0:T(8,128)(2,1)S(1)} collective-permute-done((bf16[128,1792]{1,0:T(8,128)(2,1)S(1)}, bf16[128,1792]{1,0:T(8,128)(2,1)S(1)}, u32[]{:S(2)}, u32[]{:S(2)}) %collective-permute-start) | collective-permute-done | bytes 458784 | tf_op jit(solution)/shard_map/tick_a/ppermute | solution.py:314
  28.5 1.0 pad_maximum_fusion.refs_0_
  29.6 7.6 %collective-permute-done.2.refs_2_ = bf16[112,1792]{1,0:T(8,128)(2,1)S(1)} collective-permute-done((bf16[112,1792]{1,0:T(8,128)(2,1)S(1)}, bf16[112,1792]{1,0:T(8,128)(2,1)S(1)}, u32[]{:S(2)}, u32[]{:S(2)}) %collective-permute-start.2) | collective-permute-done | bytes 401440 | tf_op jit(solution)/shard_map/tick_a/ppermute | solution.py:287
  38.0 2.6 %tick_b.1 = bf16[2,112,1792]{2,1,0:T(8,128)(2,1)} custom-call(s32[2]{0:T(128)} %pad_add_fusion.here, s32[8]{0:T(128)} %winner.15, bf16[112,1792]{1,0:T(8,128)(2,1)} %get-tuple-element.91.refs_0_, bf16[112,1792]{1,0:T(8,128)(2,1)} %copy-done.6, bf16[112,1792]{1,0:T(8,128)(2,1)} %copy-done.8, bf16[112,1792]{1,0:T(8,128)(2,1)} %copy-done.7), custom_call_target="tpu_custom_call" | custom-call | bytes 1605632 | tf_op jit(solution)/shard_map/tick_b/pallas_call | solution.py:270
  40.6 2.7 %collective-permute-start.6 = (bf16[2,112,1792]{2,1,0:T(8,128)(2,1)}, bf16[2,112,1792]{2,1,0:T(8,128)(2,1)S(1)}, u32[]{:S(2)}, u32[]{:S(2)}) collective-permute-start(bf16[2,112,1792]{2,1,0:T(8,128)(2,1)} %tick_b.1), channel_id=1, source_target_pairs={{0,32},{32,0},{64,96},{96,64},{128,160},{160,128},{192,224},{224,1... | collective-permute-start | bytes 2408456 | tf_op jit(solution)/shard_map/tick_b/ppermute | solution.py:317
  43.3 2.3 %collective-permute-start.5 = (bf16[256,1792]{1,0:T(8,128)(2,1)}, bf16[256,1792]{1,0:T(8,128)(2,1)}, u32[]{:S(2)}, u32[]{:S(2)}) collective-permute-start(bf16[256,1792]{1,0:T(8,128)(2,1)} %pad_maximum_fusion.refs_0_), channel_id=1, source_target_pairs={{4,0},{5,1},{6,2},{7,3},{8,4},{9,5},{10,6},{11,7},{12,8},{13,9},{1... | collective-permute-start | bytes 2752520 | tf_op jit(solution)/shard_map/tick_b/ppermute | solution.py:314
  46.5 1.7 collective-permute-start.13
  48.1 26.0 %collective-permute-done.6.refs_4_ = bf16[2,112,1792]{2,1,0:T(8,128)(2,1)S(1)} collective-permute-done((bf16[2,112,1792]{2,1,0:T(8,128)(2,1)}, bf16[2,112,1792]{2,1,0:T(8,128)(2,1)S(1)}, u32[]{:S(2)}, u32[]{:S(2)}) %collective-permute-start.6) | collective-permute-done | bytes 802848 | tf_op jit(solution)/shard_map/tick_b/ppermute | solution.py:317
  74.1 1.5 collective-permute-start.14
  75.9 0.9 collective-permute-done.4.refs_1_
  76.9 2.6 %collective-permute-start.8 = (bf16[256,1792]{1,0:T(8,128)(2,1)}, bf16[256,1792]{1,0:T(8,128)(2,1)}, u32[]{:S(2)}, u32[]{:S(2)}) collective-permute-start(bf16[256,1792]{1,0:T(8,128)(2,1)} %collective-permute-done.5.refs_2_), channel_id=1, source_target_pairs={{4,0},{5,1},{6,2},{7,3},{8,4},{9,5},{10,6},{11,7},{12,8},{13,9},{1... | collective-permute-start | bytes 2752520 | tf_op jit(solution)/shard_map/tick_c/ppermute | solution.py:314
  79.5 3.3 %tick_c.2 = (bf16[112,1792]{1,0:T(8,128)(2,1)}, bf16[112,1792]{1,0:T(8,128)(2,1)}, bf16[112,1792]{1,0:T(8,128)(2,1)}, bf16[112,1792]{1,0:T(8,128)(2,1)}) custom-call(s32[2]{0:T(128)} %pad_add_fusion.here, s32[8]{0:T(128)} %winner.15, bf16[112,1792]{1,0:T(8,128)(2,1)} %get-tuple-element.91.refs_0_, bf16[112,1792]{1,0:T(8,128)(2,1)} %copy-done.6, ...), custom_call_target="tpu_custom_call" | custom-call | bytes 3211264 | tf_op jit(solution)/shard_map/tick_c/pallas_call | solution.py:270
  82.9 1.3 collective-permute-start.9
  84.1 2.3 %collective-permute-start.10 = (bf16[112,1792]{1,0:T(8,128)(2,1)}, bf16[112,1792]{1,0:T(8,128)(2,1)S(1)}, u32[]{:S(2)}, u32[]{:S(2)}) collective-permute-start(bf16[112,1792]{1,0:T(8,128)(2,1)} %get-tuple-element.98), channel_id=1, source_target_pairs={{0,128},{32,160},{64,192},{96,224},{128,0},{160,32},{192,64},{224,... | collective-permute-start | bytes 1204232 | tf_op jit(solution)/shard_map/tick_c/ppermute | solution.py:287
  86.5 6.2 %collective-permute-done.14.refs_3_ = bf16[224,1792]{1,0:T(8,128)(2,1)S(1)} collective-permute-done((bf16[224,1792]{1,0:T(8,128)(2,1)}, bf16[224,1792]{1,0:T(8,128)(2,1)S(1)}, u32[]{:S(2)}, u32[]{:S(2)}) %collective-permute-start.14) | collective-permute-done | bytes 802848 | tf_op jit(solution)/shard_map/tick_b/ppermute | solution.py:287
  92.7 2.3 %collective-permute-start.11 = (bf16[112,1792]{1,0:T(8,128)(2,1)}, bf16[112,1792]{1,0:T(8,128)(2,1)S(1)}, u32[]{:S(2)}, u32[]{:S(2)}) collective-permute-start(bf16[112,1792]{1,0:T(8,128)(2,1)} %get-tuple-element.99), channel_id=1, source_target_pairs={{0,192},{32,224},{64,0},{96,32},{128,64},{160,96},{192,128},{224,1... | collective-permute-start | bytes 1204232 | tf_op jit(solution)/shard_map/tick_c/ppermute | solution.py:287
  95.0 2.6 %tick_c.3 = bf16[2,224,896]{2,1,0:T(8,128)(2,1)} custom-call(s32[2]{0:T(128)} %pad_add_fusion.here, s32[8]{0:T(128)} %winner.15, bf16[224,1792]{1,0:T(8,128)(2,1)} %bitcast.25, bf16[224,1792]{1,0:T(8,128)(2,1)} %copy-done, bf16[224,1792]{1,0:T(8,128)(2,1)} %copy-done.1, bf16[224,1792]{1,0:T(8,128)(2,1)} %copy-done.2), custom_call_target="tpu_custom_call" | custom-call | bytes 3211264 | tf_op jit(solution)/shard_map/tick_c/pallas_call | solution.py:270
  97.7 4.9 %collective-permute-done.10.refs_2_ = bf16[112,1792]{1,0:T(8,128)(2,1)S(1)} collective-permute-done((bf16[112,1792]{1,0:T(8,128)(2,1)}, bf16[112,1792]{1,0:T(8,128)(2,1)S(1)}, u32[]{:S(2)}, u32[]{:S(2)}) %collective-permute-start.10) | collective-permute-done | bytes 401440 | tf_op jit(solution)/shard_map/tick_c/ppermute | solution.py:287
  102.6 7.2 %collective-permute-done.11.refs_3_ = bf16[112,1792]{1,0:T(8,128)(2,1)S(1)} collective-permute-done((bf16[112,1792]{1,0:T(8,128)(2,1)}, bf16[112,1792]{1,0:T(8,128)(2,1)S(1)}, u32[]{:S(2)}, u32[]{:S(2)}) %collective-permute-start.11) | collective-permute-done | bytes 401440 | tf_op jit(solution)/shard_map/tick_c/ppermute | solution.py:287
  110.5 3.1 %tick_d.3 = bf16[4,112,1792]{2,1,0:T(8,128)(2,1)} custom-call(s32[2]{0:T(128)} %pad_add_fusion.here, s32[8]{0:T(128)} %winner.15, bf16[112,1792]{1,0:T(8,128)(2,1)} %get-tuple-element.104.refs_0_, bf16[112,1792]{1,0:T(8,128)(2,1)} %copy-done.19, bf16[112,1792]{1,0:T(8,128)(2,1)} %copy-done.20, bf16[112,1792]{1,0:T(8,128)(2,1)} %copy-done.21), custom_call_target="tpu_custom_call" | custom-call | bytes 3211264 | tf_op jit(solution)/shard_map/tick_d/pallas_call | solution.py:270
  113.6 2.4 %collective-permute-start.18 = (bf16[2,224,1792]{2,1,0:T(8,128)(2,1)}, bf16[2,224,1792]{2,1,0:T(8,128)(2,1)S(1)}, u32[]{:S(2)}, u32[]{:S(2)}) collective-permute-start(bf16[2,224,1792]{2,1,0:T(8,128)(2,1)} %bitcast.20), channel_id=1, source_target_pairs={{0,1},{1,0},{2,3},{3,2},{4,5},{5,4},{6,7},{7,6},{8,9},{9,8},{10,11... | collective-permute-start | bytes 4816904 | tf_op jit(solution)/shard_map/tick_d/ppermute | solution.py:314
  116.0 2.7 %collective-permute-start.16 = (bf16[256,1792]{1,0:T(8,128)(2,1)}, bf16[256,1792]{1,0:T(8,128)(2,1)}, u32[]{:S(2)}, u32[]{:S(2)}) collective-permute-start(bf16[256,1792]{1,0:T(8,128)(2,1)} %collective-permute-done.8.refs_1_), channel_id=1, source_target_pairs={{4,0},{5,1},{6,2},{7,3},{8,4},{9,5},{10,6},{11,7},{12,8},{13,9},{1... | collective-permute-start | bytes 2752520 | tf_op jit(solution)/shard_map/tick_d/ppermute | solution.py:314
  118.7 2.5 %collective-permute-start.17 = (bf16[2,224,896]{2,1,0:T(8,128)(2,1)S(1)}, bf16[2,224,896]{2,1,0:T(8,128)(2,1)S(1)}, u32[]{:S(2)}, u32[]{:S(2)}) collective-permute-start(bf16[2,224,896]{2,1,0:T(8,128)(2,1)S(1)} %copy-done.16), channel_id=1, source_target_pairs={{0,32},{32,0},{64,96},{96,64},{128,160},{160,128},{192,224},{224,1... | collective-permute-start | bytes 2408456 | tf_op jit(solution)/shard_map/tick_d/ppermute | solution.py:355
  121.1 2.6 %tick_d.5 = bf16[2,224,896]{2,1,0:T(8,128)(2,1)} custom-call(s32[2]{0:T(128)} %pad_add_fusion.here, s32[8]{0:T(128)} %winner.15, bf16[224,1792]{1,0:T(8,128)(2,1)} %bitcast.26, bf16[224,1792]{1,0:T(8,128)(2,1)} %copy-done, bf16[224,1792]{1,0:T(8,128)(2,1)} %copy-done.1, bf16[224,1792]{1,0:T(8,128)(2,1)} %copy-done.2), custom_call_target="tpu_custom_call" | custom-call | bytes 3211264 | tf_op jit(solution)/shard_map/tick_d/pallas_call | solution.py:270
  123.8 1.2 copy-done.5
  125.0 14.1 %tick_d.4 = (f32[224,1792]{1,0:T(8,128)}, f32[224,1792]{1,0:T(8,128)}, f32[224,896]{1,0:T(8,128)}, f32[224,896]{1,0:T(8,128)}, f32[224,896]{1,0:T(8,128)}, /*index=5*/f32[224,896]{1,0:T(8,128)}) custom-call(s32[2]{0:T(128)} %pad_add_fusion.here, bf16[2,224,1792]{2,1,0:T(8,128)(2,1)} %bitcast.21, bf16[2,224,1792]{2,1,0:T(8,128)(2,1)} %copy-done.5, ...), custom_call_target="tpu_custom_call" | custom-call | flops 4932501504 | bytes 20971520 | tf_op jit(solution)/shard_map/tick_d/pallas_call | solution.py:137
  140.3 3.0 %tick_e.3 = bf16[4,224,896]{2,1,0:T(8,128)(2,1)} custom-call(s32[2]{0:T(128)} %pad_add_fusion.here, s32[8]{0:T(128)} %winner.15, bf16[224,1792]{1,0:T(8,128)(2,1)} %bitcast.27, bf16[224,1792]{1,0:T(8,128)(2,1)} %copy-done, bf16[224,1792]{1,0:T(8,128)(2,1)} %copy-done.1, bf16[224,1792]{1,0:T(8,128)(2,1)} %copy-done.2, bf16[2,224,896]{2,1,0:T(8,128)(2,1)} %copy-done.12), custom_call_target="tpu_custom_call" | custom-call | bytes 6422528 | tf_op jit(solution)/shard_map/tick_e/pallas_call | solution.py:270
  143.3 4.8 %all-to-all-start.1 = ((bf16[4,224,896]{2,1,0:T(8,128)(2,1)}), bf16[4,224,896]{2,1,0:T(8,128)(2,1)S(1)}, u32[]{:S(2)}, u32[]{:S(2)}) async-start(bf16[4,224,896]{2,1,0:T(8,128)(2,1)} %tick_e.3), calls=%async_computation.1 | async-start | bytes 3211264 | tf_op jit(solution)/shard_map/tick_e/all_to_all | solution.py:324
  148.1 2.3 %collective-permute-start.21 = (bf16[2,224,896]{2,1,0:T(8,128)(2,1)S(1)}, bf16[2,224,896]{2,1,0:T(8,128)(2,1)S(1)}, u32[]{:S(2)}, u32[]{:S(2)}) collective-permute-start(bf16[2,224,896]{2,1,0:T(8,128)(2,1)S(1)} %copy-done.15), channel_id=1, source_target_pairs={{0,32},{32,0},{64,96},{96,64},{128,160},{160,128},{192,224},{224,1... | collective-permute-start | bytes 2408456 | tf_op jit(solution)/shard_map/tick_e/ppermute | solution.py:365
  150.4 1.0 slice.22
  151.5 1.8 slice.23
  153.3 2.7 %collective-permute-start.20 = (bf16[128,1792]{1,0:T(8,128)(2,1)}, bf16[128,1792]{1,0:T(8,128)(2,1)}, u32[]{:S(2)}, u32[]{:S(2)}) collective-permute-start(bf16[128,1792]{1,0:T(8,128)(2,1)} %slice.23), channel_id=1, source_target_pairs={{4,0},{5,1},{6,2},{7,3},{8,4},{9,5},{10,6},{11,7},{12,8},{13,9},{1... | collective-permute-start | bytes 1376264 | tf_op jit(solution)/shard_map/tick_e/ppermute | solution.py:314
  156.0 16.7 %tick_e.2 = (f32[224,1792]{1,0:T(8,128)}, f32[224,1792]{1,0:T(8,128)}, f32[224,896]{1,0:T(8,128)}, f32[224,896]{1,0:T(8,128)}, f32[224,896]{1,0:T(8,128)}, /*index=5*/f32[224,896]{1,0:T(8,128)}) custom-call(s32[2]{0:T(128)} %pad_add_fusion.here, bf16[2,224,1792]{2,1,0:T(8,128)(2,1)} %bitcast.22, bf16[2,224,1792]{2,1,0:T(8,128)(2,1)} %copy-done.5, ...), custom_call_target="tpu_custom_call" | custom-call | flops 6576668672 | bytes 20971520 | tf_op jit(solution)/shard_map/tick_e/pallas_call | solution.py:137
  172.8 0.9 copy-done.11
  173.7 3.0 %tick_f.2 = bf16[4,224,896]{2,1,0:T(8,128)(2,1)} custom-call(s32[2]{0:T(128)} %pad_add_fusion.here, s32[8]{0:T(128)} %winner.15, bf16[224,1792]{1,0:T(8,128)(2,1)} %bitcast.28, bf16[224,1792]{1,0:T(8,128)(2,1)} %copy-done, bf16[224,1792]{1,0:T(8,128)(2,1)} %copy-done.1, bf16[224,1792]{1,0:T(8,128)(2,1)} %copy-done.2, bf16[2,224,896]{2,1,0:T(8,128)(2,1)} %copy-done.11), custom_call_target="tpu_custom_call" | custom-call | bytes 6422528 | tf_op jit(solution)/shard_map/tick_f/pallas_call | solution.py:270
  176.6 4.2 %all-to-all-start.2 = ((bf16[4,224,896]{2,1,0:T(8,128)(2,1)}), bf16[4,224,896]{2,1,0:T(8,128)(2,1)S(1)}, u32[]{:S(2)}, u32[]{:S(2)}) async-start(bf16[4,224,896]{2,1,0:T(8,128)(2,1)} %tick_f.2), calls=%async_computation.2 | async-start | bytes 3211264 | tf_op jit(solution)/shard_map/tick_f/all_to_all | solution.py:324
  180.8 9.8 %tick_f.3 = (f32[224,1792]{1,0:T(8,128)}, f32[224,1792]{1,0:T(8,128)}, f32[224,896]{1,0:T(8,128)}, f32[224,896]{1,0:T(8,128)}, f32[224,896]{1,0:T(8,128)}, /*index=5*/f32[224,896]{1,0:T(8,128)}) custom-call(s32[2]{0:T(128)} %pad_add_fusion.here, bf16[2,224,1792]{2,1,0:T(8,128)(2,1)} %bitcast.23, bf16[2,224,1792]{2,1,0:T(8,128)(2,1)} %copy-done.5, ...), custom_call_target="tpu_custom_call" | custom-call | flops 1644167168 | bytes 20971520 | tf_op jit(solution)/shard_map/tick_f/pallas_call | solution.py:137
  190.7 2.6 %collective-permute-start.22 = (f32[224,896]{1,0:T(8,128)}, f32[224,896]{1,0:T(8,128)S(1)}, u32[]{:S(2)}, u32[]{:S(2)}) collective-permute-start(f32[224,896]{1,0:T(8,128)} %get-tuple-element.158), channel_id=1, source_target_pairs={{0,1},{1,0},{2,3},{3,2},{4,5},{5,4},{6,7},{7,6},{8,9},{9,8},{10,11... | collective-permute-start | bytes 2408456 | tf_op jit(solution)/shard_map/tick_f/ppermute | solution.py:314
  195.4 2.3 %collective-permute-done.23.refs_5_ = f32[224,896]{1,0:T(8,128)S(1)} collective-permute-done((f32[224,896]{1,0:T(8,128)}, f32[224,896]{1,0:T(8,128)S(1)}, u32[]{:S(2)}, u32[]{:S(2)}) %collective-permute-start.23) | collective-permute-done | bytes 802848 | tf_op jit(solution)/shard_map/tick_f/ppermute | solution.py:314
  197.9 1.1 collective-permute-done.25.refs_7_
  199.4 1.2 copy-done.4
  200.6 10.2 %adam.1 = (bf16[1,224,1792]{2,1,0:T(8,128)(2,1)}, bf16[1,224,1792]{2,1,0:T(8,128)(2,1)}, bf16[1,224,1792]{2,1,0:T(8,128)(2,1)}, bf16[1,224,1792]{2,1,0:T(8,128)(...) custom-call(s32[2]{0:T(128)} %pad_add_fusion.here, s32[8]{0:T(128)} %winner.15, f32[1]{0:T(128)S(6)} %div.4.rate, ...), custom_call_target="tpu_custom_call" | custom-call | tf_op jit(solution)/shard_map/adam/pallas_call | solution.py:192
  (77 shorter events, 7.5 us)
Async XLA Ops:
  4.5 10.3 %copy-start.18 = (bf16[1,128,1792]{2,1,0:T(8,128)(2,1)S(1)}, bf16[1,128,1792]{2,1,0:T(8,128)(2,1)}, u32[]{:S(2)}) copy-start(bf16[1,128,1792]{2,1,0:T(8,128)(2,1)} %param.10) | copy-start | bytes 1376260
  4.5 11.7 %copy-start.13 = (bf16[1,224,1792]{2,1,0:T(8,128)(2,1)S(1)}, bf16[1,224,1792]{2,1,0:T(8,128)(2,1)}, u32[]{:S(2)}) copy-start(bf16[1,224,1792]{2,1,0:T(8,128)(2,1)} %param.12) | copy-start | bytes 2408452
  4.5 72.3 %all-to-all-start = ((bf16[16,448,128]{2,1,0:T(8,128)(2,1)}), bf16[16,448,128]{2,1,0:T(8,128)(2,1)}, u32[]{:S(2)}, u32[]{:S(2)}) async-start(bf16[16,448,128]{2,1,0:T(8,128)(2,1)} %bitcast.13), calls=%async_computation | async-start | bytes 3670016 | tf_op jit(solution)/shard_map/tick_a/all_to_all | solution.py:339
  14.8 3.4 %copy-start.14 = (bf16[1,224,1792]{2,1,0:T(8,128)(2,1)S(1)}, bf16[1,224,1792]{2,1,0:T(8,128)(2,1)}, u32[]{:S(2)}) copy-start(bf16[1,224,1792]{2,1,0:T(8,128)(2,1)} %param.13) | copy-start | bytes 2408452
  14.8 13.7 %collective-permute-start = (bf16[128,1792]{1,0:T(8,128)(2,1)S(1)}, bf16[128,1792]{1,0:T(8,128)(2,1)S(1)}, u32[]{:S(2)}, u32[]{:S(2)}) collective-permute-start(bf16[128,1792]{1,0:T(8,128)(2,1)S(1)} %bitcast.30), channel_id=1, source_target_pairs={{0,2},{1,3},{2,0},{3,1},{4,6},{5,7},{6,4},{7,5},{8,10},{9,11},{10,... | collective-permute-start | bytes 1376264 | tf_op jit(solution)/shard_map/tick_a/ppermute | solution.py:314
  17.1 12.5 %collective-permute-start.1 = (bf16[112,1792]{1,0:T(8,128)(2,1)S(1)}, bf16[112,1792]{1,0:T(8,128)(2,1)S(1)}, u32[]{:S(2)}, u32[]{:S(2)}) collective-permute-start(bf16[112,1792]{1,0:T(8,128)(2,1)S(1)} %get-tuple-element.164), channel_id=1, source_target_pairs={{0,64},{32,96},{64,128},{96,160},{128,192},{160,224},{192,0},{224,... | collective-permute-start | bytes 1204232 | tf_op jit(solution)/shard_map/tick_a/ppermute | solution.py:287
  18.3 11.2 %collective-permute-start.3 = (bf16[112,1792]{1,0:T(8,128)(2,1)S(1)}, bf16[112,1792]{1,0:T(8,128)(2,1)S(1)}, u32[]{:S(2)}, u32[]{:S(2)}) collective-permute-start(bf16[112,1792]{1,0:T(8,128)(2,1)S(1)} %get-tuple-element.162), channel_id=1, source_target_pairs={{0,192},{32,224},{64,0},{96,32},{128,64},{160,96},{192,128},{224,1... | collective-permute-start | bytes 1204232 | tf_op jit(solution)/shard_map/tick_a/ppermute | solution.py:287
  19.9 17.4 %collective-permute-start.2 = (bf16[112,1792]{1,0:T(8,128)(2,1)S(1)}, bf16[112,1792]{1,0:T(8,128)(2,1)S(1)}, u32[]{:S(2)}, u32[]{:S(2)}) collective-permute-start(bf16[112,1792]{1,0:T(8,128)(2,1)S(1)} %get-tuple-element.163), channel_id=1, source_target_pairs={{0,128},{32,160},{64,192},{96,224},{128,0},{160,32},{192,64},{224,... | collective-permute-start | bytes 1204232 | tf_op jit(solution)/shard_map/tick_a/ppermute | solution.py:287
  29.6 7.7 %copy-start.6 = (bf16[112,1792]{1,0:T(8,128)(2,1)}, bf16[112,1792]{1,0:T(8,128)(2,1)S(1)}, u32[]{:S(2)}) copy-start(bf16[112,1792]{1,0:T(8,128)(2,1)S(1)} %collective-permute-done.1.refs_1_) | copy-start | bytes 1204228
  29.6 7.7 %copy-start.7 = (bf16[112,1792]{1,0:T(8,128)(2,1)}, bf16[112,1792]{1,0:T(8,128)(2,1)S(1)}, u32[]{:S(2)}) copy-start(bf16[112,1792]{1,0:T(8,128)(2,1)S(1)} %collective-permute-done.3.refs_3_) | copy-start | bytes 1204228
  40.6 33.5 %collective-permute-start.6 = (bf16[2,112,1792]{2,1,0:T(8,128)(2,1)}, bf16[2,112,1792]{2,1,0:T(8,128)(2,1)S(1)}, u32[]{:S(2)}, u32[]{:S(2)}) collective-permute-start(bf16[2,112,1792]{2,1,0:T(8,128)(2,1)} %tick_b.1), channel_id=1, source_target_pairs={{0,32},{32,0},{64,96},{96,64},{128,160},{160,128},{192,224},{224,1... | collective-permute-start | bytes 2408456 | tf_op jit(solution)/shard_map/tick_b/ppermute | solution.py:317
  43.3 32.6 %collective-permute-start.5 = (bf16[256,1792]{1,0:T(8,128)(2,1)}, bf16[256,1792]{1,0:T(8,128)(2,1)}, u32[]{:S(2)}, u32[]{:S(2)}) collective-permute-start(bf16[256,1792]{1,0:T(8,128)(2,1)} %pad_maximum_fusion.refs_0_), channel_id=1, source_target_pairs={{4,0},{5,1},{6,2},{7,3},{8,4},{9,5},{10,6},{11,7},{12,8},{13,9},{1... | collective-permute-start | bytes 2752520 | tf_op jit(solution)/shard_map/tick_b/ppermute | solution.py:314
  45.6 31.2 %collective-permute-start.4 = (bf16[256,1792]{1,0:T(8,128)(2,1)}, bf16[256,1792]{1,0:T(8,128)(2,1)}, u32[]{:S(2)}, u32[]{:S(2)}) collective-permute-start(bf16[256,1792]{1,0:T(8,128)(2,1)} %pad_maximum_fusion.refs_0_), channel_id=1, source_target_pairs={{0,4},{1,5},{2,6},{3,7},{4,8},{5,9},{6,10},{7,11},{8,12},{9,13},{1... | collective-permute-start | bytes 2752520 | tf_op jit(solution)/shard_map/tick_b/ppermute | solution.py:314
  45.6 37.2 %collective-permute-start.12 = (bf16[224,1792]{1,0:T(8,128)(2,1)}, bf16[224,1792]{1,0:T(8,128)(2,1)S(1)}, u32[]{:S(2)}, u32[]{:S(2)}) collective-permute-start(bf16[224,1792]{1,0:T(8,128)(2,1)} %bitcast.32), channel_id=1, source_target_pairs={{0,64},{32,96},{64,128},{96,160},{128,192},{160,224},{192,0},{224,... | collective-permute-start | bytes 2408456 | tf_op jit(solution)/shard_map/tick_b/ppermute | solution.py:287
  46.5 37.7 %collective-permute-start.13 = (bf16[224,1792]{1,0:T(8,128)(2,1)}, bf16[224,1792]{1,0:T(8,128)(2,1)S(1)}, u32[]{:S(2)}, u32[]{:S(2)}) collective-permute-start(bf16[224,1792]{1,0:T(8,128)(2,1)} %bitcast.33), channel_id=1, source_target_pairs={{0,128},{32,160},{64,192},{96,224},{128,0},{160,32},{192,64},{224,... | collective-permute-start | bytes 2408456 | tf_op jit(solution)/shard_map/tick_b/ppermute | solution.py:287
  74.1 5.4 %copy-start.17 = (bf16[2,112,1792]{2,1,0:T(8,128)(2,1)}, bf16[2,112,1792]{2,1,0:T(8,128)(2,1)S(1)}, u32[]{:S(2)}) copy-start(bf16[2,112,1792]{2,1,0:T(8,128)(2,1)S(1)} %collective-permute-done.6.refs_4_) | copy-start | bytes 2408452
  74.1 18.6 %collective-permute-start.14 = (bf16[224,1792]{1,0:T(8,128)(2,1)}, bf16[224,1792]{1,0:T(8,128)(2,1)S(1)}, u32[]{:S(2)}, u32[]{:S(2)}) collective-permute-start(bf16[224,1792]{1,0:T(8,128)(2,1)} %bitcast.34), channel_id=1, source_target_pairs={{0,192},{32,224},{64,0},{96,32},{128,64},{160,96},{192,128},{224,1... | collective-permute-start | bytes 2408456 | tf_op jit(solution)/shard_map/tick_b/ppermute | solution.py:287
  76.8 32.9 %collective-permute-start.7 = (bf16[256,1792]{1,0:T(8,128)(2,1)}, bf16[256,1792]{1,0:T(8,128)(2,1)}, u32[]{:S(2)}, u32[]{:S(2)}) collective-permute-start(bf16[256,1792]{1,0:T(8,128)(2,1)} %collective-permute-done.4.refs_1_), channel_id=1, source_target_pairs={{0,4},{1,5},{2,6},{3,7},{4,8},{5,9},{6,10},{7,11},{8,12},{9,13},{1... | collective-permute-start | bytes 2752520 | tf_op jit(solution)/shard_map/tick_c/ppermute | solution.py:314
  76.9 32.8 %collective-permute-start.8 = (bf16[256,1792]{1,0:T(8,128)(2,1)}, bf16[256,1792]{1,0:T(8,128)(2,1)}, u32[]{:S(2)}, u32[]{:S(2)}) collective-permute-start(bf16[256,1792]{1,0:T(8,128)(2,1)} %collective-permute-done.5.refs_2_), channel_id=1, source_target_pairs={{4,0},{5,1},{6,2},{7,3},{8,4},{9,5},{10,6},{11,7},{12,8},{13,9},{1... | collective-permute-start | bytes 2752520 | tf_op jit(solution)/shard_map/tick_c/ppermute | solution.py:314
  82.9 12.1 %copy-start = (bf16[224,1792]{1,0:T(8,128)(2,1)}, bf16[224,1792]{1,0:T(8,128)(2,1)S(1)}, u32[]{:S(2)}) copy-start(bf16[224,1792]{1,0:T(8,128)(2,1)S(1)} %collective-permute-done.12.refs_1_) | copy-start | bytes 2408452
  82.9 14.8 %collective-permute-start.9 = (bf16[112,1792]{1,0:T(8,128)(2,1)}, bf16[112,1792]{1,0:T(8,128)(2,1)S(1)}, u32[]{:S(2)}, u32[]{:S(2)}) collective-permute-start(bf16[112,1792]{1,0:T(8,128)(2,1)} %get-tuple-element.97), channel_id=1, source_target_pairs={{0,64},{32,96},{64,128},{96,160},{128,192},{160,224},{192,0},{224,... | collective-permute-start | bytes 1204232 | tf_op jit(solution)/shard_map/tick_c/ppermute | solution.py:287
  84.1 10.9 %copy-start.1 = (bf16[224,1792]{1,0:T(8,128)(2,1)}, bf16[224,1792]{1,0:T(8,128)(2,1)S(1)}, u32[]{:S(2)}) copy-start(bf16[224,1792]{1,0:T(8,128)(2,1)S(1)} %collective-permute-done.13.refs_2_) | copy-start | bytes 2408452
  84.1 18.5 %collective-permute-start.10 = (bf16[112,1792]{1,0:T(8,128)(2,1)}, bf16[112,1792]{1,0:T(8,128)(2,1)S(1)}, u32[]{:S(2)}, u32[]{:S(2)}) collective-permute-start(bf16[112,1792]{1,0:T(8,128)(2,1)} %get-tuple-element.98), channel_id=1, source_target_pairs={{0,128},{32,160},{64,192},{96,224},{128,0},{160,32},{192,64},{224,... | collective-permute-start | bytes 1204232 | tf_op jit(solution)/shard_map/tick_c/ppermute | solution.py:287
  92.7 2.3 %copy-start.2 = (bf16[224,1792]{1,0:T(8,128)(2,1)}, bf16[224,1792]{1,0:T(8,128)(2,1)S(1)}, u32[]{:S(2)}) copy-start(bf16[224,1792]{1,0:T(8,128)(2,1)S(1)} %collective-permute-done.14.refs_3_) | copy-start | bytes 2408452
  92.7 17.1 %collective-permute-start.11 = (bf16[112,1792]{1,0:T(8,128)(2,1)}, bf16[112,1792]{1,0:T(8,128)(2,1)S(1)}, u32[]{:S(2)}, u32[]{:S(2)}) collective-permute-start(bf16[112,1792]{1,0:T(8,128)(2,1)} %get-tuple-element.99), channel_id=1, source_target_pairs={{0,192},{32,224},{64,0},{96,32},{128,64},{160,96},{192,128},{224,1... | collective-permute-start | bytes 1204232 | tf_op jit(solution)/shard_map/tick_c/ppermute | solution.py:287
  97.7 12.1 %copy-start.19 = (bf16[112,1792]{1,0:T(8,128)(2,1)}, bf16[112,1792]{1,0:T(8,128)(2,1)S(1)}, u32[]{:S(2)}) copy-start(bf16[112,1792]{1,0:T(8,128)(2,1)S(1)} %collective-permute-done.9.refs_1_) | copy-start | bytes 1204228
  102.6 7.2 %copy-start.20 = (bf16[112,1792]{1,0:T(8,128)(2,1)}, bf16[112,1792]{1,0:T(8,128)(2,1)S(1)}, u32[]{:S(2)}) copy-start(bf16[112,1792]{1,0:T(8,128)(2,1)S(1)} %collective-permute-done.10.refs_2_) | copy-start | bytes 1204228
  110.5 8.1 %copy-start.16 = (bf16[2,224,896]{2,1,0:T(8,128)(2,1)S(1)}, bf16[2,224,896]{2,1,0:T(8,128)(2,1)}, u32[]{:S(2)}) copy-start(bf16[2,224,896]{2,1,0:T(8,128)(2,1)} %tick_c.3) | copy-start | bytes 2408452
  113.6 10.2 %collective-permute-start.18 = (bf16[2,224,1792]{2,1,0:T(8,128)(2,1)}, bf16[2,224,1792]{2,1,0:T(8,128)(2,1)S(1)}, u32[]{:S(2)}, u32[]{:S(2)}) collective-permute-start(bf16[2,224,1792]{2,1,0:T(8,128)(2,1)} %bitcast.20), channel_id=1, source_target_pairs={{0,1},{1,0},{2,3},{3,2},{4,5},{5,4},{6,7},{7,6},{8,9},{9,8},{10,11... | collective-permute-start | bytes 4816904 | tf_op jit(solution)/shard_map/tick_d/ppermute | solution.py:314
  116.0 23.3 %collective-permute-start.15 = (bf16[256,1792]{1,0:T(8,128)(2,1)}, bf16[256,1792]{1,0:T(8,128)(2,1)S(1)}, u32[]{:S(2)}, u32[]{:S(2)}) collective-permute-start(bf16[256,1792]{1,0:T(8,128)(2,1)} %collective-permute-done.7.refs_0_), channel_id=1, source_target_pairs={{0,4},{1,5},{2,6},{3,7},{4,8},{5,9},{6,10},{7,11},{8,12},{9,13},{1... | collective-permute-start | bytes 2752520 | tf_op jit(solution)/shard_map/tick_d/ppermute | solution.py:314
  116.0 23.3 %collective-permute-start.16 = (bf16[256,1792]{1,0:T(8,128)(2,1)}, bf16[256,1792]{1,0:T(8,128)(2,1)}, u32[]{:S(2)}, u32[]{:S(2)}) collective-permute-start(bf16[256,1792]{1,0:T(8,128)(2,1)} %collective-permute-done.8.refs_1_), channel_id=1, source_target_pairs={{4,0},{5,1},{6,2},{7,3},{8,4},{9,5},{10,6},{11,7},{12,8},{13,9},{1... | collective-permute-start | bytes 2752520 | tf_op jit(solution)/shard_map/tick_d/ppermute | solution.py:314
  118.7 20.4 %collective-permute-start.17 = (bf16[2,224,896]{2,1,0:T(8,128)(2,1)S(1)}, bf16[2,224,896]{2,1,0:T(8,128)(2,1)S(1)}, u32[]{:S(2)}, u32[]{:S(2)}) collective-permute-start(bf16[2,224,896]{2,1,0:T(8,128)(2,1)S(1)} %copy-done.16), channel_id=1, source_target_pairs={{0,32},{32,0},{64,96},{96,64},{128,160},{160,128},{192,224},{224,1... | collective-permute-start | bytes 2408456 | tf_op jit(solution)/shard_map/tick_d/ppermute | solution.py:355
  123.8 1.2 copy-start.5
  143.3 4.8 %copy-start.15 = (bf16[2,224,896]{2,1,0:T(8,128)(2,1)S(1)}, bf16[2,224,896]{2,1,0:T(8,128)(2,1)}, u32[]{:S(2)}) copy-start(bf16[2,224,896]{2,1,0:T(8,128)(2,1)} %tick_d.5) | copy-start | bytes 2408452
  143.3 29.5 %all-to-all-start.1 = ((bf16[4,224,896]{2,1,0:T(8,128)(2,1)}), bf16[4,224,896]{2,1,0:T(8,128)(2,1)S(1)}, u32[]{:S(2)}, u32[]{:S(2)}) async-start(bf16[4,224,896]{2,1,0:T(8,128)(2,1)} %tick_e.3), calls=%async_computation.1 | async-start | bytes 3211264 | tf_op jit(solution)/shard_map/tick_e/all_to_all | solution.py:324
  148.1 24.6 %collective-permute-start.21 = (bf16[2,224,896]{2,1,0:T(8,128)(2,1)S(1)}, bf16[2,224,896]{2,1,0:T(8,128)(2,1)S(1)}, u32[]{:S(2)}, u32[]{:S(2)}) collective-permute-start(bf16[2,224,896]{2,1,0:T(8,128)(2,1)S(1)} %copy-done.15), channel_id=1, source_target_pairs={{0,32},{32,0},{64,96},{96,64},{128,160},{160,128},{192,224},{224,1... | collective-permute-start | bytes 2408456 | tf_op jit(solution)/shard_map/tick_e/ppermute | solution.py:365
  153.3 19.4 %collective-permute-start.20 = (bf16[128,1792]{1,0:T(8,128)(2,1)}, bf16[128,1792]{1,0:T(8,128)(2,1)}, u32[]{:S(2)}, u32[]{:S(2)}) collective-permute-start(bf16[128,1792]{1,0:T(8,128)(2,1)} %slice.23), channel_id=1, source_target_pairs={{4,0},{5,1},{6,2},{7,3},{8,4},{9,5},{10,6},{11,7},{12,8},{13,9},{1... | collective-permute-start | bytes 1376264 | tf_op jit(solution)/shard_map/tick_e/ppermute | solution.py:314
  156.0 16.7 %collective-permute-start.19 = (bf16[128,1792]{1,0:T(8,128)(2,1)S(1)}, bf16[128,1792]{1,0:T(8,128)(2,1)}, u32[]{:S(2)}, u32[]{:S(2)}) collective-permute-start(bf16[128,1792]{1,0:T(8,128)(2,1)S(1)} %slice.22), channel_id=1, source_target_pairs={{0,4},{1,5},{2,6},{3,7},{4,8},{5,9},{6,10},{7,11},{8,12},{9,13},{1... | collective-permute-start | bytes 1376264 | tf_op jit(solution)/shard_map/tick_e/ppermute | solution.py:314
  172.8 3.8 %copy-start.3 = (bf16[4,224,896]{2,1,0:T(8,128)(2,1)}, bf16[4,224,896]{2,1,0:T(8,128)(2,1)S(1)}, u32[]{:S(2)}) copy-start(bf16[4,224,896]{2,1,0:T(8,128)(2,1)S(1)} %all-to-all-done.1.refs_0_) | copy-start | bytes 4816900
  176.6 22.8 %all-to-all-start.2 = ((bf16[4,224,896]{2,1,0:T(8,128)(2,1)}), bf16[4,224,896]{2,1,0:T(8,128)(2,1)S(1)}, u32[]{:S(2)}, u32[]{:S(2)}) async-start(bf16[4,224,896]{2,1,0:T(8,128)(2,1)} %tick_f.2), calls=%async_computation.2 | async-start | bytes 3211264 | tf_op jit(solution)/shard_map/tick_f/all_to_all | solution.py:324
  180.8 13.1 %copy-start.23 = (s32[8]{0:T(128)S(1)}, s32[8]{0:T(128)}, u32[]{:S(2)}) copy-start(s32[8]{0:T(128)} %param.19) | copy-start | bytes 100
  190.7 4.8 %collective-permute-start.22 = (f32[224,896]{1,0:T(8,128)}, f32[224,896]{1,0:T(8,128)S(1)}, u32[]{:S(2)}, u32[]{:S(2)}) collective-permute-start(f32[224,896]{1,0:T(8,128)} %get-tuple-element.158), channel_id=1, source_target_pairs={{0,1},{1,0},{2,3},{3,2},{4,5},{5,4},{6,7},{7,6},{8,9},{9,8},{10,11... | collective-permute-start | bytes 2408456 | tf_op jit(solution)/shard_map/tick_f/ppermute | solution.py:314
  193.3 4.4 %collective-permute-start.23 = (f32[224,896]{1,0:T(8,128)}, f32[224,896]{1,0:T(8,128)S(1)}, u32[]{:S(2)}, u32[]{:S(2)}) collective-permute-start(f32[224,896]{1,0:T(8,128)} %get-tuple-element.159), channel_id=1, source_target_pairs={{0,1},{1,0},{2,3},{3,2},{4,5},{5,4},{6,7},{7,6},{8,9},{9,8},{10,11... | collective-permute-start | bytes 2408456 | tf_op jit(solution)/shard_map/tick_f/ppermute | solution.py:314
  193.4 4.5 %collective-permute-start.24 = (f32[224,896]{1,0:T(8,128)}, f32[224,896]{1,0:T(8,128)}, u32[]{:S(2)}, u32[]{:S(2)}) collective-permute-start(f32[224,896]{1,0:T(8,128)} %get-tuple-element.160), channel_id=1, source_target_pairs={{0,1},{1,0},{2,3},{3,2},{4,5},{5,4},{6,7},{7,6},{8,9},{9,8},{10,11... | collective-permute-start | bytes 2408456 | tf_op jit(solution)/shard_map/tick_f/ppermute | solution.py:314
  193.8 5.2 %collective-permute-start.25 = (f32[224,896]{1,0:T(8,128)}, f32[224,896]{1,0:T(8,128)}, u32[]{:S(2)}, u32[]{:S(2)}) collective-permute-start(f32[224,896]{1,0:T(8,128)} %get-tuple-element.161), channel_id=1, source_target_pairs={{0,1},{1,0},{2,3},{3,2},{4,5},{5,4},{6,7},{7,6},{8,9},{9,8},{10,11... | collective-permute-start | bytes 2408456 | tf_op jit(solution)/shard_map/tick_f/ppermute | solution.py:314
  195.4 4.0 %copy-start.9 = (f32[224,896]{1,0:T(8,128)}, f32[224,896]{1,0:T(8,128)S(1)}, u32[]{:S(2)}) copy-start(f32[224,896]{1,0:T(8,128)S(1)} %collective-permute-done.22.refs_4_) | copy-start | bytes 2408452
  197.7 1.7 copy-start.10
  199.4 1.2 copy-start.4
  (5 other events, 4.3 us)

commit v7 on v6

--- a/solution.py
+++ b/solution.py
@@ -363,13 +363,13 @@
         sides = [fsdp(up3[:count], z_up), fsdp(down3[count:], z_down)]
         got1 = columns(held1, came1, spans[0])
         came2 = lax.ppermute(sent2, "member", row_swap)
-        sources = [(d, b) for d in (-2, 2, -3, 3) for b in range(2)]
-        sums = terms(here, mine, theirs, cots, [up2, down2, up3, down3], sources, sums, scale)
+        sources = [(d, b) for d in (-2, 2) for b in range(2)]
+        sums = terms(here, mine, theirs, cots, [up2, down2], sources, sums, scale)
     sides, came2, sums, got1, held1 = sync((sides, came2, sums, got1, held1))
     with jax.named_scope("tick_f"):
         got2 = columns(held1, came2, spans[1])
-        sources = [(4, b) for b in range(2)]
-        sums = terms(here, mine, theirs, cots, sides, sources, sums, scale)
+        sources = [(d, b) for d in (-3, 3, 4) for b in range(2)]
+        sums = terms(here, mine, theirs, cots, [up3, down3, *sides], sources, sums, scale)
         other = [fsdp(part, core_swap) for part in sums[2:]]
     with jax.named_scope("adam"):
         return tuple(adam(here, winner, rate, mine, [got1, got2], sums[:2], other, scale))

time: 215 us -> 214 us (level); the launches traced: 211 us -> 213 us
  waiting for transfers between devices: 64.1 us -> 69.8 us
  starting transfers between devices: 58.4 us -> 55.1 us
    ppermute x9, waiting for transfers between devices: 25.9 us -> 34 us  [spread(): return [lax.ppermute(pieces[j], 'member', along_row(j)) for j in (1, 2, 3)]]
    ppermute x1, waiting for transfers between devices: 26 us -> 22.5 us  [exchange(): lax.ppermute(pick('cross', here, winner, held, span), 'member', row_swap)]
    ppermute x14, waiting for transfers between devices: 11.8 us -> 8.8 us  [fsdp(): return lax.ppermute(value, 'fsdp', pairs)]
    ppermute x1, waiting for transfers between devices: 0.01 us -> 2.59 us  [body(): came1 = lax.ppermute(sent1, 'member', row_swap)]
    ppermute x1, starting transfers between devices: 2.47 us -> 0.01 us  [body(): came1 = lax.ppermute(sent1, 'member', row_swap)]
    unnamed x48 -> x44, local copies, waits for them, and re-layouts: 5.77 us -> 6.71 us
  transfers between devices with their start and end apart: 29 -> 29, of which waited for: 14 -> 15; matrix products, arithmetic and copies ran while one was open for 3% -> 3% of each run, Pallas kernels for 25% -> 24%
where the time goes in v7:
time: 214 us; the launch traced here: 213 us
  Pallas kernels  69.9 us (33%)
  waiting for transfers between devices  69.8 us (33%)
  starting transfers between devices  55.1 us (26%)
  local copies, waits for them, and re-layouts  15.9 us (7%)
    pallas_call x3, Pallas kernels, terms(): pl.pallas_call(kernel, in_specs=[pl.BlockSpec(memory_space=pltpu.SMEM)] +...  39.9 us
    ppermute x9, waiting for transfers between devices, spread(): return [lax.ppermute(pieces[j], 'member', along_row(j)) for j in (1, 2, 3)]  34 us
    ppermute x1, waiting for transfers between devices, exchange(): lax.ppermute(pick('cross', here, winner, held, span), 'member', row_swap)  22.5 us
    pallas_call x7, Pallas kernels, pick(): pl.pallas_call(functools.partial(pick_kernel, mode, span), in_specs=[smem...  19.7 us
    ppermute x14, starting transfers between devices, fsdp(): return lax.ppermute(value, 'fsdp', pairs)  19.4 us
    ppermute x9, starting transfers between devices, spread(): return [lax.ppermute(pieces[j], 'member', along_row(j)) for j in (1, 2, 3)]  14.7 us
    all_to_all x1, starting transfers between devices, body(): lax.all_to_all(turned, 'fsdp', 0, 0, axis_index_groups=same_core, tiled=T...  10.3 us
    pallas_call x1, Pallas kernels, adam(): pl.pallas_call(functools.partial(adam_kernel, scale), grid_spec=pltpu.Pre...  10.3 us
  transfers between devices with their start and end apart: 29, of which 15 were waited for; matrix products, arithmetic and copies ran while one was open for 3% of the time, Pallas kernels for 24%

profile of v7, /device:TPU:1, one launch (start us, length us, event | category | flops | bytes accessed | tf_op | source)
XLA Modules:
  0.0 213.2 jit_solution(16979974165289986142)
XLA Ops:
  0.6 3.9 %copy.16 = bf16[7168,128]{1,0:T(8,128)(2,1)} copy(bf16[7168,128]{0,1:T(8,128)(2,1)} %bitcast.29) | data formatting | bytes 3670016 | tf_op jit(solution)/shard_map/tick_a/transpose | solution.py:338
  4.5 10.3 %all-to-all-start = ((bf16[16,448,128]{2,1,0:T(8,128)(2,1)}), bf16[16,448,128]{2,1,0:T(8,128)(2,1)}, u32[]{:S(2)}, u32[]{:S(2)}) async-start(bf16[16,448,128]{2,1,0:T(8,128)(2,1)} %bitcast.13), calls=%async_computation | async-start | bytes 3670016 | tf_op jit(solution)/shard_map/tick_a/all_to_all | solution.py:339
  14.8 1.4 collective-permute-start
  17.2 1.2 collective-permute-start.1
  19.3 2.5 %collective-permute-start.2 = (bf16[112,1792]{1,0:T(8,128)(2,1)}, bf16[112,1792]{1,0:T(8,128)(2,1)S(1)}, u32[]{:S(2)}, u32[]{:S(2)}) collective-permute-start(bf16[112,1792]{1,0:T(8,128)(2,1)} %get-tuple-element.163), channel_id=1, source_target_pairs={{0,128},{32,160},{64,192},{96,224},{128,0},{160,32},{192,64},{224,... | collective-permute-start | bytes 1204232 | tf_op jit(solution)/shard_map/tick_a/ppermute | solution.py:287
  21.8 1.2 collective-permute-start.3
  23.6 4.9 %collective-permute-done = bf16[128,1792]{1,0:T(8,128)(2,1)S(1)} collective-permute-done((bf16[128,1792]{1,0:T(8,128)(2,1)S(1)}, bf16[128,1792]{1,0:T(8,128)(2,1)S(1)}, u32[]{:S(2)}, u32[]{:S(2)}) %collective-permute-start) | collective-permute-done | bytes 458784 | tf_op jit(solution)/shard_map/tick_a/ppermute | solution.py:314
  28.6 8.9 %collective-permute-done.2.refs_2_ = bf16[112,1792]{1,0:T(8,128)(2,1)S(1)} collective-permute-done((bf16[112,1792]{1,0:T(8,128)(2,1)}, bf16[112,1792]{1,0:T(8,128)(2,1)S(1)}, u32[]{:S(2)}, u32[]{:S(2)}) %collective-permute-start.2) | collective-permute-done | bytes 401440 | tf_op jit(solution)/shard_map/tick_a/ppermute | solution.py:287
  37.6 1.5 collective-permute-done.3.refs_3_
  39.8 2.6 %tick_b.1 = bf16[2,112,1792]{2,1,0:T(8,128)(2,1)} custom-call(s32[2]{0:T(128)} %pad_add_fusion.here, s32[8]{0:T(128)} %winner.15, bf16[112,1792]{1,0:T(8,128)(2,1)} %get-tuple-element.91.refs_0_, bf16[112,1792]{1,0:T(8,128)(2,1)} %copy-done.6, bf16[112,1792]{1,0:T(8,128)(2,1)} %copy-done.7, bf16[112,1792]{1,0:T(8,128)(2,1)} %copy-done.8), custom_call_target="tpu_custom_call" | custom-call | bytes 1605632 | tf_op jit(solution)/shard_map/tick_b/pallas_call | solution.py:270
  42.4 2.7 %collective-permute-start.6 = (bf16[2,112,1792]{2,1,0:T(8,128)(2,1)}, bf16[2,112,1792]{2,1,0:T(8,128)(2,1)}, u32[]{:S(2)}, u32[]{:S(2)}) collective-permute-start(bf16[2,112,1792]{2,1,0:T(8,128)(2,1)} %tick_b.1), channel_id=1, source_target_pairs={{0,32},{32,0},{64,96},{96,64},{128,160},{160,128},{192,224},{224,1... | collective-permute-start | bytes 2408456 | tf_op jit(solution)/shard_map/tick_b/ppermute | solution.py:317
  45.1 1.2 collective-permute-start.4
  46.3 1.5 collective-permute-start.5
  47.8 1.7 collective-permute-start.12
  49.6 2.9 %collective-permute-start.13 = (bf16[224,1792]{1,0:T(8,128)(2,1)}, bf16[224,1792]{1,0:T(8,128)(2,1)S(1)}, u32[]{:S(2)}, u32[]{:S(2)}) collective-permute-start(bf16[224,1792]{1,0:T(8,128)(2,1)} %bitcast.9), channel_id=1, source_target_pairs={{0,128},{32,160},{64,192},{96,224},{128,0},{160,32},{192,64},{224,... | collective-permute-start | bytes 2408456 | tf_op jit(solution)/shard_map/tick_b/ppermute | solution.py:287
  52.4 22.5 %collective-permute-done.6.refs_4_ = bf16[2,112,1792]{2,1,0:T(8,128)(2,1)} collective-permute-done((bf16[2,112,1792]{2,1,0:T(8,128)(2,1)}, bf16[2,112,1792]{2,1,0:T(8,128)(2,1)}, u32[]{:S(2)}, u32[]{:S(2)}) %collective-permute-start.6) | collective-permute-done | bytes 802848 | tf_op jit(solution)/shard_map/tick_b/ppermute | solution.py:317
  74.9 3.0 %collective-permute-start.14 = (bf16[224,1792]{1,0:T(8,128)(2,1)}, bf16[224,1792]{1,0:T(8,128)(2,1)S(1)}, u32[]{:S(2)}, u32[]{:S(2)}) collective-permute-start(bf16[224,1792]{1,0:T(8,128)(2,1)} %bitcast.32), channel_id=1, source_target_pairs={{0,192},{32,224},{64,0},{96,32},{128,64},{160,96},{192,128},{224,1... | collective-permute-start | bytes 2408456 | tf_op jit(solution)/shard_map/tick_b/ppermute | solution.py:287
  77.9 1.0 copy-done.20
  79.0 2.7 %collective-permute-start.8 = (bf16[256,1792]{1,0:T(8,128)(2,1)}, bf16[256,1792]{1,0:T(8,128)(2,1)}, u32[]{:S(2)}, u32[]{:S(2)}) collective-permute-start(bf16[256,1792]{1,0:T(8,128)(2,1)} %collective-permute-done.5.refs_2_), channel_id=1, source_target_pairs={{4,0},{5,1},{6,2},{7,3},{8,4},{9,5},{10,6},{11,7},{12,8},{13,9},{1... | collective-permute-start | bytes 2752520 | tf_op jit(solution)/shard_map/tick_c/ppermute | solution.py:314
  81.7 2.9 %tick_c.2 = (bf16[112,1792]{1,0:T(8,128)(2,1)}, bf16[112,1792]{1,0:T(8,128)(2,1)}, bf16[112,1792]{1,0:T(8,128)(2,1)}, bf16[112,1792]{1,0:T(8,128)(2,1)}) custom-call(s32[2]{0:T(128)} %pad_add_fusion.here, s32[8]{0:T(128)} %winner.15, bf16[112,1792]{1,0:T(8,128)(2,1)} %get-tuple-element.91.refs_0_, bf16[112,1792]{1,0:T(8,128)(2,1)} %copy-done.6, ...), custom_call_target="tpu_custom_call" | custom-call | bytes 3211264 | tf_op jit(solution)/shard_map/tick_c/pallas_call | solution.py:270
  84.6 1.6 collective-permute-start.10
  87.1 15.7 %collective-permute-done.14.refs_3_ = bf16[224,1792]{1,0:T(8,128)(2,1)S(1)} collective-permute-done((bf16[224,1792]{1,0:T(8,128)(2,1)}, bf16[224,1792]{1,0:T(8,128)(2,1)S(1)}, u32[]{:S(2)}, u32[]{:S(2)}) %collective-permute-start.14) | collective-permute-done | bytes 802848 | tf_op jit(solution)/shard_map/tick_b/ppermute | solution.py:287
  103.7 2.6 %tick_c.3 = bf16[2,224,896]{2,1,0:T(8,128)(2,1)} custom-call(s32[2]{0:T(128)} %pad_add_fusion.here, s32[8]{0:T(128)} %winner.15, bf16[224,1792]{1,0:T(8,128)(2,1)} %bitcast.25, bf16[224,1792]{1,0:T(8,128)(2,1)} %copy-done, bf16[224,1792]{1,0:T(8,128)(2,1)} %copy-done.1, bf16[224,1792]{1,0:T(8,128)(2,1)} %copy-done.2), custom_call_target="tpu_custom_call" | custom-call | bytes 3211264 | tf_op jit(solution)/shard_map/tick_c/pallas_call | solution.py:270
  106.4 5.8 %collective-permute-done.11.refs_3_ = bf16[112,1792]{1,0:T(8,128)(2,1)} collective-permute-done((bf16[112,1792]{1,0:T(8,128)(2,1)}, bf16[112,1792]{1,0:T(8,128)(2,1)}, u32[]{:S(2)}, u32[]{:S(2)}) %collective-permute-start.11) | collective-permute-done | bytes 401440 | tf_op jit(solution)/shard_map/tick_c/ppermute | solution.py:287
  112.2 1.8 collective-permute-done.9.refs_1_
  114.0 2.9 %tick_d.3 = bf16[4,112,1792]{2,1,0:T(8,128)(2,1)} custom-call(s32[2]{0:T(128)} %pad_add_fusion.here, s32[8]{0:T(128)} %winner.15, bf16[112,1792]{1,0:T(8,128)(2,1)} %get-tuple-element.104.refs_0_, bf16[112,1792]{1,0:T(8,128)(2,1)} %collective-permute-done.9.refs_1_, bf16[112,1792]{1,0:T(8,128)(2,1)} %copy-done.19, ...), custom_call_target="tpu_custom_call" | custom-call | bytes 3211264 | tf_op jit(solution)/shard_map/tick_d/pallas_call | solution.py:270
  117.0 3.5 %collective-permute-start.18 = (bf16[2,224,1792]{2,1,0:T(8,128)(2,1)}, bf16[2,224,1792]{2,1,0:T(8,128)(2,1)S(1)}, u32[]{:S(2)}, u32[]{:S(2)}) collective-permute-start(bf16[2,224,1792]{2,1,0:T(8,128)(2,1)} %bitcast.20), channel_id=1, source_target_pairs={{0,1},{1,0},{2,3},{3,2},{4,5},{5,4},{6,7},{7,6},{8,9},{9,8},{10,11... | collective-permute-start | bytes 4816904 | tf_op jit(solution)/shard_map/tick_d/ppermute | solution.py:314
  120.4 2.7 %collective-permute-start.16 = (bf16[256,1792]{1,0:T(8,128)(2,1)}, bf16[256,1792]{1,0:T(8,128)(2,1)}, u32[]{:S(2)}, u32[]{:S(2)}) collective-permute-start(bf16[256,1792]{1,0:T(8,128)(2,1)} %collective-permute-done.8.refs_1_), channel_id=1, source_target_pairs={{4,0},{5,1},{6,2},{7,3},{8,4},{9,5},{10,6},{11,7},{12,8},{13,9},{1... | collective-permute-start | bytes 2752520 | tf_op jit(solution)/shard_map/tick_d/ppermute | solution.py:314
  123.1 2.6 %tick_d.5 = bf16[2,224,896]{2,1,0:T(8,128)(2,1)} custom-call(s32[2]{0:T(128)} %pad_add_fusion.here, s32[8]{0:T(128)} %winner.15, bf16[224,1792]{1,0:T(8,128)(2,1)} %bitcast.26, bf16[224,1792]{1,0:T(8,128)(2,1)} %copy-done, bf16[224,1792]{1,0:T(8,128)(2,1)} %copy-done.1, bf16[224,1792]{1,0:T(8,128)(2,1)} %copy-done.2), custom_call_target="tpu_custom_call" | custom-call | bytes 3211264 | tf_op jit(solution)/shard_map/tick_d/pallas_call | solution.py:270
  125.8 1.2 copy-done.5
  127.0 14.0 %tick_d.4 = (f32[224,1792]{1,0:T(8,128)}, f32[224,1792]{1,0:T(8,128)}, f32[224,896]{1,0:T(8,128)}, f32[224,896]{1,0:T(8,128)}, f32[224,896]{1,0:T(8,128)}, /*index=5*/f32[224,896]{1,0:T(8,128)}) custom-call(s32[2]{0:T(128)} %pad_add_fusion.here, bf16[2,224,1792]{2,1,0:T(8,128)(2,1)} %bitcast.21, bf16[2,224,1792]{2,1,0:T(8,128)(2,1)} %copy-done.5, ...), custom_call_target="tpu_custom_call" | custom-call | flops 4932501504 | bytes 20971520 | tf_op jit(solution)/shard_map/tick_d/pallas_call | solution.py:137
  141.0 2.6 %collective-permute-done.17.refs_4_ = bf16[2,224,896]{2,1,0:T(8,128)(2,1)S(1)} collective-permute-done((bf16[2,224,896]{2,1,0:T(8,128)(2,1)}, bf16[2,224,896]{2,1,0:T(8,128)(2,1)S(1)}, u32[]{:S(2)}, u32[]{:S(2)}) %collective-permute-start.17) | collective-permute-done | bytes 802848 | tf_op jit(solution)/shard_map/tick_d/ppermute | solution.py:355
  144.5 3.0 %tick_e.3 = bf16[4,224,896]{2,1,0:T(8,128)(2,1)} custom-call(s32[2]{0:T(128)} %pad_add_fusion.here, s32[8]{0:T(128)} %winner.15, bf16[224,1792]{1,0:T(8,128)(2,1)} %bitcast.27, bf16[224,1792]{1,0:T(8,128)(2,1)} %copy-done, bf16[224,1792]{1,0:T(8,128)(2,1)} %copy-done.1, bf16[224,1792]{1,0:T(8,128)(2,1)} %copy-done.2, bf16[2,224,896]{2,1,0:T(8,128)(2,1)} %copy-done.14), custom_call_target="tpu_custom_call" | custom-call | bytes 6422528 | tf_op jit(solution)/shard_map/tick_e/pallas_call | solution.py:270
  147.6 3.7 %all-to-all-start.1 = ((bf16[4,224,896]{2,1,0:T(8,128)(2,1)}), bf16[4,224,896]{2,1,0:T(8,128)(2,1)S(1)}, u32[]{:S(2)}, u32[]{:S(2)}) async-start(bf16[4,224,896]{2,1,0:T(8,128)(2,1)} %tick_e.3), calls=%async_computation.1 | async-start | bytes 3211264 | tf_op jit(solution)/shard_map/tick_e/all_to_all | solution.py:324
  151.7 1.0 slice.22
  152.8 1.1 collective-permute-start.19
  153.9 1.8 slice.23
  155.7 1.6 collective-permute-start.20
  157.4 11.5 %tick_e.2 = (f32[224,1792]{1,0:T(8,128)}, f32[224,1792]{1,0:T(8,128)}, f32[224,896]{1,0:T(8,128)}, f32[224,896]{1,0:T(8,128)}, f32[224,896]{1,0:T(8,128)}, /*index=5*/f32[224,896]{1,0:T(8,128)}) custom-call(s32[2]{0:T(128)} %pad_add_fusion.here, bf16[2,224,1792]{2,1,0:T(8,128)(2,1)} %bitcast.22, bf16[2,224,1792]{2,1,0:T(8,128)(2,1)} %copy-done.5, ...), custom_call_target="tpu_custom_call" | custom-call | flops 3288334336 | bytes 20971520 | tf_op jit(solution)/shard_map/tick_e/pallas_call | solution.py:137
  168.9 1.8 collective-permute-done.21.refs_4_
  171.6 2.9 %tick_f.2 = bf16[4,224,896]{2,1,0:T(8,128)(2,1)} custom-call(s32[2]{0:T(128)} %pad_add_fusion.here, s32[8]{0:T(128)} %winner.15, bf16[224,1792]{1,0:T(8,128)(2,1)} %bitcast.28, bf16[224,1792]{1,0:T(8,128)(2,1)} %copy-done, bf16[224,1792]{1,0:T(8,128)(2,1)} %copy-done.1, bf16[224,1792]{1,0:T(8,128)(2,1)} %copy-done.2, bf16[2,224,896]{2,1,0:T(8,128)(2,1)} %copy-done.13), custom_call_target="tpu_custom_call" | custom-call | bytes 6422528 | tf_op jit(solution)/shard_map/tick_f/pallas_call | solution.py:270
  174.6 3.8 %all-to-all-start.2 = ((bf16[4,224,896]{2,1,0:T(8,128)(2,1)}), bf16[4,224,896]{2,1,0:T(8,128)(2,1)S(1)}, u32[]{:S(2)}, u32[]{:S(2)}) async-start(bf16[4,224,896]{2,1,0:T(8,128)(2,1)} %tick_f.2), calls=%async_computation.2 | async-start | bytes 3211264 | tf_op jit(solution)/shard_map/tick_f/all_to_all | solution.py:324
  178.4 14.4 %tick_f.3 = (f32[224,1792]{1,0:T(8,128)}, f32[224,1792]{1,0:T(8,128)}, f32[224,896]{1,0:T(8,128)}, f32[224,896]{1,0:T(8,128)}, f32[224,896]{1,0:T(8,128)}, /*index=5*/f32[224,896]{1,0:T(8,128)}) custom-call(s32[2]{0:T(128)} %pad_add_fusion.here, bf16[2,224,1792]{2,1,0:T(8,128)(2,1)} %bitcast.23, bf16[2,224,1792]{2,1,0:T(8,128)(2,1)} %copy-done.5, ...), custom_call_target="tpu_custom_call" | custom-call | flops 4932501504 | bytes 20971520 | tf_op jit(solution)/shard_map/tick_f/pallas_call | solution.py:137
  192.8 3.1 %collective-permute-start.22 = (f32[224,896]{1,0:T(8,128)}, f32[224,896]{1,0:T(8,128)S(1)}, u32[]{:S(2)}, u32[]{:S(2)}) collective-permute-start(f32[224,896]{1,0:T(8,128)} %get-tuple-element.158), channel_id=1, source_target_pairs={{0,1},{1,0},{2,3},{3,2},{4,5},{5,4},{6,7},{7,6},{8,9},{9,8},{10,11... | collective-permute-start | bytes 2408456 | tf_op jit(solution)/shard_map/tick_f/ppermute | solution.py:314
  198.0 2.3 %collective-permute-done.23.refs_5_ = f32[224,896]{1,0:T(8,128)S(1)} collective-permute-done((f32[224,896]{1,0:T(8,128)}, f32[224,896]{1,0:T(8,128)S(1)}, u32[]{:S(2)}, u32[]{:S(2)}) %collective-permute-start.23) | collective-permute-done | bytes 802848 | tf_op jit(solution)/shard_map/tick_f/ppermute | solution.py:314
  200.4 1.1 collective-permute-done.25.refs_7_
  201.6 1.2 copy-done.4
  202.8 10.3 %adam.1 = (bf16[1,224,1792]{2,1,0:T(8,128)(2,1)}, bf16[1,224,1792]{2,1,0:T(8,128)(2,1)}, bf16[1,224,1792]{2,1,0:T(8,128)(2,1)}, bf16[1,224,1792]{2,1,0:T(8,128)(...) custom-call(s32[2]{0:T(128)} %pad_add_fusion.here, s32[8]{0:T(128)} %winner.15, f32[1]{0:T(128)S(6)} %div.4.rate, ...), custom_call_target="tpu_custom_call" | custom-call | tf_op jit(solution)/shard_map/adam/pallas_call | solution.py:192
  (73 shorter events, 9.1 us)
Async XLA Ops:
  4.5 10.3 %copy-start.18 = (bf16[1,128,1792]{2,1,0:T(8,128)(2,1)S(1)}, bf16[1,128,1792]{2,1,0:T(8,128)(2,1)}, u32[]{:S(2)}) copy-start(bf16[1,128,1792]{2,1,0:T(8,128)(2,1)} %param.10) | copy-start | bytes 1376260
  4.5 11.7 %copy-start.15 = (bf16[1,224,1792]{2,1,0:T(8,128)(2,1)S(1)}, bf16[1,224,1792]{2,1,0:T(8,128)(2,1)}, u32[]{:S(2)}) copy-start(bf16[1,224,1792]{2,1,0:T(8,128)(2,1)} %param.12) | copy-start | bytes 2408452
  4.5 74.4 %all-to-all-start = ((bf16[16,448,128]{2,1,0:T(8,128)(2,1)}), bf16[16,448,128]{2,1,0:T(8,128)(2,1)}, u32[]{:S(2)}, u32[]{:S(2)}) async-start(bf16[16,448,128]{2,1,0:T(8,128)(2,1)} %bitcast.13), calls=%async_computation | async-start | bytes 3670016 | tf_op jit(solution)/shard_map/tick_a/all_to_all | solution.py:339
  14.8 3.6 %copy-start.16 = (bf16[1,224,1792]{2,1,0:T(8,128)(2,1)S(1)}, bf16[1,224,1792]{2,1,0:T(8,128)(2,1)}, u32[]{:S(2)}) copy-start(bf16[1,224,1792]{2,1,0:T(8,128)(2,1)} %param.13) | copy-start | bytes 2408452
  14.8 13.7 %collective-permute-start = (bf16[128,1792]{1,0:T(8,128)(2,1)S(1)}, bf16[128,1792]{1,0:T(8,128)(2,1)S(1)}, u32[]{:S(2)}, u32[]{:S(2)}) collective-permute-start(bf16[128,1792]{1,0:T(8,128)(2,1)S(1)} %bitcast.30), channel_id=1, source_target_pairs={{0,2},{1,3},{2,0},{3,1},{4,6},{5,7},{6,4},{7,5},{8,10},{9,11},{10,... | collective-permute-start | bytes 1376264 | tf_op jit(solution)/shard_map/tick_a/ppermute | solution.py:314
  17.2 11.4 %collective-permute-start.1 = (bf16[112,1792]{1,0:T(8,128)(2,1)}, bf16[112,1792]{1,0:T(8,128)(2,1)S(1)}, u32[]{:S(2)}, u32[]{:S(2)}) collective-permute-start(bf16[112,1792]{1,0:T(8,128)(2,1)} %get-tuple-element.164), channel_id=1, source_target_pairs={{0,64},{32,96},{64,128},{96,160},{128,192},{160,224},{192,0},{224,... | collective-permute-start | bytes 1204232 | tf_op jit(solution)/shard_map/tick_a/ppermute | solution.py:287
  19.3 18.2 %collective-permute-start.2 = (bf16[112,1792]{1,0:T(8,128)(2,1)}, bf16[112,1792]{1,0:T(8,128)(2,1)S(1)}, u32[]{:S(2)}, u32[]{:S(2)}) collective-permute-start(bf16[112,1792]{1,0:T(8,128)(2,1)} %get-tuple-element.163), channel_id=1, source_target_pairs={{0,128},{32,160},{64,192},{96,224},{128,0},{160,32},{192,64},{224,... | collective-permute-start | bytes 1204232 | tf_op jit(solution)/shard_map/tick_a/ppermute | solution.py:287
  21.8 17.2 %collective-permute-start.3 = (bf16[112,1792]{1,0:T(8,128)(2,1)}, bf16[112,1792]{1,0:T(8,128)(2,1)S(1)}, u32[]{:S(2)}, u32[]{:S(2)}) collective-permute-start(bf16[112,1792]{1,0:T(8,128)(2,1)} %get-tuple-element.162), channel_id=1, source_target_pairs={{0,192},{32,224},{64,0},{96,32},{128,64},{160,96},{192,128},{224,1... | collective-permute-start | bytes 1204232 | tf_op jit(solution)/shard_map/tick_a/ppermute | solution.py:287
  28.6 50.3 %copy-start.10 = (bf16[256,1792]{1,0:T(8,128)(2,1)}, bf16[256,1792]{1,0:T(8,128)(2,1)S(1)}, u32[]{:S(2)}) copy-start(bf16[256,1792]{1,0:T(8,128)(2,1)S(1)} %pad_maximum_fusion.refs_0_) | copy-start | bytes 2752516
  28.6 10.4 %copy-start.6 = (bf16[112,1792]{1,0:T(8,128)(2,1)}, bf16[112,1792]{1,0:T(8,128)(2,1)S(1)}, u32[]{:S(2)}) copy-start(bf16[112,1792]{1,0:T(8,128)(2,1)S(1)} %collective-permute-done.1.refs_1_) | copy-start | bytes 1204228
  37.6 1.5 copy-start.7
  42.4 32.5 %collective-permute-start.6 = (bf16[2,112,1792]{2,1,0:T(8,128)(2,1)}, bf16[2,112,1792]{2,1,0:T(8,128)(2,1)}, u32[]{:S(2)}, u32[]{:S(2)}) collective-permute-start(bf16[2,112,1792]{2,1,0:T(8,128)(2,1)} %tick_b.1), channel_id=1, source_target_pairs={{0,32},{32,0},{64,96},{96,64},{128,160},{160,128},{192,224},{224,1... | collective-permute-start | bytes 2408456 | tf_op jit(solution)/shard_map/tick_b/ppermute | solution.py:317
  45.1 32.8 %collective-permute-start.4 = (bf16[256,1792]{1,0:T(8,128)(2,1)S(1)}, bf16[256,1792]{1,0:T(8,128)(2,1)S(1)}, u32[]{:S(2)}, u32[]{:S(2)}) collective-permute-start(bf16[256,1792]{1,0:T(8,128)(2,1)S(1)} %pad_maximum_fusion.refs_0_), channel_id=1, source_target_pairs={{0,4},{1,5},{2,6},{3,7},{4,8},{5,9},{6,10},{7,11},{8,12},{9,13},{1... | collective-permute-start | bytes 2752520 | tf_op jit(solution)/shard_map/tick_b/ppermute | solution.py:314
  46.3 32.6 %collective-permute-start.5 = (bf16[256,1792]{1,0:T(8,128)(2,1)S(1)}, bf16[256,1792]{1,0:T(8,128)(2,1)}, u32[]{:S(2)}, u32[]{:S(2)}) collective-permute-start(bf16[256,1792]{1,0:T(8,128)(2,1)S(1)} %pad_maximum_fusion.refs_0_), channel_id=1, source_target_pairs={{4,0},{5,1},{6,2},{7,3},{8,4},{9,5},{10,6},{11,7},{12,8},{13,9},{1... | collective-permute-start | bytes 2752520 | tf_op jit(solution)/shard_map/tick_b/ppermute | solution.py:314
  47.8 36.8 %collective-permute-start.12 = (bf16[224,1792]{1,0:T(8,128)(2,1)}, bf16[224,1792]{1,0:T(8,128)(2,1)S(1)}, u32[]{:S(2)}, u32[]{:S(2)}) collective-permute-start(bf16[224,1792]{1,0:T(8,128)(2,1)} %bitcast.8), channel_id=1, source_target_pairs={{0,64},{32,96},{64,128},{96,160},{128,192},{160,224},{192,0},{224,... | collective-permute-start | bytes 2408456 | tf_op jit(solution)/shard_map/tick_b/ppermute | solution.py:287
  49.6 37.0 %collective-permute-start.13 = (bf16[224,1792]{1,0:T(8,128)(2,1)}, bf16[224,1792]{1,0:T(8,128)(2,1)S(1)}, u32[]{:S(2)}, u32[]{:S(2)}) collective-permute-start(bf16[224,1792]{1,0:T(8,128)(2,1)} %bitcast.9), channel_id=1, source_target_pairs={{0,128},{32,160},{64,192},{96,224},{128,0},{160,32},{192,64},{224,... | collective-permute-start | bytes 2408456 | tf_op jit(solution)/shard_map/tick_b/ppermute | solution.py:287
  74.9 27.9 %collective-permute-start.14 = (bf16[224,1792]{1,0:T(8,128)(2,1)}, bf16[224,1792]{1,0:T(8,128)(2,1)S(1)}, u32[]{:S(2)}, u32[]{:S(2)}) collective-permute-start(bf16[224,1792]{1,0:T(8,128)(2,1)} %bitcast.32), channel_id=1, source_target_pairs={{0,192},{32,224},{64,0},{96,32},{128,64},{160,96},{192,128},{224,1... | collective-permute-start | bytes 2408456 | tf_op jit(solution)/shard_map/tick_b/ppermute | solution.py:287
  77.9 1.0 copy-start.20
  78.9 35.1 %collective-permute-start.7 = (bf16[256,1792]{1,0:T(8,128)(2,1)}, bf16[256,1792]{1,0:T(8,128)(2,1)S(1)}, u32[]{:S(2)}, u32[]{:S(2)}) collective-permute-start(bf16[256,1792]{1,0:T(8,128)(2,1)} %copy-done.20), channel_id=1, source_target_pairs={{0,4},{1,5},{2,6},{3,7},{4,8},{5,9},{6,10},{7,11},{8,12},{9,13},{1... | collective-permute-start | bytes 2752520 | tf_op jit(solution)/shard_map/tick_c/ppermute | solution.py:314
  79.0 35.0 %collective-permute-start.8 = (bf16[256,1792]{1,0:T(8,128)(2,1)}, bf16[256,1792]{1,0:T(8,128)(2,1)}, u32[]{:S(2)}, u32[]{:S(2)}) collective-permute-start(bf16[256,1792]{1,0:T(8,128)(2,1)} %collective-permute-done.5.refs_2_), channel_id=1, source_target_pairs={{4,0},{5,1},{6,2},{7,3},{8,4},{9,5},{10,6},{11,7},{12,8},{13,9},{1... | collective-permute-start | bytes 2752520 | tf_op jit(solution)/shard_map/tick_c/ppermute | solution.py:314
  84.6 18.2 %copy-start = (bf16[224,1792]{1,0:T(8,128)(2,1)}, bf16[224,1792]{1,0:T(8,128)(2,1)S(1)}, u32[]{:S(2)}) copy-start(bf16[224,1792]{1,0:T(8,128)(2,1)S(1)} %collective-permute-done.12.refs_1_) | copy-start | bytes 2408452
  84.6 21.8 %collective-permute-start.10 = (bf16[112,1792]{1,0:T(8,128)(2,1)}, bf16[112,1792]{1,0:T(8,128)(2,1)S(1)}, u32[]{:S(2)}, u32[]{:S(2)}) collective-permute-start(bf16[112,1792]{1,0:T(8,128)(2,1)} %get-tuple-element.98), channel_id=1, source_target_pairs={{0,128},{32,160},{64,192},{96,224},{128,0},{160,32},{192,64},{224,... | collective-permute-start | bytes 1204232 | tf_op jit(solution)/shard_map/tick_c/ppermute | solution.py:287
  86.5 16.3 %copy-start.1 = (bf16[224,1792]{1,0:T(8,128)(2,1)}, bf16[224,1792]{1,0:T(8,128)(2,1)S(1)}, u32[]{:S(2)}) copy-start(bf16[224,1792]{1,0:T(8,128)(2,1)S(1)} %collective-permute-done.13.refs_2_) | copy-start | bytes 2408452
  86.5 25.7 %collective-permute-start.11 = (bf16[112,1792]{1,0:T(8,128)(2,1)}, bf16[112,1792]{1,0:T(8,128)(2,1)}, u32[]{:S(2)}, u32[]{:S(2)}) collective-permute-start(bf16[112,1792]{1,0:T(8,128)(2,1)} %get-tuple-element.99), channel_id=1, source_target_pairs={{0,192},{32,224},{64,0},{96,32},{128,64},{160,96},{192,128},{224,1... | collective-permute-start | bytes 1204232 | tf_op jit(solution)/shard_map/tick_c/ppermute | solution.py:287
  102.8 11.2 %collective-permute-start.9 = (bf16[112,1792]{1,0:T(8,128)(2,1)}, bf16[112,1792]{1,0:T(8,128)(2,1)}, u32[]{:S(2)}, u32[]{:S(2)}) collective-permute-start(bf16[112,1792]{1,0:T(8,128)(2,1)} %get-tuple-element.97), channel_id=1, source_target_pairs={{0,64},{32,96},{64,128},{96,160},{128,192},{160,224},{192,0},{224,... | collective-permute-start | bytes 1204232 | tf_op jit(solution)/shard_map/tick_c/ppermute | solution.py:287
  106.4 7.6 %copy-start.19 = (bf16[112,1792]{1,0:T(8,128)(2,1)}, bf16[112,1792]{1,0:T(8,128)(2,1)S(1)}, u32[]{:S(2)}) copy-start(bf16[112,1792]{1,0:T(8,128)(2,1)S(1)} %collective-permute-done.10.refs_2_) | copy-start | bytes 1204228
  114.0 6.4 %copy-start.9 = (bf16[256,1792]{1,0:T(8,128)(2,1)}, bf16[256,1792]{1,0:T(8,128)(2,1)S(1)}, u32[]{:S(2)}) copy-start(bf16[256,1792]{1,0:T(8,128)(2,1)S(1)} %collective-permute-done.7.refs_0_) | copy-start | bytes 2752516
  117.0 8.8 %collective-permute-start.18 = (bf16[2,224,1792]{2,1,0:T(8,128)(2,1)}, bf16[2,224,1792]{2,1,0:T(8,128)(2,1)S(1)}, u32[]{:S(2)}, u32[]{:S(2)}) collective-permute-start(bf16[2,224,1792]{2,1,0:T(8,128)(2,1)} %bitcast.20), channel_id=1, source_target_pairs={{0,1},{1,0},{2,3},{3,2},{4,5},{5,4},{6,7},{7,6},{8,9},{9,8},{10,11... | collective-permute-start | bytes 4816904 | tf_op jit(solution)/shard_map/tick_d/ppermute | solution.py:314
  120.4 23.2 %collective-permute-start.15 = (bf16[256,1792]{1,0:T(8,128)(2,1)S(1)}, bf16[256,1792]{1,0:T(8,128)(2,1)}, u32[]{:S(2)}, u32[]{:S(2)}) collective-permute-start(bf16[256,1792]{1,0:T(8,128)(2,1)S(1)} %collective-permute-done.7.refs_0_), channel_id=1, source_target_pairs={{0,4},{1,5},{2,6},{3,7},{4,8},{5,9},{6,10},{7,11},{8,12},{9,13},{1... | collective-permute-start | bytes 2752520 | tf_op jit(solution)/shard_map/tick_d/ppermute | solution.py:314
  120.4 23.2 %collective-permute-start.16 = (bf16[256,1792]{1,0:T(8,128)(2,1)}, bf16[256,1792]{1,0:T(8,128)(2,1)}, u32[]{:S(2)}, u32[]{:S(2)}) collective-permute-start(bf16[256,1792]{1,0:T(8,128)(2,1)} %collective-permute-done.8.refs_1_), channel_id=1, source_target_pairs={{4,0},{5,1},{6,2},{7,3},{8,4},{9,5},{10,6},{11,7},{12,8},{13,9},{1... | collective-permute-start | bytes 2752520 | tf_op jit(solution)/shard_map/tick_d/ppermute | solution.py:314
  123.1 20.5 %collective-permute-start.17 = (bf16[2,224,896]{2,1,0:T(8,128)(2,1)}, bf16[2,224,896]{2,1,0:T(8,128)(2,1)S(1)}, u32[]{:S(2)}, u32[]{:S(2)}) collective-permute-start(bf16[2,224,896]{2,1,0:T(8,128)(2,1)} %tick_c.3), channel_id=1, source_target_pairs={{0,32},{32,0},{64,96},{96,64},{128,160},{160,128},{192,224},{224,1... | collective-permute-start | bytes 2408456 | tf_op jit(solution)/shard_map/tick_d/ppermute | solution.py:355
  125.8 1.2 copy-start.5
  143.6 0.9 copy-start.14
  147.5 3.7 %copy-start.17 = (bf16[2,224,896]{2,1,0:T(8,128)(2,1)S(1)}, bf16[2,224,896]{2,1,0:T(8,128)(2,1)}, u32[]{:S(2)}) copy-start(bf16[2,224,896]{2,1,0:T(8,128)(2,1)} %tick_d.5) | copy-start | bytes 2408452
  147.6 23.3 %all-to-all-start.1 = ((bf16[4,224,896]{2,1,0:T(8,128)(2,1)}), bf16[4,224,896]{2,1,0:T(8,128)(2,1)S(1)}, u32[]{:S(2)}, u32[]{:S(2)}) async-start(bf16[4,224,896]{2,1,0:T(8,128)(2,1)} %tick_e.3), calls=%async_computation.1 | async-start | bytes 3211264 | tf_op jit(solution)/shard_map/tick_e/all_to_all | solution.py:324
  151.3 19.5 %collective-permute-start.21 = (bf16[2,224,896]{2,1,0:T(8,128)(2,1)S(1)}, bf16[2,224,896]{2,1,0:T(8,128)(2,1)S(1)}, u32[]{:S(2)}, u32[]{:S(2)}) collective-permute-start(bf16[2,224,896]{2,1,0:T(8,128)(2,1)S(1)} %copy-done.17), channel_id=1, source_target_pairs={{0,32},{32,0},{64,96},{96,64},{128,160},{160,128},{192,224},{224,1... | collective-permute-start | bytes 2408456 | tf_op jit(solution)/shard_map/tick_e/ppermute | solution.py:365
  152.8 16.1 %collective-permute-start.19 = (bf16[128,1792]{1,0:T(8,128)(2,1)S(1)}, bf16[128,1792]{1,0:T(8,128)(2,1)}, u32[]{:S(2)}, u32[]{:S(2)}) collective-permute-start(bf16[128,1792]{1,0:T(8,128)(2,1)S(1)} %slice.22), channel_id=1, source_target_pairs={{0,4},{1,5},{2,6},{3,7},{4,8},{5,9},{6,10},{7,11},{8,12},{9,13},{1... | collective-permute-start | bytes 1376264 | tf_op jit(solution)/shard_map/tick_e/ppermute | solution.py:314
  155.7 13.2 %collective-permute-start.20 = (bf16[128,1792]{1,0:T(8,128)(2,1)}, bf16[128,1792]{1,0:T(8,128)(2,1)}, u32[]{:S(2)}, u32[]{:S(2)}) collective-permute-start(bf16[128,1792]{1,0:T(8,128)(2,1)} %slice.23), channel_id=1, source_target_pairs={{4,0},{5,1},{6,2},{7,3},{8,4},{9,5},{10,6},{11,7},{12,8},{13,9},{1... | collective-permute-start | bytes 1376264 | tf_op jit(solution)/shard_map/tick_e/ppermute | solution.py:314
  170.8 3.7 %copy-start.3 = (bf16[4,224,896]{2,1,0:T(8,128)(2,1)}, bf16[4,224,896]{2,1,0:T(8,128)(2,1)S(1)}, u32[]{:S(2)}) copy-start(bf16[4,224,896]{2,1,0:T(8,128)(2,1)S(1)} %all-to-all-done.1.refs_0_) | copy-start | bytes 4816900
  174.6 27.0 %all-to-all-start.2 = ((bf16[4,224,896]{2,1,0:T(8,128)(2,1)}), bf16[4,224,896]{2,1,0:T(8,128)(2,1)S(1)}, u32[]{:S(2)}, u32[]{:S(2)}) async-start(bf16[4,224,896]{2,1,0:T(8,128)(2,1)} %tick_f.2), calls=%async_computation.2 | async-start | bytes 3211264 | tf_op jit(solution)/shard_map/tick_f/all_to_all | solution.py:324
  178.4 18.1 %copy-start.21 = (s32[8]{0:T(128)S(1)}, s32[8]{0:T(128)}, u32[]{:S(2)}) copy-start(s32[8]{0:T(128)} %param.19) | copy-start | bytes 100
  192.8 5.2 %collective-permute-start.22 = (f32[224,896]{1,0:T(8,128)}, f32[224,896]{1,0:T(8,128)S(1)}, u32[]{:S(2)}, u32[]{:S(2)}) collective-permute-start(f32[224,896]{1,0:T(8,128)} %get-tuple-element.158), channel_id=1, source_target_pairs={{0,1},{1,0},{2,3},{3,2},{4,5},{5,4},{6,7},{7,6},{8,9},{9,8},{10,11... | collective-permute-start | bytes 2408456 | tf_op jit(solution)/shard_map/tick_f/ppermute | solution.py:314
  195.9 4.4 %collective-permute-start.23 = (f32[224,896]{1,0:T(8,128)}, f32[224,896]{1,0:T(8,128)S(1)}, u32[]{:S(2)}, u32[]{:S(2)}) collective-permute-start(f32[224,896]{1,0:T(8,128)} %get-tuple-element.159), channel_id=1, source_target_pairs={{0,1},{1,0},{2,3},{3,2},{4,5},{5,4},{6,7},{7,6},{8,9},{9,8},{10,11... | collective-permute-start | bytes 2408456 | tf_op jit(solution)/shard_map/tick_f/ppermute | solution.py:314
  196.0 4.5 %collective-permute-start.24 = (f32[224,896]{1,0:T(8,128)}, f32[224,896]{1,0:T(8,128)}, u32[]{:S(2)}, u32[]{:S(2)}) collective-permute-start(f32[224,896]{1,0:T(8,128)} %get-tuple-element.160), channel_id=1, source_target_pairs={{0,1},{1,0},{2,3},{3,2},{4,5},{5,4},{6,7},{7,6},{8,9},{9,8},{10,11... | collective-permute-start | bytes 2408456 | tf_op jit(solution)/shard_map/tick_f/ppermute | solution.py:314
  196.4 5.2 %collective-permute-start.25 = (f32[224,896]{1,0:T(8,128)}, f32[224,896]{1,0:T(8,128)}, u32[]{:S(2)}, u32[]{:S(2)}) collective-permute-start(f32[224,896]{1,0:T(8,128)} %get-tuple-element.161), channel_id=1, source_target_pairs={{0,1},{1,0},{2,3},{3,2},{4,5},{5,4},{6,7},{7,6},{8,9},{9,8},{10,11... | collective-permute-start | bytes 2408456 | tf_op jit(solution)/shard_map/tick_f/ppermute | solution.py:314
  198.0 3.6 %copy-start.11 = (f32[224,896]{1,0:T(8,128)}, f32[224,896]{1,0:T(8,128)S(1)}, u32[]{:S(2)}) copy-start(f32[224,896]{1,0:T(8,128)S(1)} %collective-permute-done.22.refs_4_) | copy-start | bytes 2408452
  200.3 1.3 copy-start.12
  201.6 1.2 copy-start.4
  (3 other events, 2.5 us)
